TPU v7x, 32 devices: a whole 2x2x4 slice. The times are simulated.
32 devices in a mesh: groups: 2 (over y), tm: 4 (over x, core), win: 4 (over z).
Axes of the slice: x: 2, y: 2, z: 4, core: 2. Of those that a mesh axis runs over, the one named last changes fastest.
Arguments:
- unitaries: float32 [8, 4, 2, 2, 256, 256], P(('groups', 'win'), 'tm'), parts along dimension 0, may hold values from -1 to 1, as said below
Outputs:
- propagators: float32 [8, 4, 2, 2, 256, 256], P(('groups', 'win'), 'tm'), parts along dimension 0
There are 2 independent parts, one for each index of `groups`. A program takes and returns all parts, laid end to end along the dimension named above; each array names one. Nothing has to cross between parts.
Inputs may be any that keep to these rules, and one draw needn't show every extreme that they name: `unitaries`: each slot's complex matrix is unitary.
All inputs are finite; a program needn't handle non-finite values.
Results may differ from a plain program's by a relative error of at most 0.0003.
Values sent between devices are 32-bit elements; how exact they have to be, the bound alone decides.
No kernel may reach another device: no remote copies, remote signals or barrier semaphores. Data moves between devices by JAX's collectives and lax.ppermute only.
A program may use at most 64 MiB of HBM per device.

v0:
```python
import jax
import jax.numpy as jnp
from jax import lax
from jax.sharding import PartitionSpec as P


def prefix(value, axis, join, neutral):
    count, mine = (lax.axis_size(axis), lax.axis_index(axis))
    pieces = lax.all_gather(value, axis)
    running = jnp.full_like(value, 0) + jnp.asarray(neutral, value.dtype)

    def hop(position, running):
        longer = join(running, pieces[position])
        return jnp.where(position < mine, longer, running)

    return lax.fori_loop(0, count - 1, hop, running)


def from_root(value, axis, source):
    kept = jnp.where(lax.axis_index(axis) == source, value, 0).astype(value.dtype)
    return lax.psum(kept, axis)


def complex_product(left, right):
    hi = lax.Precision.HIGHEST
    real_part = jnp.dot(
        left[0], right[0], precision=hi, preferred_element_type=jnp.float32
    ) - jnp.dot(left[1], right[1], precision=hi, preferred_element_type=jnp.float32)
    imag_part = jnp.dot(
        left[0], right[1], precision=hi, preferred_element_type=jnp.float32
    ) + jnp.dot(left[1], right[0], precision=hi, preferred_element_type=jnp.float32)
    return jnp.stack([real_part, imag_part])


def later_first(earlier, later):
    return complex_product(later, earlier)


def on_device(unitaries):
    own_slots = unitaries[0, 0]
    width = own_slots.shape[-1]
    identity_pair = jnp.stack(
        [jnp.eye(width, dtype=jnp.float32), jnp.zeros((width, width), jnp.float32)]
    )
    prefixes = [own_slots[0]]
    prefixes.append(complex_product(own_slots[1], prefixes[-1]))
    block_total = prefixes[-1]
    before = prefix(block_total, "tm", later_first, identity_pair)
    through = complex_product(block_total, before)
    window_product = from_root(through, "tm", lax.axis_size("tm") - 1)
    window_carry = prefix(window_product, "win", later_first, identity_pair)
    offset = complex_product(before, window_carry)
    results = jnp.stack([complex_product(piece, offset) for piece in prefixes])
    return results[None, None]


def solution(mesh):
    placed = (P(("groups", "win"), "tm", None, None, None, None),)
    return jax.shard_map(
        on_device,
        mesh=mesh,
        in_specs=placed,
        out_specs=P(("groups", "win"), "tm", None, None, None, None),
        check_vma=False,
    )
```

profile of v0, /device:TPU:0, one launch (start us, length us, event | category | flops | bytes accessed | tf_op | source)
XLA Modules:
  0.0 168.4 jit_solution(17108181392384072371)
XLA Ops:
  6.5 1.5 fusion.67
  8.0 1.4 fusion.57
  9.5 1.4 convolution_subtract_fusion.6
  10.9 0.4 convolution_add_fusion.6
  11.3 0.8 pad_maximum_fusion
  12.1 0.0 all-gather.6.cloned.1.call-update
  12.1 0.0 all-reduce.3.cloned.1.call-start
  12.3 25.3 %all-gather.6.cloned.1.call-done = f32[8,256,256]{2,1,0:T(8,128)} async-done(((f32[2,256,256]{2,1,0:T(8,128)}), f32[8,256,256]{2,1,0:T(8,128)}) %all-gather.6.cloned.1.call-update) | async-done | bytes 2097168 | tf_op jit(solution)/shard_map/all_gather | solution.py:9
  37.6 16.6 %while.26 = (s32[]{:T(128)}, f32[2,256,256]{2,1,0:T(8,128)S(1)}, s32[]{:T(128)}, f32[4,2,256,256]{3,2,1,0:T(8,128)}, s32[]{:T(128)}, /*index=5*/s32[]{:T(128)}, s32[]{}) while((s32[]{:T(128)}, f32[2,256,256]{2,1,0:T(8,128)S(1)}, s32[]{:T(128)}, f32[4,2,256,256]{3,2,1,0:T(8,128)}, s32[]{:T(128)}, /*index=5*/s32[]{:T(128)}, s32[]{}) %tuple.64), condition=%wide.region_1.2_spmd, body=%wide.region_0.1_spmd.sunk | while | flops 805699584 | bytes 5245035 | solution.py:16
  37.6 1.3 fusion.133
  38.9 1.3 fusion.134
  40.2 1.3 fusion.135
  41.6 1.3 fusion.136
  42.9 0.1 maximum_select_fusion.5
  43.1 1.3 fusion.133
  44.4 1.3 fusion.134
  45.8 1.3 fusion.135
  47.1 1.3 fusion.136
  48.5 0.1 maximum_select_fusion.5
  48.6 1.3 fusion.133
  49.9 1.3 fusion.134
  51.3 1.3 fusion.135
  52.6 1.3 fusion.136
  54.0 0.1 maximum_select_fusion.5
  54.1 0.4 fusion.53
  54.5 0.4 fusion.47
  54.9 0.4 fusion.37
  55.3 0.4 fusion.36
  55.7 0.8 fusion.38
  56.5 0.0 all-reduce.3.cloned.1.call-update
  56.5 0.2 all-gather.4.cloned.1.call-start
  56.8 33.1 %all-reduce.3.cloned.1.call-done = f32[1,2,256,256]{3,2,1,0:T(8,128)} async-done(((f32[1,2,256,256]{3,2,1,0:T(8,128)}), f32[1,2,256,256]{3,2,1,0:T(8,128)}) %all-reduce.3.cloned.1.call-update) | async-done | bytes 524304 | tf_op jit(solution)/shard_map/psum | solution.py:21
  89.9 47.5 %all-gather.4.cloned.1.call-done = f32[4,2,256,256]{3,2,1,0:T(8,128)} async-done(((f32[1,2,256,256]{3,2,1,0:T(8,128)}), f32[4,2,256,256]{3,2,1,0:T(8,128)}) %all-gather.4.cloned.1.call-update) | async-done | bytes 2097168 | tf_op jit(solution)/shard_map/all_gather | solution.py:9
  137.4 16.6 %while.27 = (s32[]{:T(128)}, f32[2,256,256]{2,1,0:T(8,128)S(1)}, s32[]{:T(128)}, f32[4,2,256,256]{3,2,1,0:T(8,128)}, s32[]{:T(128)}, /*index=5*/s32[]{:T(128)}, s32[]{}) while((s32[]{:T(128)}, f32[2,256,256]{2,1,0:T(8,128)S(1)}, s32[]{:T(128)}, f32[4,2,256,256]{3,2,1,0:T(8,128)}, s32[]{:T(128)}, /*index=5*/s32[]{:T(128)}, s32[]{}) %tuple.55), condition=%wide.region_4.5_spmd, body=%wide.region_3.4_spmd.sunk | while | flops 805699584 | bytes 5245035 | solution.py:16
  137.4 1.3 fusion.141
  138.8 1.3 fusion.142
  140.1 1.3 fusion.143
  141.4 1.3 fusion.144
  142.8 0.1 maximum_select_fusion.6
  142.9 1.3 fusion.141
  144.3 1.3 fusion.142
  145.6 1.3 fusion.143
  147.0 1.3 fusion.144
  148.3 0.1 maximum_select_fusion.6
  148.5 1.3 fusion.141
  149.8 1.3 fusion.142
  151.1 1.3 fusion.143
  152.5 1.3 fusion.144
  153.8 0.1 maximum_select_fusion.6
  154.0 0.4 fusion.43
  154.4 0.4 fusion.39
  154.8 0.4 convolution_subtract_fusion.4
  155.2 0.6 fusion.95
  155.8 0.6 fusion.64
  156.4 0.4 convolution_add_fusion.4
  156.7 0.6 fusion.96
  157.4 0.6 fusion.62
  158.0 0.6 fusion.33
  158.6 0.6 fusion.32
  159.2 0.6 fusion.35
  159.8 0.6 fusion.34
  160.4 0.1 maximum_bitcast_fusion.1
  160.5 0.1 maximum_bitcast_fusion
  160.6 1.3 copy.11
  (7 shorter events, 0.1 us)
Async XLA Ops:
  6.5 4.3 %copy-start = (f32[1,1,2,2,256,256]{5,4,3,2,1,0:T(8,128)S(1)}, f32[1,1,2,2,256,256]{5,4,3,2,1,0:T(8,128)}, u32[]{:S(2)}) copy-start(f32[1,1,2,2,256,256]{5,4,3,2,1,0:T(8,128)} %param.5) | copy-start | bytes 3145732
  6.5 31.0 %all-gather.6.cloned.1.call-start = ((), (), s32[]{:S(2)}) async-start(), calls=%async_computation.2 | async-start | bytes 2621440 | tf_op jit(solution)/shard_map/all_gather | solution.py:9
  12.1 77.7 %all-reduce.3.cloned.1.call-start = ((), (), s32[]{:S(2)}) async-start(), calls=%async_computation | async-start | bytes 1048576 | tf_op jit(solution)/shard_map/psum | solution.py:21
  56.5 80.9 %all-gather.4.cloned.1.call-start = ((), (), s32[]{:S(2)}) async-start(), calls=%async_computation.1 | async-start | bytes 2621440 | tf_op jit(solution)/shard_map/all_gather | solution.py:9
Sparse Core Ops, SparseCore 0:
  12.3 25.2 all-gather.5
  56.7 33.1 all-reduce.2
  91.4 45.9 all-gather.3
where the time goes:
time: 169 us; the launch traced here: 168 us
  waiting for transfers between devices  106 us (63%)
  matrix products  44.5 us (26%)
  between operations  13.3 us (8%)
  other arithmetic  2.66 us (2%)
    all_gather x2, waiting for transfers between devices, prefix(): pieces = lax.all_gather(value, axis)  72.8 us
    psum x1, waiting for transfers between devices, from_root(): return lax.psum(kept, axis)  33.1 us
    dot_general x11, matrix products, complex_product(): jnp.dot(left[0], right[0], precision=hi, preferred_element_type=jnp.float32)  11.5 us
    dot_general x11, matrix products, complex_product(): jnp.dot(left[1], right[1], precision=hi, preferred_element_type=jnp.float32)  11.4 us
    dot_general x11, matrix products, complex_product(): jnp.dot(left[0], right[1], precision=hi, preferred_element_type=jnp.float32)  11.3 us
    dot_general x11, matrix products, complex_product(): jnp.dot(left[1], right[0], precision=hi, preferred_element_type=jnp.float32)  10.4 us
  transfers between devices with their start and end apart: 3, of which 3 were waited for; matrix products, arithmetic and copies ran while one was open for 0% of the time, Pallas kernels for 0%

commit v1 on v0

v1 whole, which is shorter than its diff:
```python
import functools

import jax
import jax.numpy as jnp
from jax import lax
from jax.experimental import pallas as pl
from jax.experimental.pallas import tpu as pltpu
from jax.sharding import PartitionSpec as P

F32 = jnp.float32
AXES = ("tm", "win")
NN = (((1,), (0,)), ((), ()))
NT = (((1,), (1,)), ((), ()))


def halves(x):
    high = x.astype(jnp.bfloat16)
    return high, (x - high.astype(F32)).astype(jnp.bfloat16)


def product(left, right, dims=NN):
    (lr, lrl), (li, lil) = halves(left[0]), halves(left[1])
    (rr, rrl), (ri, ril) = halves(right[0]), halves(right[1])
    dot = functools.partial(
        lax.dot_general, dimension_numbers=dims, preferred_element_type=F32
    )

    def real(a, al, b, bl):
        return dot(a, b) + (dot(a, bl) + dot(al, b))

    return (
        real(lr, lrl, rr, rrl) - real(li, lil, ri, ril),
        real(lr, lrl, ri, ril) + real(li, lil, rr, rrl),
    )


def pick(condition, yes, no):
    return tuple(jnp.where(condition, a, b) for a, b in zip(yes, no, strict=True))


def pair(ref):
    return ref[0], ref[1]


def put(ref, value):
    ref[0] = value[0]
    ref[1] = value[1]


def identity(width):
    rows = lax.broadcasted_iota(jnp.int32, (width, width), 0)
    columns = lax.broadcasted_iota(jnp.int32, (width, width), 1)
    one = (rows == columns).astype(F32)
    return one, jnp.zeros_like(one)


def call(body, outs, *operands, name):
    whole = pl.BlockSpec(memory_space=pltpu.VMEM)
    shapes = [jax.ShapeDtypeStruct(shape, F32) for shape in outs]
    return pl.pallas_call(
        body,
        out_shape=shapes,
        in_specs=[whole] * len(operands),
        out_specs=[whole] * len(outs),
        compiler_params=pltpu.CompilerParams(vmem_limit_bytes=32 << 20),
        name=name,
    )(*operands)


def place():
    t, w = lax.axis_index("tm"), lax.axis_index("win")
    return t // 2, t % 2, w


def block_kernel(u, block, turned):
    b = product(pair(u[0, 0, 1]), pair(u[0, 0, 0]))
    put(block, b)
    put(turned, (b[0].T, b[1].T))


def chip_kernel(mine, theirs, chip, plane):
    _, k, _ = place()
    first = pick(k == 0, pair(mine), pair(theirs))
    second = pick(k == 0, pair(theirs), pair(mine))
    value = product(first, second)
    put(chip, value)
    plane[...] = jnp.where(k == 0, value[0], value[1])


def window_kernel(chip, near, far, window, piece):
    x, k, _ = place()
    mine = pair(chip)
    other = pick(k == 0, (near[...], far[...]), (far[...], near[...]))
    value = product(pick(x == 0, mine, other), pick(x == 0, other, mine))
    put(window, value)
    rows = piece.shape[1]
    start = pl.multiple_of((2 * k + x) * rows, rows)
    piece[...] = window[:, pl.ds(start, rows), :]


def extend_kernel(piece, window, out):
    put(out, product(pair(piece), pair(window)))


def join(flag, a, b):
    return tuple(
        jnp.concatenate([jnp.where(flag, p, q), jnp.where(flag, q, p)], axis=0)
        for p, q in zip(a, b, strict=True)
    )


def left_kernel(u, block, turned, near_chip, far_chip, near, far, out):
    x, k, w = place()
    width = block.shape[-1]
    one = identity(width)
    other_chip = pick(k == 0, (near_chip[...], far_chip[...]), (far_chip[...], near_chip[...]))
    earlier = product(pick(x == 1, other_chip, one), pick(k == 1, pair(turned), one))
    mine = join(x == 0, pair(near[0]), pair(near[1]))
    theirs = join(x == 0, pair(far[0]), pair(far[1]))
    window = pick(w >= 2, join(k == 0, mine, theirs), one)
    before = product(window, earlier)
    put(out.at[0], product(pair(u[0, 0, 0]), before, NT))
    put(out.at[1], product(pair(block), before, NT))


def final_kernel(left, near, far, out):
    x, k, w = place()
    mine = join(x == 0, pair(near[0]), pair(near[1]))
    theirs = join(x == 0, pair(far[0]), pair(far[1]))
    offset = pick(w >= 1, join(k == 0, mine, theirs), identity(left.shape[-1]))
    for slot in range(2):
        put(out.at[0, 0, slot], product(pair(left[slot]), offset, NT))


def permute(value, pairs):
    windows = lax.axis_size("win")
    flat = [(a * windows + b, c * windows + d) for (a, b), (c, d) in pairs]
    return lax.ppermute(value, AXES, flat)


def small(unitaries):
    width = unitaries.shape[-1]
    full, rows = (2, width, width), width // 4
    strip = (2, rows, width)
    tms, wins = range(4), range(4)
    w = lax.axis_index("win")
    cores = [((t, v), (t ^ 1, v)) for t in tms for v in wins]

    block, turned = call(block_kernel, [full, full], unitaries, name="block")
    turned_other = permute(turned, cores)
    chip, plane = call(chip_kernel, [full, full[1:]], turned, turned_other, name="chip")
    near_chip = permute(plane, [((t, v), (t ^ 2, v)) for t in tms for v in wins])
    far_chip = permute(near_chip, cores)
    window, piece = call(window_kernel, [full, strip], chip, near_chip, far_chip, name="window")

    one_on = permute(piece, [((t, v), (t, v + 1)) for t in tms for v in wins[:-1]])
    two_on = permute(piece, [((t, 0), (t, 2)) for t in tms])
    (both,) = call(extend_kernel, [strip], one_on, window, name="extend")
    both_on = permute(both, [((t, 1), (t, 3)) for t in tms])
    one_across = permute(one_on, [((t, v), (t ^ 2, v)) for t in tms for v in wins[1:]])
    across = permute(
        jnp.where(w == 2, two_on, both),
        [((t, 1), (t ^ 2, 3)) for t in tms] + [((t, 2), (t ^ 2, 2)) for t in tms],
    )

    near_one = jnp.stack([one_on, one_across])
    far_one = permute(near_one, cores)
    (left,) = call(
        left_kernel, [(2, *full)], unitaries, block, turned_other, near_chip, far_chip, near_one, far_one, name="left"
    )

    near = jnp.where(
        w == 1,
        near_one,
        jnp.stack([jnp.where(w == 2, two_on, both_on), across]),
    )
    far = permute(near, cores)
    (out,) = call(final_kernel, [unitaries.shape], left, near, far, name="final")
    return out


def multiply(left, right):
    def body(a, b, out):
        put(out, product(pair(a), pair(b)))

    return call(body, [right.shape], left, right, name="multiply")[0]


def scan(value, axis):
    count, mine = lax.axis_size(axis), lax.axis_index(axis)
    width = value.shape[-1]
    one = jnp.stack([jnp.eye(width, dtype=F32), jnp.zeros((width, width), F32)])
    shifted = lax.ppermute(value, axis, [(i, i + 1) for i in range(count - 1)])
    running = jnp.where(mine >= 1, shifted, one)
    step = 1
    while step < count - 1:
        arrived = lax.ppermute(running, axis, [(i, i + step) for i in range(count - step)])
        running = multiply(running, jnp.where(mine >= step, arrived, one))
        step *= 2
    return running


def general(unitaries):
    own = unitaries[0, 0]
    count = lax.axis_size("tm")
    block = multiply(own[1], own[0])
    before = scan(block, "tm")
    through = multiply(block, before)
    step, mine = 1, lax.axis_index("tm")
    total = through
    while step < count:
        pairs = [(count - 1 - i, count - 1 - i - step) for i in range(min(step, count - step))]
        arrived = lax.ppermute(total, "tm", pairs)
        behind = count - 1 - mine
        total = jnp.where((behind >= step) & (behind < 2 * step), arrived, total)
        step *= 2
    offset = multiply(before, scan(total, "win"))
    first = multiply(own[0], offset)
    return jnp.stack([first, multiply(own[1], first)])[None, None]


def solution(mesh):
    spec = P(("groups", "win"), "tm", None, None, None, None)
    plain = mesh.shape["tm"] == 4 and mesh.shape["win"] == 4
    return jax.shard_map(
        small if plain else general,
        mesh=mesh,
        in_specs=(spec,),
        out_specs=spec,
        check_vma=False,
    )
```

time: 169 us -> 46 us (0.27)
  the two profiles are of different devices: /device:TPU:0 before, /device:TPU:29 now
where the time goes in v1:
time: 46 us; the launch traced here: 45.7 us
  waiting for transfers between devices  23.1 us (50%)
  starting transfers between devices  14.7 us (32%)
  Pallas kernels  6.56 us (14%)
  local copies, waits for them, and re-layouts  1.23 us (3%)
    ppermute x10, waiting for transfers between devices, permute(): return lax.ppermute(value, AXES, flat)  23.1 us
    ppermute x10, starting transfers between devices, permute(): return lax.ppermute(value, AXES, flat)  14.7 us
    pallas_call x6, Pallas kernels, call(): pl.pallas_call(body, out_shape=shapes, in_specs=[whole] * len(operands),...  6.56 us
    unnamed x4, local copies, waits for them, and re-layouts  1.23 us
  transfers between devices with their start and end apart: 10, of which 7 were waited for; matrix products, arithmetic and copies ran while one was open for 0% of the time, Pallas kernels for 6%

profile of v1, /device:TPU:29, one launch (start us, length us, event | category | flops | bytes accessed | tf_op | source)
XLA Modules:
  0.0 45.7 jit_solution(3255204639406030549)
XLA Ops:
  0.0 0.0 copy-start
  0.0 1.2 %copy-done = f32[1,1,2,2,256,256]{5,4,3,2,1,0:T(8,128)S(1)} copy-done((f32[1,1,2,2,256,256]{5,4,3,2,1,0:T(8,128)S(1)}, f32[1,1,2,2,256,256]{5,4,3,2,1,0:T(8,128)}, u32[]{:S(2)}) %copy-start) | copy-done | bytes 1048600
  1.2 0.7 %block.1 = (f32[2,256,256]{2,1,0:T(8,128)S(1)}, f32[2,256,256]{2,1,0:T(8,128)S(1)}) custom-call(f32[1,1,2,2,256,256]{5,4,3,2,1,0:T(8,128)S(1)} %copy-done), custom_call_target="tpu_custom_call" | custom-call | tf_op jit(solution)/shard_map/block/pallas_call | solution.py:60
  1.9 0.7 %collective-permute-start = (f32[2,256,256]{2,1,0:T(8,128)S(1)}, f32[2,256,256]{2,1,0:T(8,128)S(1)}, u32[]{:S(2)}, u32[]{:S(2)}) collective-permute-start(f32[2,256,256]{2,1,0:T(8,128)S(1)} %get-tuple-element.12.mine), channel_id=1, source_target_pairs={{0,4},{1,5},{2,6},{3,7},{4,0},{5,1},{6,2},{7,3},{8,12},{9,13},{10,... | collective-permute-start | bytes 1572872 | tf_op jit(solution)/shard_map/ppermute | solution.py:138
  2.7 1.5 %collective-permute-done.theirs.turned = f32[2,256,256]{2,1,0:T(8,128)S(1)} collective-permute-done((f32[2,256,256]{2,1,0:T(8,128)S(1)}, f32[2,256,256]{2,1,0:T(8,128)S(1)}, u32[]{:S(2)}, u32[]{:S(2)}) %collective-permute-start) | collective-permute-done | bytes 524320 | tf_op jit(solution)/shard_map/ppermute | solution.py:138
  4.2 0.6 %chip.1 = (f32[2,256,256]{2,1,0:T(8,128)S(1)}, f32[256,256]{1,0:T(8,128)S(1)}) custom-call(f32[2,256,256]{2,1,0:T(8,128)S(1)} %get-tuple-element.12.mine, f32[2,256,256]{2,1,0:T(8,128)S(1)} %collective-permute-done.theirs.turned), custom_call_target="tpu_custom_call" | custom-call | tf_op jit(solution)/shard_map/chip/pallas_call | solution.py:60
  4.8 1.3 %collective-permute-start.1 = (f32[256,256]{1,0:T(8,128)S(1)}, f32[256,256]{1,0:T(8,128)S(1)}, u32[]{:S(2)}, u32[]{:S(2)}) collective-permute-start(f32[256,256]{1,0:T(8,128)S(1)} %get-tuple-element.13), channel_id=1, source_target_pairs={{0,8},{1,9},{2,10},{3,11},{4,12},{5,13},{6,14},{7,15},{8,0},{9,1},... | collective-permute-start | bytes 786440 | tf_op jit(solution)/shard_map/ppermute | solution.py:138
  6.1 6.3 %collective-permute-done.1.near.near_chip = f32[256,256]{1,0:T(8,128)S(1)} collective-permute-done((f32[256,256]{1,0:T(8,128)S(1)}, f32[256,256]{1,0:T(8,128)S(1)}, u32[]{:S(2)}, u32[]{:S(2)}) %collective-permute-start.1) | collective-permute-done | bytes 262176 | tf_op jit(solution)/shard_map/ppermute | solution.py:138
  12.4 1.2 %collective-permute-start.2 = (f32[256,256]{1,0:T(8,128)S(1)}, f32[256,256]{1,0:T(8,128)S(1)}, u32[]{:S(2)}, u32[]{:S(2)}) collective-permute-start(f32[256,256]{1,0:T(8,128)S(1)} %collective-permute-done.1.near.near_chip), channel_id=1, source_target_pairs={{0,4},{1,5},{2,6},{3,7},{4,0},{5,1},{6,2},{7,3},{8,12},{9,13},{10,... | collective-permute-start | bytes 786440 | tf_op jit(solution)/shard_map/ppermute | solution.py:138
  13.6 1.2 %collective-permute-done.2.far.far_chip = f32[256,256]{1,0:T(8,128)S(1)} collective-permute-done((f32[256,256]{1,0:T(8,128)S(1)}, f32[256,256]{1,0:T(8,128)S(1)}, u32[]{:S(2)}, u32[]{:S(2)}) %collective-permute-start.2) | collective-permute-done | bytes 262176 | tf_op jit(solution)/shard_map/ppermute | solution.py:138
  14.8 0.7 %window.1 = (f32[2,256,256]{2,1,0:T(8,128)S(1)}, f32[2,64,256]{2,1,0:T(8,128)S(1)}) custom-call(f32[2,256,256]{2,1,0:T(8,128)S(1)} %get-tuple-element.14.chip, f32[256,256]{1,0:T(8,128)S(1)} %collective-permute-done.1.near.near_chip, f32[256,256]{1,0:T(8,128)S(1)} %collective-permute-done.2.far.far_chip), custom_call_target="tpu_custom_call" | custom-call | tf_op jit(solution)/shard_map/window/pallas_call | solution.py:60
  15.5 1.3 %collective-permute-start.3 = (f32[2,64,256]{2,1,0:T(8,128)S(1)}, f32[2,64,256]{2,1,0:T(8,128)S(1)}, u32[]{:S(2)}, u32[]{:S(2)}) collective-permute-start(f32[2,64,256]{2,1,0:T(8,128)S(1)} %get-tuple-element.15), channel_id=1, source_target_pairs={{0,1},{1,2},{2,3},{4,5},{5,6},{6,7},{8,9},{9,10},{10,11},{12,13},{... | collective-permute-start | bytes 393224 | tf_op jit(solution)/shard_map/ppermute | solution.py:138
  16.8 0.7 %collective-permute-start.6 = (f32[2,64,256]{2,1,0:T(8,128)S(1)}, f32[2,64,256]{2,1,0:T(8,128)S(1)}, u32[]{:S(2)}, u32[]{:S(2)}) collective-permute-start(f32[2,64,256]{2,1,0:T(8,128)S(1)} %get-tuple-element.15), channel_id=1, source_target_pairs={{0,2},{4,6},{8,10},{12,14},{16,18},{20,22},{24,26},{28,30}} | collective-permute-start | bytes 393224 | tf_op jit(solution)/shard_map/ppermute | solution.py:138
  17.4 4.6 %collective-permute-done.3.piece = f32[2,64,256]{2,1,0:T(8,128)S(1)} collective-permute-done((f32[2,64,256]{2,1,0:T(8,128)S(1)}, f32[2,64,256]{2,1,0:T(8,128)S(1)}, u32[]{:S(2)}, u32[]{:S(2)}) %collective-permute-start.3) | collective-permute-done | bytes 131104 | tf_op jit(solution)/shard_map/ppermute | solution.py:138
  22.1 0.4 extend.1
  22.5 0.0 copy-start.1
  22.5 1.4 %collective-permute-start.7 = (f32[2,64,256]{2,1,0:T(8,128)S(1)}, f32[2,64,256]{2,1,0:T(8,128)S(1)}, u32[]{:S(2)}, u32[]{:S(2)}) collective-permute-start(f32[2,64,256]{2,1,0:T(8,128)S(1)} %extend.1), channel_id=1, source_target_pairs={{1,3},{5,7},{9,11},{13,15},{17,19},{21,23},{25,27},{29,31}} | collective-permute-start | bytes 393224 | tf_op jit(solution)/shard_map/ppermute | solution.py:138
  23.9 3.1 %collective-permute-start.4 = (f32[2,64,256]{2,1,0:T(8,128)S(1)}, f32[2,64,256]{2,1,0:T(8,128)S(1)}, u32[]{:S(2)}, u32[]{:S(2)}) collective-permute-start(f32[2,64,256]{2,1,0:T(8,128)S(1)} %collective-permute-done.3.piece), channel_id=1, source_target_pairs={{1,9},{2,10},{3,11},{5,13},{6,14},{7,15},{9,1},{10,2},{11,3},{13,5... | collective-permute-start | bytes 393224 | tf_op jit(solution)/shard_map/ppermute | solution.py:138
  27.0 0.0 collective-permute-done.6
  27.1 2.2 %collective-permute-done.7 = f32[2,64,256]{2,1,0:T(8,128)S(1)} collective-permute-done((f32[2,64,256]{2,1,0:T(8,128)S(1)}, f32[2,64,256]{2,1,0:T(8,128)S(1)}, u32[]{:S(2)}, u32[]{:S(2)}) %collective-permute-start.7) | collective-permute-done | bytes 131104 | tf_op jit(solution)/shard_map/ppermute | solution.py:138
  29.2 1.3 %collective-permute-start.8 = (f32[2,64,256]{2,1,0:T(8,128)S(1)}, f32[2,64,256]{2,1,0:T(8,128)S(1)}, u32[]{:S(2)}, u32[]{:S(2)}) collective-permute-start(f32[2,64,256]{2,1,0:T(8,128)S(1)} %get-tuple-element.20), channel_id=1, source_target_pairs={{1,11},{5,15},{9,3},{13,7},{2,10},{6,14},{10,2},{14,6},{17,27},{21... | collective-permute-start | bytes 393224 | tf_op jit(solution)/shard_map/ppermute | solution.py:138
  30.5 0.0 collective-permute-done.4
  30.6 6.2 %collective-permute-done.8 = f32[2,64,256]{2,1,0:T(8,128)S(1)} collective-permute-done((f32[2,64,256]{2,1,0:T(8,128)S(1)}, f32[2,64,256]{2,1,0:T(8,128)S(1)}, u32[]{:S(2)}, u32[]{:S(2)}) %collective-permute-start.8) | collective-permute-done | bytes 131104 | tf_op jit(solution)/shard_map/ppermute | solution.py:138
  36.8 3.6 %collective-permute-start.5 = (f32[2,2,64,256]{3,2,1,0:T(8,128)S(1)}, f32[2,2,64,256]{3,2,1,0:T(8,128)S(1)}, u32[]{:S(2)}, u32[]{:S(2)}) collective-permute-start(f32[2,2,64,256]{3,2,1,0:T(8,128)S(1)} %get-tuple-element.18.near), channel_id=1, source_target_pairs={{0,4},{1,5},{2,6},{3,7},{4,0},{5,1},{6,2},{7,3},{8,12},{9,13},{10,... | collective-permute-start | bytes 786440 | tf_op jit(solution)/shard_map/ppermute | solution.py:138
  40.4 0.1 collective-permute-start.9
  40.4 1.1 %collective-permute-done.5.far = f32[2,2,64,256]{3,2,1,0:T(8,128)S(1)} collective-permute-done((f32[2,2,64,256]{3,2,1,0:T(8,128)S(1)}, f32[2,2,64,256]{3,2,1,0:T(8,128)S(1)}, u32[]{:S(2)}, u32[]{:S(2)}) %collective-permute-start.5) | collective-permute-done | bytes 262176 | tf_op jit(solution)/shard_map/ppermute | solution.py:138
  41.5 0.0 copy-done.1
  41.5 2.1 %left.1 = f32[2,2,256,256]{3,2,1,0:T(8,128)S(1)} custom-call(f32[1,1,2,2,256,256]{5,4,3,2,1,0:T(8,128)S(1)} %copy-done.1, f32[2,256,256]{2,1,0:T(8,128)S(1)} %get-tuple-element.11.block, f32[2,256,256]{2,1,0:T(8,128)S(1)} %collective-permute-done.theirs.turned, f32[256,256]{1,0:T(8,128)S(1)} %collective-permute-done.1.near.near_chip, ...), custom_call_target="tpu_custom_call" | custom-call | tf_op jit(solution)/shard_map/left/pallas_call | solution.py:60
  43.7 0.0 collective-permute-done.9.far
  43.7 2.1 %final.1 = f32[1,1,2,2,256,256]{5,4,3,2,1,0:T(8,128)} custom-call(f32[2,2,256,256]{3,2,1,0:T(8,128)S(1)} %left.1, f32[2,2,64,256]{3,2,1,0:T(8,128)S(1)} %get-tuple-element.17.near, f32[2,2,64,256]{3,2,1,0:T(8,128)S(1)} %collective-permute-done.9.far), custom_call_target="tpu_custom_call" | custom-call | tf_op jit(solution)/shard_map/final/pallas_call | solution.py:60
  (2 shorter events, 0.1 us)
Async XLA Ops:
  0.0 1.2 %copy-start = (f32[1,1,2,2,256,256]{5,4,3,2,1,0:T(8,128)S(1)}, f32[1,1,2,2,256,256]{5,4,3,2,1,0:T(8,128)}, u32[]{:S(2)}) copy-start(f32[1,1,2,2,256,256]{5,4,3,2,1,0:T(8,128)} %u.3) | copy-start | bytes 3145732
  1.9 2.3 %collective-permute-start = (f32[2,256,256]{2,1,0:T(8,128)S(1)}, f32[2,256,256]{2,1,0:T(8,128)S(1)}, u32[]{:S(2)}, u32[]{:S(2)}) collective-permute-start(f32[2,256,256]{2,1,0:T(8,128)S(1)} %get-tuple-element.12.mine), channel_id=1, source_target_pairs={{0,4},{1,5},{2,6},{3,7},{4,0},{5,1},{6,2},{7,3},{8,12},{9,13},{10,... | collective-permute-start | bytes 1572872 | tf_op jit(solution)/shard_map/ppermute | solution.py:138
  4.8 7.6 %collective-permute-start.1 = (f32[256,256]{1,0:T(8,128)S(1)}, f32[256,256]{1,0:T(8,128)S(1)}, u32[]{:S(2)}, u32[]{:S(2)}) collective-permute-start(f32[256,256]{1,0:T(8,128)S(1)} %get-tuple-element.13), channel_id=1, source_target_pairs={{0,8},{1,9},{2,10},{3,11},{4,12},{5,13},{6,14},{7,15},{8,0},{9,1},... | collective-permute-start | bytes 786440 | tf_op jit(solution)/shard_map/ppermute | solution.py:138
  12.4 2.4 %collective-permute-start.2 = (f32[256,256]{1,0:T(8,128)S(1)}, f32[256,256]{1,0:T(8,128)S(1)}, u32[]{:S(2)}, u32[]{:S(2)}) collective-permute-start(f32[256,256]{1,0:T(8,128)S(1)} %collective-permute-done.1.near.near_chip), channel_id=1, source_target_pairs={{0,4},{1,5},{2,6},{3,7},{4,0},{5,1},{6,2},{7,3},{8,12},{9,13},{10,... | collective-permute-start | bytes 786440 | tf_op jit(solution)/shard_map/ppermute | solution.py:138
  15.5 6.6 %collective-permute-start.3 = (f32[2,64,256]{2,1,0:T(8,128)S(1)}, f32[2,64,256]{2,1,0:T(8,128)S(1)}, u32[]{:S(2)}, u32[]{:S(2)}) collective-permute-start(f32[2,64,256]{2,1,0:T(8,128)S(1)} %get-tuple-element.15), channel_id=1, source_target_pairs={{0,1},{1,2},{2,3},{4,5},{5,6},{6,7},{8,9},{9,10},{10,11},{12,13},{... | collective-permute-start | bytes 393224 | tf_op jit(solution)/shard_map/ppermute | solution.py:138
  16.8 10.3 %collective-permute-start.6 = (f32[2,64,256]{2,1,0:T(8,128)S(1)}, f32[2,64,256]{2,1,0:T(8,128)S(1)}, u32[]{:S(2)}, u32[]{:S(2)}) collective-permute-start(f32[2,64,256]{2,1,0:T(8,128)S(1)} %get-tuple-element.15), channel_id=1, source_target_pairs={{0,2},{4,6},{8,10},{12,14},{16,18},{20,22},{24,26},{28,30}} | collective-permute-start | bytes 393224 | tf_op jit(solution)/shard_map/ppermute | solution.py:138
  22.5 19.1 %copy-start.1 = (f32[1,1,2,2,256,256]{5,4,3,2,1,0:T(8,128)S(1)}, f32[1,1,2,2,256,256]{5,4,3,2,1,0:T(8,128)}, u32[]{:S(2)}) copy-start(f32[1,1,2,2,256,256]{5,4,3,2,1,0:T(8,128)} %u.3) | copy-start | bytes 3145732
  22.5 6.7 %collective-permute-start.7 = (f32[2,64,256]{2,1,0:T(8,128)S(1)}, f32[2,64,256]{2,1,0:T(8,128)S(1)}, u32[]{:S(2)}, u32[]{:S(2)}) collective-permute-start(f32[2,64,256]{2,1,0:T(8,128)S(1)} %extend.1), channel_id=1, source_target_pairs={{1,3},{5,7},{9,11},{13,15},{17,19},{21,23},{25,27},{29,31}} | collective-permute-start | bytes 393224 | tf_op jit(solution)/shard_map/ppermute | solution.py:138
  23.9 6.6 %collective-permute-start.4 = (f32[2,64,256]{2,1,0:T(8,128)S(1)}, f32[2,64,256]{2,1,0:T(8,128)S(1)}, u32[]{:S(2)}, u32[]{:S(2)}) collective-permute-start(f32[2,64,256]{2,1,0:T(8,128)S(1)} %collective-permute-done.3.piece), channel_id=1, source_target_pairs={{1,9},{2,10},{3,11},{5,13},{6,14},{7,15},{9,1},{10,2},{11,3},{13,5... | collective-permute-start | bytes 393224 | tf_op jit(solution)/shard_map/ppermute | solution.py:138
  29.2 7.5 %collective-permute-start.8 = (f32[2,64,256]{2,1,0:T(8,128)S(1)}, f32[2,64,256]{2,1,0:T(8,128)S(1)}, u32[]{:S(2)}, u32[]{:S(2)}) collective-permute-start(f32[2,64,256]{2,1,0:T(8,128)S(1)} %get-tuple-element.20), channel_id=1, source_target_pairs={{1,11},{5,15},{9,3},{13,7},{2,10},{6,14},{10,2},{14,6},{17,27},{21... | collective-permute-start | bytes 393224 | tf_op jit(solution)/shard_map/ppermute | solution.py:138
  36.8 4.7 %collective-permute-start.5 = (f32[2,2,64,256]{3,2,1,0:T(8,128)S(1)}, f32[2,2,64,256]{3,2,1,0:T(8,128)S(1)}, u32[]{:S(2)}, u32[]{:S(2)}) collective-permute-start(f32[2,2,64,256]{3,2,1,0:T(8,128)S(1)} %get-tuple-element.18.near), channel_id=1, source_target_pairs={{0,4},{1,5},{2,6},{3,7},{4,0},{5,1},{6,2},{7,3},{8,12},{9,13},{10,... | collective-permute-start | bytes 786440 | tf_op jit(solution)/shard_map/ppermute | solution.py:138
  40.4 3.3 %collective-permute-start.9 = (f32[2,2,64,256]{3,2,1,0:T(8,128)S(1)}, f32[2,2,64,256]{3,2,1,0:T(8,128)S(1)}, u32[]{:S(2)}, u32[]{:S(2)}) collective-permute-start(f32[2,2,64,256]{3,2,1,0:T(8,128)S(1)} %get-tuple-element.17.near), channel_id=1, source_target_pairs={{0,4},{1,5},{2,6},{3,7},{4,0},{5,1},{6,2},{7,3},{8,12},{9,13},{10,... | collective-permute-start | bytes 786440 | tf_op jit(solution)/shard_map/ppermute | solution.py:138

commit v2 on v1

--- a/solution.py
+++ b/solution.py
@@ -54,7 +54,7 @@
     return one, jnp.zeros_like(one)
 
 
-def call(body, outs, *operands, name):
+def call(body, outs, *operands, name, scratch=()):
     whole = pl.BlockSpec(memory_space=pltpu.VMEM)
     shapes = [jax.ShapeDtypeStruct(shape, F32) for shape in outs]
     return pl.pallas_call(
@@ -62,6 +62,7 @@
         out_shape=shapes,
         in_specs=[whole] * len(operands),
         out_specs=[whole] * len(outs),
+        scratch_shapes=[pltpu.VMEM(shape, F32) for shape in scratch],
         compiler_params=pltpu.CompilerParams(vmem_limit_bytes=32 << 20),
         name=name,
     )(*operands)
@@ -87,47 +88,60 @@
     plane[...] = jnp.where(k == 0, value[0], value[1])
 
 
-def window_kernel(chip, near, far, window, piece):
-    x, k, _ = place()
+def ordered(x, k, chip, near, far):
     mine = pair(chip)
     other = pick(k == 0, (near[...], far[...]), (far[...], near[...]))
-    value = product(pick(x == 0, mine, other), pick(x == 0, other, mine))
-    put(window, value)
-    rows = piece.shape[1]
-    start = pl.multiple_of((2 * k + x) * rows, rows)
-    piece[...] = window[:, pl.ds(start, rows), :]
+    return pick(x == 0, mine, other), pick(x == 0, other, mine)
+
+
+def window_kernel(chip, near, far, window, own, other):
+    x, k, _ = place()
+    put(window, product(*ordered(x, k, chip, near, far)))
+    rows = own.shape[1]
+    for strip, at in ((own, x), (other, 1 - x)):
+        strip[...] = window[:, pl.ds(pl.multiple_of((2 * k + at) * rows, rows), rows), :]
 
 
 def extend_kernel(piece, window, out):
     put(out, product(pair(piece), pair(window)))
 
 
-def join(flag, a, b):
-    return tuple(
-        jnp.concatenate([jnp.where(flag, p, q), jnp.where(flag, q, p)], axis=0)
-        for p, q in zip(a, b, strict=True)
-    )
-
-
-def left_kernel(u, block, turned, near_chip, far_chip, near, far, out):
-    x, k, w = place()
-    width = block.shape[-1]
-    one = identity(width)
-    other_chip = pick(k == 0, (near_chip[...], far_chip[...]), (far_chip[...], near_chip[...]))
-    earlier = product(pick(x == 1, other_chip, one), pick(k == 1, pair(turned), one))
-    mine = join(x == 0, pair(near[0]), pair(near[1]))
-    theirs = join(x == 0, pair(far[0]), pair(far[1]))
-    window = pick(w >= 2, join(k == 0, mine, theirs), one)
-    before = product(window, earlier)
+def stack(upper, lower):
+    return tuple(jnp.concatenate([a, b], axis=0) for a, b in zip(upper, lower, strict=True))
+
+
+def whole(near, across, far, far_across):
+    x, k, _ = place()
+    near, across, far, far_across = map(pair, (near, across, far, far_across))
+    mine = stack(pick(x == 0, near, across), pick(x == 0, across, near))
+    theirs = stack(pick(x == 0, far, far_across), pick(x == 0, far_across, far))
+    return stack(pick(k == 0, mine, theirs), pick(k == 0, theirs, mine))
+
+
+def before_kernel(u, block, turned, near, far, out):
+    x, k, _ = place()
+    one = identity(block.shape[-1])
+    other = pick(k == 0, (near[...], far[...]), (far[...], near[...]))
+    before = product(pick(x == 1, other, one), pick(k == 1, pair(turned), one))
     put(out.at[0], product(pair(u[0, 0, 0]), before, NT))
     put(out.at[1], product(pair(block), before, NT))
 
 
-def final_kernel(left, near, far, out):
-    x, k, w = place()
-    mine = join(x == 0, pair(near[0]), pair(near[1]))
-    theirs = join(x == 0, pair(far[0]), pair(far[1]))
-    offset = pick(w >= 1, join(k == 0, mine, theirs), identity(left.shape[-1]))
+def left_kernel(before, near, across, far, far_across, out):
+    _, _, w = place()
+    window = pick(w == 3, whole(near, across, far, far_across), identity(before.shape[-1]))
+    for slot in range(2):
+        put(out.at[slot], product(pair(before[slot]), window, NT))
+
+
+def merge_kernel(one, two, three, out):
+    _, _, w = place()
+    out[...] = jnp.where(w == 1, one[...], jnp.where(w == 2, two[...], three[...]))
+
+
+def final_kernel(left, near, across, far, far_across, out):
+    _, _, w = place()
+    offset = pick(w >= 1, whole(near, across, far, far_across), identity(left.shape[-1]))
     for slot in range(2):
         put(out.at[0, 0, slot], product(pair(left[slot]), offset, NT))
 
@@ -140,42 +154,44 @@
 
 def small(unitaries):
     width = unitaries.shape[-1]
-    full, rows = (2, width, width), width // 4
-    strip = (2, rows, width)
-    tms, wins = range(4), range(4)
-    w = lax.axis_index("win")
-    cores = [((t, v), (t ^ 1, v)) for t in tms for v in wins]
+    full, strip = (2, width, width), (2, width // 4, width)
+    spots = [(t, v) for t in range(4) for v in range(4)]
+    cores = [((t, v), (t ^ 1, v)) for t, v in spots]
+    chips = [((t, v), (t ^ 2, v)) for t, v in spots]
+    twins = [((t, v), (t, v ^ 1)) for t, v in spots]
+    one_two = [((t, 1), (t, 2)) for t in range(4)]
+    one_three = [((t, 1), (t, 3)) for t in range(4)]
+    tie = lax.optimization_barrier
 
     block, turned = call(block_kernel, [full, full], unitaries, name="block")
     turned_other = permute(turned, cores)
     chip, plane = call(chip_kernel, [full, full[1:]], turned, turned_other, name="chip")
-    near_chip = permute(plane, [((t, v), (t ^ 2, v)) for t in tms for v in wins])
+    near_chip = permute(plane, chips)
     far_chip = permute(near_chip, cores)
-    window, piece = call(window_kernel, [full, strip], chip, near_chip, far_chip, name="window")
-
-    one_on = permute(piece, [((t, v), (t, v + 1)) for t in tms for v in wins[:-1]])
-    two_on = permute(piece, [((t, 0), (t, 2)) for t in tms])
-    (both,) = call(extend_kernel, [strip], one_on, window, name="extend")
-    both_on = permute(both, [((t, 1), (t, 3)) for t in tms])
-    one_across = permute(one_on, [((t, v), (t ^ 2, v)) for t in tms for v in wins[1:]])
-    across = permute(
-        jnp.where(w == 2, two_on, both),
-        [((t, 1), (t ^ 2, 3)) for t in tms] + [((t, 2), (t ^ 2, 2)) for t in tms],
-    )
-
-    near_one = jnp.stack([one_on, one_across])
-    far_one = permute(near_one, cores)
+    window, own, other = call(window_kernel, [full, strip, strip], chip, near_chip, far_chip, name="window")
+
+    one, one_other = permute(own, twins), permute(other, twins)
+    (before,) = call(
+        before_kernel, [(2, *full)], unitaries, block, turned_other, near_chip, far_chip, name="before"
+    )
+    one, before = tie((one, before))
+    (both,) = call(extend_kernel, [strip], one, window, name="extend")
+    two = permute(both, one_two)
+    (both_other,) = call(extend_kernel, [strip], one_other, window, name="extend_other")
+    three_other = permute(both_other, one_three)
+    three = permute(two, twins)
+    two_other = permute(two, chips)
+
+    (across,) = call(merge_kernel, [strip], one_other, two_other, three_other, name="merge_across")
+    far_across = permute(across, cores)
+    three, across = tie((three, across))
+    (near,) = call(merge_kernel, [strip], one, two, three, name="merge_near")
+    far = permute(near, cores)
+    one, one_other, _ = tie((one, one_other, both_other))
     (left,) = call(
-        left_kernel, [(2, *full)], unitaries, block, turned_other, near_chip, far_chip, near_one, far_one, name="left"
-    )
-
-    near = jnp.where(
-        w == 1,
-        near_one,
-        jnp.stack([jnp.where(w == 2, two_on, both_on), across]),
-    )
-    far = permute(near, cores)
-    (out,) = call(final_kernel, [unitaries.shape], left, near, far, name="final")
+        left_kernel, [(2, *full)], before, one, one_other, permute(one, cores), permute(one_other, cores), name="left"
+    )
+    (out,) = call(final_kernel, [unitaries.shape], left, near, across, far, far_across, name="final")
     return out
 
 

time: 46 us -> 40 us (0.87)
  the two profiles are of different devices: /device:TPU:29 before, /device:TPU:0 now
where the time goes in v2:
time: 40 us; the launch traced here: 39.8 us
  waiting for transfers between devices  15.8 us (40%)
  starting transfers between devices  15.1 us (38%)
  Pallas kernels  7.55 us (19%)
  local copies, waits for them, and re-layouts  1.23 us (3%)
    ppermute x13, waiting for transfers between devices, permute(): return lax.ppermute(value, AXES, flat)  15.8 us
    ppermute x13, starting transfers between devices, permute(): return lax.ppermute(value, AXES, flat)  15.1 us
    pallas_call x10, Pallas kernels, call(): pl.pallas_call(body, out_shape=shapes, in_specs=[whole] * len(operands),...  7.55 us
    unnamed x4, local copies, waits for them, and re-layouts  1.23 us
  transfers between devices with their start and end apart: 13, of which 6 were waited for; matrix products, arithmetic and copies ran while one was open for 0% of the time, Pallas kernels for 9%

profile of v2, /device:TPU:0, one launch (start us, length us, event | category | flops | bytes accessed | tf_op | source)
XLA Modules:
  0.0 39.8 jit_solution(16640690533288161157)
XLA Ops:
  0.0 0.0 copy-start
  0.0 1.2 %copy-done = f32[1,1,2,2,256,256]{5,4,3,2,1,0:T(8,128)S(1)} copy-done((f32[1,1,2,2,256,256]{5,4,3,2,1,0:T(8,128)S(1)}, f32[1,1,2,2,256,256]{5,4,3,2,1,0:T(8,128)}, u32[]{:S(2)}) %copy-start) | copy-done | bytes 1048600
  1.2 0.7 %block.1 = (f32[2,256,256]{2,1,0:T(8,128)S(1)}, f32[2,256,256]{2,1,0:T(8,128)S(1)}) custom-call(f32[1,1,2,2,256,256]{5,4,3,2,1,0:T(8,128)S(1)} %copy-done), custom_call_target="tpu_custom_call" | custom-call | tf_op jit(solution)/shard_map/block/pallas_call | solution.py:60
  1.9 0.0 copy-start.1
  2.0 0.5 %collective-permute-start = (f32[2,256,256]{2,1,0:T(8,128)S(1)}, f32[2,256,256]{2,1,0:T(8,128)S(1)}, u32[]{:S(2)}, u32[]{:S(2)}) collective-permute-start(f32[2,256,256]{2,1,0:T(8,128)S(1)} %get-tuple-element.18.mine), channel_id=1, source_target_pairs={{0,4},{1,5},{2,6},{3,7},{4,0},{5,1},{6,2},{7,3},{8,12},{9,13},{10,... | collective-permute-start | bytes 1572872 | tf_op jit(solution)/shard_map/ppermute | solution.py:152
  2.5 1.5 %collective-permute-done.theirs.turned = f32[2,256,256]{2,1,0:T(8,128)S(1)} collective-permute-done((f32[2,256,256]{2,1,0:T(8,128)S(1)}, f32[2,256,256]{2,1,0:T(8,128)S(1)}, u32[]{:S(2)}, u32[]{:S(2)}) %collective-permute-start) | collective-permute-done | bytes 524320 | tf_op jit(solution)/shard_map/ppermute | solution.py:152
  4.0 0.6 %chip.1 = (f32[2,256,256]{2,1,0:T(8,128)S(1)}, f32[256,256]{1,0:T(8,128)S(1)}) custom-call(f32[2,256,256]{2,1,0:T(8,128)S(1)} %get-tuple-element.18.mine, f32[2,256,256]{2,1,0:T(8,128)S(1)} %collective-permute-done.theirs.turned), custom_call_target="tpu_custom_call" | custom-call | tf_op jit(solution)/shard_map/chip/pallas_call | solution.py:60
  4.6 2.9 %collective-permute-start.1 = (f32[256,256]{1,0:T(8,128)S(1)}, f32[256,256]{1,0:T(8,128)S(1)}, u32[]{:S(2)}, u32[]{:S(2)}) collective-permute-start(f32[256,256]{1,0:T(8,128)S(1)} %get-tuple-element.20), channel_id=1, source_target_pairs={{0,8},{1,9},{2,10},{3,11},{4,12},{5,13},{6,14},{7,15},{8,0},{9,1},... | collective-permute-start | bytes 786440 | tf_op jit(solution)/shard_map/ppermute | solution.py:152
  7.6 6.6 %collective-permute-done.1.near = f32[256,256]{1,0:T(8,128)S(1)} collective-permute-done((f32[256,256]{1,0:T(8,128)S(1)}, f32[256,256]{1,0:T(8,128)S(1)}, u32[]{:S(2)}, u32[]{:S(2)}) %collective-permute-start.1) | collective-permute-done | bytes 262176 | tf_op jit(solution)/shard_map/ppermute | solution.py:152
  14.2 0.0 collective-permute-start.2
  14.2 1.5 %collective-permute-done.2.far = f32[256,256]{1,0:T(8,128)S(1)} collective-permute-done((f32[256,256]{1,0:T(8,128)S(1)}, f32[256,256]{1,0:T(8,128)S(1)}, u32[]{:S(2)}, u32[]{:S(2)}) %collective-permute-start.2) | collective-permute-done | bytes 262176 | tf_op jit(solution)/shard_map/ppermute | solution.py:152
  15.7 0.7 %window.1 = (f32[2,256,256]{2,1,0:T(8,128)S(1)}, f32[2,64,256]{2,1,0:T(8,128)S(1)}, f32[2,64,256]{2,1,0:T(8,128)S(1)}) custom-call(f32[2,256,256]{2,1,0:T(8,128)S(1)} %get-tuple-element.19.chip, f32[256,256]{1,0:T(8,128)S(1)} %collective-permute-done.1.near, f32[256,256]{1,0:T(8,128)S(1)} %collective-permute-done.2.far), custom_call_target="tpu_custom_call" | custom-call | tf_op jit(solution)/shard_map/window/pallas_call | solution.py:60
  16.4 1.9 %collective-permute-start.3 = (f32[2,64,256]{2,1,0:T(8,128)S(1)}, f32[2,64,256]{2,1,0:T(8,128)S(1)}, u32[]{:S(2)}, u32[]{:S(2)}) collective-permute-start(f32[2,64,256]{2,1,0:T(8,128)S(1)} %get-tuple-element.21), channel_id=1, source_target_pairs={{0,1},{1,0},{2,3},{3,2},{4,5},{5,4},{6,7},{7,6},{8,9},{9,8},{10,11... | collective-permute-start | bytes 393224 | tf_op jit(solution)/shard_map/ppermute | solution.py:152
  18.3 0.2 collective-permute-start.4
  18.5 0.0 copy-done.1
  18.5 1.6 %before.1 = f32[2,2,256,256]{3,2,1,0:T(8,128)S(1)} custom-call(f32[1,1,2,2,256,256]{5,4,3,2,1,0:T(8,128)S(1)} %copy-done.1, f32[2,256,256]{2,1,0:T(8,128)S(1)} %get-tuple-element.22.block, f32[2,256,256]{2,1,0:T(8,128)S(1)} %collective-permute-done.theirs.turned, f32[256,256]{1,0:T(8,128)S(1)} %collective-permute-done.1.near, ...), custom_call_target="tpu_custom_call" | custom-call | tf_op jit(solution)/shard_map/before/pallas_call | solution.py:60
  20.1 2.7 %collective-permute-done.3.near.piece.one = f32[2,64,256]{2,1,0:T(8,128)S(1)} collective-permute-done((f32[2,64,256]{2,1,0:T(8,128)S(1)}, f32[2,64,256]{2,1,0:T(8,128)S(1)}, u32[]{:S(2)}, u32[]{:S(2)}) %collective-permute-start.3) | collective-permute-done | bytes 131104 | tf_op jit(solution)/shard_map/ppermute | solution.py:152
  22.8 0.4 %extend.1 = f32[2,64,256]{2,1,0:T(8,128)S(1)} custom-call(f32[2,64,256]{2,1,0:T(8,128)S(1)} %collective-permute-done.3.near.piece.one, f32[2,256,256]{2,1,0:T(8,128)S(1)} %get-tuple-element.26.window), custom_call_target="tpu_custom_call" | custom-call | tf_op jit(solution)/shard_map/extend/pallas_call | solution.py:60
  23.2 0.7 %collective-permute-start.7 = (f32[2,64,256]{2,1,0:T(8,128)S(1)}, f32[2,64,256]{2,1,0:T(8,128)S(1)}, u32[]{:S(2)}, u32[]{:S(2)}) collective-permute-start(f32[2,64,256]{2,1,0:T(8,128)S(1)} %extend.1), channel_id=1, source_target_pairs={{1,2},{5,6},{9,10},{13,14},{17,18},{21,22},{25,26},{29,30}} | collective-permute-start | bytes 393224 | tf_op jit(solution)/shard_map/ppermute | solution.py:152
  23.9 1.0 %collective-permute-done.4.piece.across.one = f32[2,64,256]{2,1,0:T(8,128)S(1)} collective-permute-done((f32[2,64,256]{2,1,0:T(8,128)S(1)}, f32[2,64,256]{2,1,0:T(8,128)S(1)}, u32[]{:S(2)}, u32[]{:S(2)}) %collective-permute-start.4) | collective-permute-done | bytes 131104 | tf_op jit(solution)/shard_map/ppermute | solution.py:152
  24.9 0.4 extend_other.1
  25.3 0.7 %collective-permute-start.10 = (f32[2,64,256]{2,1,0:T(8,128)S(1)}, f32[2,64,256]{2,1,0:T(8,128)S(1)}, u32[]{:S(2)}, u32[]{:S(2)}) collective-permute-start(f32[2,64,256]{2,1,0:T(8,128)S(1)} %extend_other.1), channel_id=1, source_target_pairs={{1,3},{5,7},{9,11},{13,15},{17,19},{21,23},{25,27},{29,31}} | collective-permute-start | bytes 393224 | tf_op jit(solution)/shard_map/ppermute | solution.py:152
  25.9 0.0 collective-permute-done.7.two
  26.0 1.7 %collective-permute-start.9 = (f32[2,64,256]{2,1,0:T(8,128)S(1)}, f32[2,64,256]{2,1,0:T(8,128)S(1)}, u32[]{:S(2)}, u32[]{:S(2)}) collective-permute-start(f32[2,64,256]{2,1,0:T(8,128)S(1)} %collective-permute-done.7.two), channel_id=1, source_target_pairs={{0,8},{1,9},{2,10},{3,11},{4,12},{5,13},{6,14},{7,15},{8,0},{9,1},... | collective-permute-start | bytes 393224 | tf_op jit(solution)/shard_map/ppermute | solution.py:152
  27.7 5.4 %collective-permute-start.8 = (f32[2,64,256]{2,1,0:T(8,128)S(1)}, f32[2,64,256]{2,1,0:T(8,128)S(1)}, u32[]{:S(2)}, u32[]{:S(2)}) collective-permute-start(f32[2,64,256]{2,1,0:T(8,128)S(1)} %collective-permute-done.7.two), channel_id=1, source_target_pairs={{0,1},{1,0},{2,3},{3,2},{4,5},{5,4},{6,7},{7,6},{8,9},{9,8},{10,11... | collective-permute-start | bytes 393224 | tf_op jit(solution)/shard_map/ppermute | solution.py:152
  33.1 0.0 collective-permute-start.5
  33.1 0.5 %collective-permute-start.6 = (f32[2,64,256]{2,1,0:T(8,128)S(1)}, f32[2,64,256]{2,1,0:T(8,128)S(1)}, u32[]{:S(2)}, u32[]{:S(2)}) collective-permute-start(f32[2,64,256]{2,1,0:T(8,128)S(1)} %collective-permute-done.4.piece.across.one), channel_id=1, source_target_pairs={{0,4},{1,5},{2,6},{3,7},{4,0},{5,1},{6,2},{7,3},{8,12},{9,13},{10,... | collective-permute-start | bytes 393224 | tf_op jit(solution)/shard_map/ppermute | solution.py:152
  33.6 0.0 collective-permute-done.10.three
  33.6 0.0 collective-permute-done.9.two
  33.6 2.4 %collective-permute-done.8.three = f32[2,64,256]{2,1,0:T(8,128)S(1)} collective-permute-done((f32[2,64,256]{2,1,0:T(8,128)S(1)}, f32[2,64,256]{2,1,0:T(8,128)S(1)}, u32[]{:S(2)}, u32[]{:S(2)}) %collective-permute-start.8) | collective-permute-done | bytes 131104 | tf_op jit(solution)/shard_map/ppermute | solution.py:152
  36.1 0.1 collective-permute-start.11
  36.1 0.5 %collective-permute-start.12 = (f32[2,64,256]{2,1,0:T(8,128)S(1)}, f32[2,64,256]{2,1,0:T(8,128)S(1)}, u32[]{:S(2)}, u32[]{:S(2)}) collective-permute-start(f32[2,64,256]{2,1,0:T(8,128)S(1)} %merge_across.1.across), channel_id=1, source_target_pairs={{0,4},{1,5},{2,6},{3,7},{4,0},{5,1},{6,2},{7,3},{8,12},{9,13},{10,... | collective-permute-start | bytes 393224 | tf_op jit(solution)/shard_map/ppermute | solution.py:152
  36.6 0.0 collective-permute-done.5.far
  36.6 0.0 collective-permute-done.6.far_across
  36.6 1.1 %left.1 = f32[2,2,256,256]{3,2,1,0:T(8,128)S(1)} custom-call(f32[2,2,256,256]{3,2,1,0:T(8,128)S(1)} %before.1, f32[2,64,256]{2,1,0:T(8,128)S(1)} %collective-permute-done.3.near.piece.one, f32[2,64,256]{2,1,0:T(8,128)S(1)} %collective-permute-done.4.piece.across.one, f32[2,64,256]{2,1,0:T(8,128)S(1)} %collective-permute-done.5.far, ...), custom_call_target="tpu_custom_call" | custom-call | tf_op jit(solution)/shard_map/left/pallas_call | solution.py:60
  37.7 0.0 collective-permute-done.11.far
  37.7 0.0 collective-permute-done.12.far_across
  37.7 2.1 %final.1 = f32[1,1,2,2,256,256]{5,4,3,2,1,0:T(8,128)} custom-call(f32[2,2,256,256]{3,2,1,0:T(8,128)S(1)} %left.1, f32[2,64,256]{2,1,0:T(8,128)S(1)} %merge_near.1.near, f32[2,64,256]{2,1,0:T(8,128)S(1)} %merge_across.1.across, f32[2,64,256]{2,1,0:T(8,128)S(1)} %collective-permute-done.11.far, f32[2,64,256]{2,1,0:T(8,128)S(1)} %collective-permute-done.12.far_across), custom_call_target="tpu_custom_call" | custom-call | tf_op jit(solution)/shard_map/final/pallas_call | solution.py:60
  (2 shorter events, 0.0 us)
Async XLA Ops:
  0.0 1.2 %copy-start = (f32[1,1,2,2,256,256]{5,4,3,2,1,0:T(8,128)S(1)}, f32[1,1,2,2,256,256]{5,4,3,2,1,0:T(8,128)}, u32[]{:S(2)}) copy-start(f32[1,1,2,2,256,256]{5,4,3,2,1,0:T(8,128)} %u.3) | copy-start | bytes 3145732
  1.9 16.5 %copy-start.1 = (f32[1,1,2,2,256,256]{5,4,3,2,1,0:T(8,128)S(1)}, f32[1,1,2,2,256,256]{5,4,3,2,1,0:T(8,128)}, u32[]{:S(2)}) copy-start(f32[1,1,2,2,256,256]{5,4,3,2,1,0:T(8,128)} %u.3) | copy-start | bytes 3145732
  2.0 2.1 %collective-permute-start = (f32[2,256,256]{2,1,0:T(8,128)S(1)}, f32[2,256,256]{2,1,0:T(8,128)S(1)}, u32[]{:S(2)}, u32[]{:S(2)}) collective-permute-start(f32[2,256,256]{2,1,0:T(8,128)S(1)} %get-tuple-element.18.mine), channel_id=1, source_target_pairs={{0,4},{1,5},{2,6},{3,7},{4,0},{5,1},{6,2},{7,3},{8,12},{9,13},{10,... | collective-permute-start | bytes 1572872 | tf_op jit(solution)/shard_map/ppermute | solution.py:152
  4.6 9.5 %collective-permute-start.1 = (f32[256,256]{1,0:T(8,128)S(1)}, f32[256,256]{1,0:T(8,128)S(1)}, u32[]{:S(2)}, u32[]{:S(2)}) collective-permute-start(f32[256,256]{1,0:T(8,128)S(1)} %get-tuple-element.20), channel_id=1, source_target_pairs={{0,8},{1,9},{2,10},{3,11},{4,12},{5,13},{6,14},{7,15},{8,0},{9,1},... | collective-permute-start | bytes 786440 | tf_op jit(solution)/shard_map/ppermute | solution.py:152
  14.2 1.5 %collective-permute-start.2 = (f32[256,256]{1,0:T(8,128)S(1)}, f32[256,256]{1,0:T(8,128)S(1)}, u32[]{:S(2)}, u32[]{:S(2)}) collective-permute-start(f32[256,256]{1,0:T(8,128)S(1)} %collective-permute-done.1.near), channel_id=1, source_target_pairs={{0,4},{1,5},{2,6},{3,7},{4,0},{5,1},{6,2},{7,3},{8,12},{9,13},{10,... | collective-permute-start | bytes 786440 | tf_op jit(solution)/shard_map/ppermute | solution.py:152
  16.4 6.4 %collective-permute-start.3 = (f32[2,64,256]{2,1,0:T(8,128)S(1)}, f32[2,64,256]{2,1,0:T(8,128)S(1)}, u32[]{:S(2)}, u32[]{:S(2)}) collective-permute-start(f32[2,64,256]{2,1,0:T(8,128)S(1)} %get-tuple-element.21), channel_id=1, source_target_pairs={{0,1},{1,0},{2,3},{3,2},{4,5},{5,4},{6,7},{7,6},{8,9},{9,8},{10,11... | collective-permute-start | bytes 393224 | tf_op jit(solution)/shard_map/ppermute | solution.py:152
  18.3 6.6 %collective-permute-start.4 = (f32[2,64,256]{2,1,0:T(8,128)S(1)}, f32[2,64,256]{2,1,0:T(8,128)S(1)}, u32[]{:S(2)}, u32[]{:S(2)}) collective-permute-start(f32[2,64,256]{2,1,0:T(8,128)S(1)} %get-tuple-element.25), channel_id=1, source_target_pairs={{0,1},{1,0},{2,3},{3,2},{4,5},{5,4},{6,7},{7,6},{8,9},{9,8},{10,11... | collective-permute-start | bytes 393224 | tf_op jit(solution)/shard_map/ppermute | solution.py:152
  23.2 2.8 %collective-permute-start.7 = (f32[2,64,256]{2,1,0:T(8,128)S(1)}, f32[2,64,256]{2,1,0:T(8,128)S(1)}, u32[]{:S(2)}, u32[]{:S(2)}) collective-permute-start(f32[2,64,256]{2,1,0:T(8,128)S(1)} %extend.1), channel_id=1, source_target_pairs={{1,2},{5,6},{9,10},{13,14},{17,18},{21,22},{25,26},{29,30}} | collective-permute-start | bytes 393224 | tf_op jit(solution)/shard_map/ppermute | solution.py:152
  25.3 8.3 %collective-permute-start.10 = (f32[2,64,256]{2,1,0:T(8,128)S(1)}, f32[2,64,256]{2,1,0:T(8,128)S(1)}, u32[]{:S(2)}, u32[]{:S(2)}) collective-permute-start(f32[2,64,256]{2,1,0:T(8,128)S(1)} %extend_other.1), channel_id=1, source_target_pairs={{1,3},{5,7},{9,11},{13,15},{17,19},{21,23},{25,27},{29,31}} | collective-permute-start | bytes 393224 | tf_op jit(solution)/shard_map/ppermute | solution.py:152
  26.0 7.6 %collective-permute-start.9 = (f32[2,64,256]{2,1,0:T(8,128)S(1)}, f32[2,64,256]{2,1,0:T(8,128)S(1)}, u32[]{:S(2)}, u32[]{:S(2)}) collective-permute-start(f32[2,64,256]{2,1,0:T(8,128)S(1)} %collective-permute-done.7.two), channel_id=1, source_target_pairs={{0,8},{1,9},{2,10},{3,11},{4,12},{5,13},{6,14},{7,15},{8,0},{9,1},... | collective-permute-start | bytes 393224 | tf_op jit(solution)/shard_map/ppermute | solution.py:152
  27.7 8.3 %collective-permute-start.8 = (f32[2,64,256]{2,1,0:T(8,128)S(1)}, f32[2,64,256]{2,1,0:T(8,128)S(1)}, u32[]{:S(2)}, u32[]{:S(2)}) collective-permute-start(f32[2,64,256]{2,1,0:T(8,128)S(1)} %collective-permute-done.7.two), channel_id=1, source_target_pairs={{0,1},{1,0},{2,3},{3,2},{4,5},{5,4},{6,7},{7,6},{8,9},{9,8},{10,11... | collective-permute-start | bytes 393224 | tf_op jit(solution)/shard_map/ppermute | solution.py:152
  33.1 3.5 %collective-permute-start.5 = (f32[2,64,256]{2,1,0:T(8,128)S(1)}, f32[2,64,256]{2,1,0:T(8,128)S(1)}, u32[]{:S(2)}, u32[]{:S(2)}) collective-permute-start(f32[2,64,256]{2,1,0:T(8,128)S(1)} %collective-permute-done.3.near.piece.one), channel_id=1, source_target_pairs={{0,4},{1,5},{2,6},{3,7},{4,0},{5,1},{6,2},{7,3},{8,12},{9,13},{10,... | collective-permute-start | bytes 393224 | tf_op jit(solution)/shard_map/ppermute | solution.py:152
  33.1 3.5 %collective-permute-start.6 = (f32[2,64,256]{2,1,0:T(8,128)S(1)}, f32[2,64,256]{2,1,0:T(8,128)S(1)}, u32[]{:S(2)}, u32[]{:S(2)}) collective-permute-start(f32[2,64,256]{2,1,0:T(8,128)S(1)} %collective-permute-done.4.piece.across.one), channel_id=1, source_target_pairs={{0,4},{1,5},{2,6},{3,7},{4,0},{5,1},{6,2},{7,3},{8,12},{9,13},{10,... | collective-permute-start | bytes 393224 | tf_op jit(solution)/shard_map/ppermute | solution.py:152
  36.1 1.7 %collective-permute-start.11 = (f32[2,64,256]{2,1,0:T(8,128)S(1)}, f32[2,64,256]{2,1,0:T(8,128)S(1)}, u32[]{:S(2)}, u32[]{:S(2)}) collective-permute-start(f32[2,64,256]{2,1,0:T(8,128)S(1)} %merge_near.1.near), channel_id=1, source_target_pairs={{0,4},{1,5},{2,6},{3,7},{4,0},{5,1},{6,2},{7,3},{8,12},{9,13},{10,... | collective-permute-start | bytes 393224 | tf_op jit(solution)/shard_map/ppermute | solution.py:152
  36.1 1.6 %collective-permute-start.12 = (f32[2,64,256]{2,1,0:T(8,128)S(1)}, f32[2,64,256]{2,1,0:T(8,128)S(1)}, u32[]{:S(2)}, u32[]{:S(2)}) collective-permute-start(f32[2,64,256]{2,1,0:T(8,128)S(1)} %merge_across.1.across), channel_id=1, source_target_pairs={{0,4},{1,5},{2,6},{3,7},{4,0},{5,1},{6,2},{7,3},{8,12},{9,13},{10,... | collective-permute-start | bytes 393224 | tf_op jit(solution)/shard_map/ppermute | solution.py:152

commit v3 on v2

--- a/solution.py
+++ b/solution.py
@@ -54,15 +54,16 @@
     return one, jnp.zeros_like(one)
 
 
-def call(body, outs, *operands, name, scratch=()):
-    whole = pl.BlockSpec(memory_space=pltpu.VMEM)
+def call(body, outs, *operands, name, scratch=(), hbm_out=False, alias=None):
+    whole, far = pl.BlockSpec(memory_space=pltpu.VMEM), pl.BlockSpec(memory_space=pl.ANY)
     shapes = [jax.ShapeDtypeStruct(shape, F32) for shape in outs]
     return pl.pallas_call(
         body,
         out_shape=shapes,
-        in_specs=[whole] * len(operands),
-        out_specs=[whole] * len(outs),
-        scratch_shapes=[pltpu.VMEM(shape, F32) for shape in scratch],
+        in_specs=[far if i == alias else whole for i in range(len(operands))],
+        out_specs=[far if hbm_out else whole] * len(outs),
+        input_output_aliases={} if alias is None else {alias: 0},
+        scratch_shapes=list(scratch),
         compiler_params=pltpu.CompilerParams(vmem_limit_bytes=32 << 20),
         name=name,
     )(*operands)
@@ -103,18 +104,25 @@
 
 
 def extend_kernel(piece, window, out):
-    put(out, product(pair(piece), pair(window)))
+    _, _, w = place()
+
+    @pl.when(w == 1)
+    def _():
+        put(out, product(pair(piece), pair(window)))
 
 
 def stack(upper, lower):
     return tuple(jnp.concatenate([a, b], axis=0) for a, b in zip(upper, lower, strict=True))
 
 
+def half(x, near, across):
+    near, across = pair(near), pair(across)
+    return stack(pick(x == 0, near, across), pick(x == 0, across, near))
+
+
 def whole(near, across, far, far_across):
     x, k, _ = place()
-    near, across, far, far_across = map(pair, (near, across, far, far_across))
-    mine = stack(pick(x == 0, near, across), pick(x == 0, across, near))
-    theirs = stack(pick(x == 0, far, far_across), pick(x == 0, far_across, far))
+    mine, theirs = half(x, near, across), half(x, far, far_across)
     return stack(pick(k == 0, mine, theirs), pick(k == 0, theirs, mine))
 
 
@@ -129,9 +137,16 @@
 
 def left_kernel(before, near, across, far, far_across, out):
     _, _, w = place()
-    window = pick(w == 3, whole(near, across, far, far_across), identity(before.shape[-1]))
-    for slot in range(2):
-        put(out.at[slot], product(pair(before[slot]), window, NT))
+
+    @pl.when(w == 3)
+    def _():
+        window = whole(near, across, far, far_across)
+        for slot in range(2):
+            put(out.at[slot], product(pair(before[slot]), window, NT))
+
+    @pl.when(w != 3)
+    def _():
+        out[...] = before[...]
 
 
 def merge_kernel(one, two, three, out):
@@ -139,11 +154,51 @@
     out[...] = jnp.where(w == 1, one[...], jnp.where(w == 2, two[...], three[...]))
 
 
-def final_kernel(left, near, across, far, far_across, out):
-    _, _, w = place()
-    offset = pick(w >= 1, whole(near, across, far, far_across), identity(left.shape[-1]))
+def send(out, columns, at, sems, left, offset):
+    width, copies = columns.shape[-1], []
+    high, low = halves(jnp.concatenate(offset, axis=0))
+    dot = functools.partial(lax.dot_general, dimension_numbers=NT, preferred_element_type=F32)
     for slot in range(2):
-        put(out.at[0, 0, slot], product(pair(left[slot]), offset, NT))
+        parts = []
+        for plane in range(2):
+            a, al = halves(left[slot, plane])
+            parts.append(dot(a, high) + (dot(a, low) + dot(al, high)))
+        real, imag = parts
+        columns[slot, 0] = real[:, :width] - imag[:, width:]
+        columns[slot, 1] = real[:, width:] + imag[:, :width]
+        copies.append(pltpu.make_async_copy(columns.at[slot], out.at[0, 0, slot, :, :, at], sems.at[slot]))
+        copies[-1].start()
+    return copies
+
+
+def near_kernel(left, near, across, out, columns, sems):
+    x, k, w = place()
+    width = columns.shape[-1]
+
+    @pl.when(w == 0)
+    def _():
+        copies = [pltpu.make_async_copy(left.at[s], out.at[0, 0, s], sems.at[s]) for s in range(2)]
+        for copy in copies:
+            copy.start()
+        for copy in copies:
+            copy.wait()
+
+    @pl.when(w != 0)
+    def _():
+        at = pl.ds(pl.multiple_of(k * width, width), width)
+        for copy in send(out, columns, at, sems, left, half(x, near, across)):
+            copy.wait()
+
+
+def far_kernel(_, left, far, far_across, out, columns, sems):
+    x, k, w = place()
+    width = columns.shape[-1]
+
+    @pl.when(w != 0)
+    def _():
+        at = pl.ds(pl.multiple_of((1 - k) * width, width), width)
+        for copy in send(out, columns, at, sems, left, half(x, far, far_across)):
+            copy.wait()
 
 
 def permute(value, pairs):
@@ -180,7 +235,7 @@
     (both_other,) = call(extend_kernel, [strip], one_other, window, name="extend_other")
     three_other = permute(both_other, one_three)
     three = permute(two, twins)
-    two_other = permute(two, chips)
+    two_other = permute(both_other, one_two)
 
     (across,) = call(merge_kernel, [strip], one_other, two_other, three_other, name="merge_across")
     far_across = permute(across, cores)
@@ -191,7 +246,10 @@
     (left,) = call(
         left_kernel, [(2, *full)], before, one, one_other, permute(one, cores), permute(one_other, cores), name="left"
     )
-    (out,) = call(final_kernel, [unitaries.shape], left, near, across, far, far_across, name="final")
+    scratch = pltpu.VMEM((2, 2, width, width // 2), F32), pltpu.SemaphoreType.DMA((2,))
+    shape = [unitaries.shape]
+    (out,) = call(near_kernel, shape, left, near, across, name="near", scratch=scratch, hbm_out=True)
+    (out,) = call(far_kernel, shape, out, left, far, far_across, name="far", scratch=scratch, hbm_out=True, alias=0)
     return out
 
 

time: 40 us -> 38.2 us (0.955)
  the two profiles are of different devices: /device:TPU:0 before, /device:TPU:29 now
where the time goes in v3:
time: 38.2 us; the launch traced here: 37.8 us
  starting transfers between devices  15.9 us (42%)
  waiting for transfers between devices  13.1 us (34%)
  Pallas kernels  7.41 us (19%)
  local copies, waits for them, and re-layouts  1.23 us (3%)
    ppermute x13, starting transfers between devices, permute(): return lax.ppermute(value, AXES, flat)  15.9 us
    ppermute x13, waiting for transfers between devices, permute(): return lax.ppermute(value, AXES, flat)  13.1 us
    pallas_call x11, Pallas kernels, call(): pl.pallas_call(body, out_shape=shapes, in_specs=[far if i == alias else w...  7.41 us
    unnamed x4, local copies, waits for them, and re-layouts  1.23 us
  transfers between devices with their start and end apart: 13, of which 6 were waited for; matrix products, arithmetic and copies ran while one was open for 0% of the time, Pallas kernels for 11%

profile of v3, /device:TPU:29, one launch (start us, length us, event | category | flops | bytes accessed | tf_op | source)
XLA Modules:
  0.0 37.8 jit_solution(14597194446673476579)
XLA Ops:
  0.0 0.0 copy-start
  0.0 1.2 %copy-done = f32[1,1,2,2,256,256]{5,4,3,2,1,0:T(8,128)S(1)} copy-done((f32[1,1,2,2,256,256]{5,4,3,2,1,0:T(8,128)S(1)}, f32[1,1,2,2,256,256]{5,4,3,2,1,0:T(8,128)}, u32[]{:S(2)}) %copy-start) | copy-done | bytes 1048600
  1.2 0.7 %block.1 = (f32[2,256,256]{2,1,0:T(8,128)S(1)}, f32[2,256,256]{2,1,0:T(8,128)S(1)}) custom-call(f32[1,1,2,2,256,256]{5,4,3,2,1,0:T(8,128)S(1)} %copy-done), custom_call_target="tpu_custom_call" | custom-call | tf_op jit(solution)/shard_map/block/pallas_call | solution.py:60
  1.9 0.0 copy-start.1
  2.0 0.7 %collective-permute-start = (f32[2,256,256]{2,1,0:T(8,128)S(1)}, f32[2,256,256]{2,1,0:T(8,128)S(1)}, u32[]{:S(2)}, u32[]{:S(2)}) collective-permute-start(f32[2,256,256]{2,1,0:T(8,128)S(1)} %get-tuple-element.18.mine), channel_id=1, source_target_pairs={{0,4},{1,5},{2,6},{3,7},{4,0},{5,1},{6,2},{7,3},{8,12},{9,13},{10,... | collective-permute-start | bytes 1572872 | tf_op jit(solution)/shard_map/ppermute | solution.py:207
  2.7 1.5 %collective-permute-done.theirs.turned = f32[2,256,256]{2,1,0:T(8,128)S(1)} collective-permute-done((f32[2,256,256]{2,1,0:T(8,128)S(1)}, f32[2,256,256]{2,1,0:T(8,128)S(1)}, u32[]{:S(2)}, u32[]{:S(2)}) %collective-permute-start) | collective-permute-done | bytes 524320 | tf_op jit(solution)/shard_map/ppermute | solution.py:207
  4.2 0.6 %chip.1 = (f32[2,256,256]{2,1,0:T(8,128)S(1)}, f32[256,256]{1,0:T(8,128)S(1)}) custom-call(f32[2,256,256]{2,1,0:T(8,128)S(1)} %get-tuple-element.18.mine, f32[2,256,256]{2,1,0:T(8,128)S(1)} %collective-permute-done.theirs.turned), custom_call_target="tpu_custom_call" | custom-call | tf_op jit(solution)/shard_map/chip/pallas_call | solution.py:60
  4.9 1.3 %collective-permute-start.1 = (f32[256,256]{1,0:T(8,128)S(1)}, f32[256,256]{1,0:T(8,128)S(1)}, u32[]{:S(2)}, u32[]{:S(2)}) collective-permute-start(f32[256,256]{1,0:T(8,128)S(1)} %get-tuple-element.20), channel_id=1, source_target_pairs={{0,8},{1,9},{2,10},{3,11},{4,12},{5,13},{6,14},{7,15},{8,0},{9,1},... | collective-permute-start | bytes 786440 | tf_op jit(solution)/shard_map/ppermute | solution.py:207
  6.1 6.3 %collective-permute-done.1.near = f32[256,256]{1,0:T(8,128)S(1)} collective-permute-done((f32[256,256]{1,0:T(8,128)S(1)}, f32[256,256]{1,0:T(8,128)S(1)}, u32[]{:S(2)}, u32[]{:S(2)}) %collective-permute-start.1) | collective-permute-done | bytes 262176 | tf_op jit(solution)/shard_map/ppermute | solution.py:207
  12.4 1.2 %collective-permute-start.2 = (f32[256,256]{1,0:T(8,128)S(1)}, f32[256,256]{1,0:T(8,128)S(1)}, u32[]{:S(2)}, u32[]{:S(2)}) collective-permute-start(f32[256,256]{1,0:T(8,128)S(1)} %collective-permute-done.1.near), channel_id=1, source_target_pairs={{0,4},{1,5},{2,6},{3,7},{4,0},{5,1},{6,2},{7,3},{8,12},{9,13},{10,... | collective-permute-start | bytes 786440 | tf_op jit(solution)/shard_map/ppermute | solution.py:207
  13.6 1.2 %collective-permute-done.2.far = f32[256,256]{1,0:T(8,128)S(1)} collective-permute-done((f32[256,256]{1,0:T(8,128)S(1)}, f32[256,256]{1,0:T(8,128)S(1)}, u32[]{:S(2)}, u32[]{:S(2)}) %collective-permute-start.2) | collective-permute-done | bytes 262176 | tf_op jit(solution)/shard_map/ppermute | solution.py:207
  14.8 0.7 %window.1 = (f32[2,256,256]{2,1,0:T(8,128)S(1)}, f32[2,64,256]{2,1,0:T(8,128)S(1)}, f32[2,64,256]{2,1,0:T(8,128)S(1)}) custom-call(f32[2,256,256]{2,1,0:T(8,128)S(1)} %get-tuple-element.19.chip, f32[256,256]{1,0:T(8,128)S(1)} %collective-permute-done.1.near, f32[256,256]{1,0:T(8,128)S(1)} %collective-permute-done.2.far), custom_call_target="tpu_custom_call" | custom-call | tf_op jit(solution)/shard_map/window/pallas_call | solution.py:60
  15.5 0.2 collective-permute-start.3
  15.7 1.3 %collective-permute-start.4 = (f32[2,64,256]{2,1,0:T(8,128)S(1)}, f32[2,64,256]{2,1,0:T(8,128)S(1)}, u32[]{:S(2)}, u32[]{:S(2)}) collective-permute-start(f32[2,64,256]{2,1,0:T(8,128)S(1)} %get-tuple-element.25), channel_id=1, source_target_pairs={{0,1},{1,0},{2,3},{3,2},{4,5},{5,4},{6,7},{7,6},{8,9},{9,8},{10,11... | collective-permute-start | bytes 393224 | tf_op jit(solution)/shard_map/ppermute | solution.py:207
  17.0 0.0 copy-done.1
  17.0 1.6 %before.1 = f32[2,2,256,256]{3,2,1,0:T(8,128)S(1)} custom-call(f32[1,1,2,2,256,256]{5,4,3,2,1,0:T(8,128)S(1)} %copy-done.1, f32[2,256,256]{2,1,0:T(8,128)S(1)} %get-tuple-element.22.block, f32[2,256,256]{2,1,0:T(8,128)S(1)} %collective-permute-done.theirs.turned, f32[256,256]{1,0:T(8,128)S(1)} %collective-permute-done.1.near, ...), custom_call_target="tpu_custom_call" | custom-call | tf_op jit(solution)/shard_map/before/pallas_call | solution.py:60
  18.6 1.7 %collective-permute-done.3.near.piece.one = f32[2,64,256]{2,1,0:T(8,128)S(1)} collective-permute-done((f32[2,64,256]{2,1,0:T(8,128)S(1)}, f32[2,64,256]{2,1,0:T(8,128)S(1)}, u32[]{:S(2)}, u32[]{:S(2)}) %collective-permute-start.3) | collective-permute-done | bytes 131104 | tf_op jit(solution)/shard_map/ppermute | solution.py:207
  20.3 0.7 %collective-permute-start.7 = (f32[2,64,256]{2,1,0:T(8,128)S(1)}, f32[2,64,256]{2,1,0:T(8,128)S(1)}, u32[]{:S(2)}, u32[]{:S(2)}) collective-permute-start(f32[2,64,256]{2,1,0:T(8,128)S(1)} %extend.1), channel_id=1, source_target_pairs={{1,2},{5,6},{9,10},{13,14},{17,18},{21,22},{25,26},{29,30}} | collective-permute-start | bytes 393224 | tf_op jit(solution)/shard_map/ppermute | solution.py:207
  20.9 2.1 %collective-permute-done.4.piece.across.one = f32[2,64,256]{2,1,0:T(8,128)S(1)} collective-permute-done((f32[2,64,256]{2,1,0:T(8,128)S(1)}, f32[2,64,256]{2,1,0:T(8,128)S(1)}, u32[]{:S(2)}, u32[]{:S(2)}) %collective-permute-start.4) | collective-permute-done | bytes 131104 | tf_op jit(solution)/shard_map/ppermute | solution.py:207
  23.1 1.3 %collective-permute-start.10 = (f32[2,64,256]{2,1,0:T(8,128)S(1)}, f32[2,64,256]{2,1,0:T(8,128)S(1)}, u32[]{:S(2)}, u32[]{:S(2)}) collective-permute-start(f32[2,64,256]{2,1,0:T(8,128)S(1)} %extend_other.1), channel_id=1, source_target_pairs={{1,3},{5,7},{9,11},{13,15},{17,19},{21,23},{25,27},{29,31}} | collective-permute-start | bytes 393224 | tf_op jit(solution)/shard_map/ppermute | solution.py:207
  24.3 0.7 %collective-permute-start.9 = (f32[2,64,256]{2,1,0:T(8,128)S(1)}, f32[2,64,256]{2,1,0:T(8,128)S(1)}, u32[]{:S(2)}, u32[]{:S(2)}) collective-permute-start(f32[2,64,256]{2,1,0:T(8,128)S(1)} %extend_other.1), channel_id=1, source_target_pairs={{1,2},{5,6},{9,10},{13,14},{17,18},{21,22},{25,26},{29,30}} | collective-permute-start | bytes 393224 | tf_op jit(solution)/shard_map/ppermute | solution.py:207
  25.0 0.0 collective-permute-done.7.two
  25.0 1.1 %collective-permute-start.8 = (f32[2,64,256]{2,1,0:T(8,128)S(1)}, f32[2,64,256]{2,1,0:T(8,128)S(1)}, u32[]{:S(2)}, u32[]{:S(2)}) collective-permute-start(f32[2,64,256]{2,1,0:T(8,128)S(1)} %collective-permute-done.7.two), channel_id=1, source_target_pairs={{0,1},{1,0},{2,3},{3,2},{4,5},{5,4},{6,7},{7,6},{8,9},{9,8},{10,11... | collective-permute-start | bytes 393224 | tf_op jit(solution)/shard_map/ppermute | solution.py:207
  26.1 3.4 %collective-permute-start.5 = (f32[2,64,256]{2,1,0:T(8,128)S(1)}, f32[2,64,256]{2,1,0:T(8,128)S(1)}, u32[]{:S(2)}, u32[]{:S(2)}) collective-permute-start(f32[2,64,256]{2,1,0:T(8,128)S(1)} %collective-permute-done.3.near.piece.one), channel_id=1, source_target_pairs={{0,4},{1,5},{2,6},{3,7},{4,0},{5,1},{6,2},{7,3},{8,12},{9,13},{10,... | collective-permute-start | bytes 393224 | tf_op jit(solution)/shard_map/ppermute | solution.py:207
  29.6 0.0 collective-permute-start.6
  29.6 0.3 collective-permute-done.10.three
  29.8 0.0 collective-permute-done.9.two
  29.8 3.5 %collective-permute-start.12 = (f32[2,64,256]{2,1,0:T(8,128)S(1)}, f32[2,64,256]{2,1,0:T(8,128)S(1)}, u32[]{:S(2)}, u32[]{:S(2)}) collective-permute-start(f32[2,64,256]{2,1,0:T(8,128)S(1)} %merge_across.1.across), channel_id=1, source_target_pairs={{0,4},{1,5},{2,6},{3,7},{4,0},{5,1},{6,2},{7,3},{8,12},{9,13},{10,... | collective-permute-start | bytes 393224 | tf_op jit(solution)/shard_map/ppermute | solution.py:207
  33.4 0.0 collective-permute-done.8.three
  33.4 0.5 %collective-permute-start.11 = (f32[2,64,256]{2,1,0:T(8,128)S(1)}, f32[2,64,256]{2,1,0:T(8,128)S(1)}, u32[]{:S(2)}, u32[]{:S(2)}) collective-permute-start(f32[2,64,256]{2,1,0:T(8,128)S(1)} %merge_near.1.near), channel_id=1, source_target_pairs={{0,4},{1,5},{2,6},{3,7},{4,0},{5,1},{6,2},{7,3},{8,12},{9,13},{10,... | collective-permute-start | bytes 393224 | tf_op jit(solution)/shard_map/ppermute | solution.py:207
  33.9 0.0 collective-permute-done.5.far
  33.9 0.0 collective-permute-done.6.far_across
  33.9 1.1 %left.1 = f32[2,2,256,256]{3,2,1,0:T(8,128)S(1)} custom-call(f32[2,2,256,256]{3,2,1,0:T(8,128)S(1)} %before.1, f32[2,64,256]{2,1,0:T(8,128)S(1)} %collective-permute-done.3.near.piece.one, f32[2,64,256]{2,1,0:T(8,128)S(1)} %collective-permute-done.4.piece.across.one, f32[2,64,256]{2,1,0:T(8,128)S(1)} %collective-permute-done.5.far, ...), custom_call_target="tpu_custom_call" | custom-call | tf_op jit(solution)/shard_map/left/pallas_call | solution.py:60
  35.0 1.4 %near.1._ = f32[1,1,2,2,256,256]{5,4,3,2,1,0:T(8,128)} custom-call(f32[2,2,256,256]{3,2,1,0:T(8,128)S(1)} %left.1, f32[2,64,256]{2,1,0:T(8,128)S(1)} %merge_near.1.near, f32[2,64,256]{2,1,0:T(8,128)S(1)} %merge_across.1.across), custom_call_target="tpu_custom_call" | custom-call | tf_op jit(solution)/shard_map/near/pallas_call | solution.py:60
  36.4 0.0 collective-permute-done.12.far_across
  36.4 0.0 collective-permute-done.11.far
  36.4 1.4 %far.1 = f32[1,1,2,2,256,256]{5,4,3,2,1,0:T(8,128)} custom-call(f32[1,1,2,2,256,256]{5,4,3,2,1,0:T(8,128)} %near.1._, f32[2,2,256,256]{3,2,1,0:T(8,128)S(1)} %left.1, f32[2,64,256]{2,1,0:T(8,128)S(1)} %collective-permute-done.11.far, f32[2,64,256]{2,1,0:T(8,128)S(1)} %collective-permute-done.12.far_across), custom_call_target="tpu_custom_call", output_to_operand_aliasing={{}: (0, {})} | custom-call | tf_op jit(solution)/shard_map/far/pallas_call | solution.py:60
  (4 shorter events, 0.0 us)
Async XLA Ops:
  0.0 1.2 %copy-start = (f32[1,1,2,2,256,256]{5,4,3,2,1,0:T(8,128)S(1)}, f32[1,1,2,2,256,256]{5,4,3,2,1,0:T(8,128)}, u32[]{:S(2)}) copy-start(f32[1,1,2,2,256,256]{5,4,3,2,1,0:T(8,128)} %u.3) | copy-start | bytes 3145732
  1.9 15.1 %copy-start.1 = (f32[1,1,2,2,256,256]{5,4,3,2,1,0:T(8,128)S(1)}, f32[1,1,2,2,256,256]{5,4,3,2,1,0:T(8,128)}, u32[]{:S(2)}) copy-start(f32[1,1,2,2,256,256]{5,4,3,2,1,0:T(8,128)} %u.3) | copy-start | bytes 3145732
  2.0 2.3 %collective-permute-start = (f32[2,256,256]{2,1,0:T(8,128)S(1)}, f32[2,256,256]{2,1,0:T(8,128)S(1)}, u32[]{:S(2)}, u32[]{:S(2)}) collective-permute-start(f32[2,256,256]{2,1,0:T(8,128)S(1)} %get-tuple-element.18.mine), channel_id=1, source_target_pairs={{0,4},{1,5},{2,6},{3,7},{4,0},{5,1},{6,2},{7,3},{8,12},{9,13},{10,... | collective-permute-start | bytes 1572872 | tf_op jit(solution)/shard_map/ppermute | solution.py:207
  4.9 7.6 %collective-permute-start.1 = (f32[256,256]{1,0:T(8,128)S(1)}, f32[256,256]{1,0:T(8,128)S(1)}, u32[]{:S(2)}, u32[]{:S(2)}) collective-permute-start(f32[256,256]{1,0:T(8,128)S(1)} %get-tuple-element.20), channel_id=1, source_target_pairs={{0,8},{1,9},{2,10},{3,11},{4,12},{5,13},{6,14},{7,15},{8,0},{9,1},... | collective-permute-start | bytes 786440 | tf_op jit(solution)/shard_map/ppermute | solution.py:207
  12.4 2.4 %collective-permute-start.2 = (f32[256,256]{1,0:T(8,128)S(1)}, f32[256,256]{1,0:T(8,128)S(1)}, u32[]{:S(2)}, u32[]{:S(2)}) collective-permute-start(f32[256,256]{1,0:T(8,128)S(1)} %collective-permute-done.1.near), channel_id=1, source_target_pairs={{0,4},{1,5},{2,6},{3,7},{4,0},{5,1},{6,2},{7,3},{8,12},{9,13},{10,... | collective-permute-start | bytes 786440 | tf_op jit(solution)/shard_map/ppermute | solution.py:207
  15.5 4.8 %collective-permute-start.3 = (f32[2,64,256]{2,1,0:T(8,128)S(1)}, f32[2,64,256]{2,1,0:T(8,128)S(1)}, u32[]{:S(2)}, u32[]{:S(2)}) collective-permute-start(f32[2,64,256]{2,1,0:T(8,128)S(1)} %get-tuple-element.21), channel_id=1, source_target_pairs={{0,1},{1,0},{2,3},{3,2},{4,5},{5,4},{6,7},{7,6},{8,9},{9,8},{10,11... | collective-permute-start | bytes 393224 | tf_op jit(solution)/shard_map/ppermute | solution.py:207
  15.7 7.4 %collective-permute-start.4 = (f32[2,64,256]{2,1,0:T(8,128)S(1)}, f32[2,64,256]{2,1,0:T(8,128)S(1)}, u32[]{:S(2)}, u32[]{:S(2)}) collective-permute-start(f32[2,64,256]{2,1,0:T(8,128)S(1)} %get-tuple-element.25), channel_id=1, source_target_pairs={{0,1},{1,0},{2,3},{3,2},{4,5},{5,4},{6,7},{7,6},{8,9},{9,8},{10,11... | collective-permute-start | bytes 393224 | tf_op jit(solution)/shard_map/ppermute | solution.py:207
  20.3 4.8 %collective-permute-start.7 = (f32[2,64,256]{2,1,0:T(8,128)S(1)}, f32[2,64,256]{2,1,0:T(8,128)S(1)}, u32[]{:S(2)}, u32[]{:S(2)}) collective-permute-start(f32[2,64,256]{2,1,0:T(8,128)S(1)} %extend.1), channel_id=1, source_target_pairs={{1,2},{5,6},{9,10},{13,14},{17,18},{21,22},{25,26},{29,30}} | collective-permute-start | bytes 393224 | tf_op jit(solution)/shard_map/ppermute | solution.py:207
  23.1 6.7 %collective-permute-start.10 = (f32[2,64,256]{2,1,0:T(8,128)S(1)}, f32[2,64,256]{2,1,0:T(8,128)S(1)}, u32[]{:S(2)}, u32[]{:S(2)}) collective-permute-start(f32[2,64,256]{2,1,0:T(8,128)S(1)} %extend_other.1), channel_id=1, source_target_pairs={{1,3},{5,7},{9,11},{13,15},{17,19},{21,23},{25,27},{29,31}} | collective-permute-start | bytes 393224 | tf_op jit(solution)/shard_map/ppermute | solution.py:207
  24.3 5.5 %collective-permute-start.9 = (f32[2,64,256]{2,1,0:T(8,128)S(1)}, f32[2,64,256]{2,1,0:T(8,128)S(1)}, u32[]{:S(2)}, u32[]{:S(2)}) collective-permute-start(f32[2,64,256]{2,1,0:T(8,128)S(1)} %extend_other.1), channel_id=1, source_target_pairs={{1,2},{5,6},{9,10},{13,14},{17,18},{21,22},{25,26},{29,30}} | collective-permute-start | bytes 393224 | tf_op jit(solution)/shard_map/ppermute | solution.py:207
  25.0 8.3 %collective-permute-start.8 = (f32[2,64,256]{2,1,0:T(8,128)S(1)}, f32[2,64,256]{2,1,0:T(8,128)S(1)}, u32[]{:S(2)}, u32[]{:S(2)}) collective-permute-start(f32[2,64,256]{2,1,0:T(8,128)S(1)} %collective-permute-done.7.two), channel_id=1, source_target_pairs={{0,1},{1,0},{2,3},{3,2},{4,5},{5,4},{6,7},{7,6},{8,9},{9,8},{10,11... | collective-permute-start | bytes 393224 | tf_op jit(solution)/shard_map/ppermute | solution.py:207
  26.1 7.8 %collective-permute-start.5 = (f32[2,64,256]{2,1,0:T(8,128)S(1)}, f32[2,64,256]{2,1,0:T(8,128)S(1)}, u32[]{:S(2)}, u32[]{:S(2)}) collective-permute-start(f32[2,64,256]{2,1,0:T(8,128)S(1)} %collective-permute-done.3.near.piece.one), channel_id=1, source_target_pairs={{0,4},{1,5},{2,6},{3,7},{4,0},{5,1},{6,2},{7,3},{8,12},{9,13},{10,... | collective-permute-start | bytes 393224 | tf_op jit(solution)/shard_map/ppermute | solution.py:207
  29.6 4.4 %collective-permute-start.6 = (f32[2,64,256]{2,1,0:T(8,128)S(1)}, f32[2,64,256]{2,1,0:T(8,128)S(1)}, u32[]{:S(2)}, u32[]{:S(2)}) collective-permute-start(f32[2,64,256]{2,1,0:T(8,128)S(1)} %collective-permute-done.4.piece.across.one), channel_id=1, source_target_pairs={{0,4},{1,5},{2,6},{3,7},{4,0},{5,1},{6,2},{7,3},{8,12},{9,13},{10,... | collective-permute-start | bytes 393224 | tf_op jit(solution)/shard_map/ppermute | solution.py:207
  29.8 6.5 %collective-permute-start.12 = (f32[2,64,256]{2,1,0:T(8,128)S(1)}, f32[2,64,256]{2,1,0:T(8,128)S(1)}, u32[]{:S(2)}, u32[]{:S(2)}) collective-permute-start(f32[2,64,256]{2,1,0:T(8,128)S(1)} %merge_across.1.across), channel_id=1, source_target_pairs={{0,4},{1,5},{2,6},{3,7},{4,0},{5,1},{6,2},{7,3},{8,12},{9,13},{10,... | collective-permute-start | bytes 393224 | tf_op jit(solution)/shard_map/ppermute | solution.py:207
  33.4 3.0 %collective-permute-start.11 = (f32[2,64,256]{2,1,0:T(8,128)S(1)}, f32[2,64,256]{2,1,0:T(8,128)S(1)}, u32[]{:S(2)}, u32[]{:S(2)}) collective-permute-start(f32[2,64,256]{2,1,0:T(8,128)S(1)} %merge_near.1.near), channel_id=1, source_target_pairs={{0,4},{1,5},{2,6},{3,7},{4,0},{5,1},{6,2},{7,3},{8,12},{9,13},{10,... | collective-permute-start | bytes 393224 | tf_op jit(solution)/shard_map/ppermute | solution.py:207

commit v4 on v3

--- a/solution.py
+++ b/solution.py
@@ -56,12 +56,12 @@
 
 def call(body, outs, *operands, name, scratch=(), hbm_out=False, alias=None):
     whole, far = pl.BlockSpec(memory_space=pltpu.VMEM), pl.BlockSpec(memory_space=pl.ANY)
-    shapes = [jax.ShapeDtypeStruct(shape, F32) for shape in outs]
+    shapes = [out if isinstance(out, jax.ShapeDtypeStruct) else jax.ShapeDtypeStruct(out, F32) for out in outs]
     return pl.pallas_call(
         body,
         out_shape=shapes,
         in_specs=[far if i == alias else whole for i in range(len(operands))],
-        out_specs=[far if hbm_out else whole] * len(outs),
+        out_specs=[far if hbm_out and i == 0 else whole for i in range(len(outs))],
         input_output_aliases={} if alias is None else {alias: 0},
         scratch_shapes=list(scratch),
         compiler_params=pltpu.CompilerParams(vmem_limit_bytes=32 << 20),
@@ -95,12 +95,27 @@
     return pick(x == 0, mine, other), pick(x == 0, other, mine)
 
 
-def window_kernel(chip, near, far, window, own, other):
-    x, k, _ = place()
-    put(window, product(*ordered(x, k, chip, near, far)))
-    rows = own.shape[1]
-    for strip, at in ((own, x), (other, 1 - x)):
-        strip[...] = window[:, pl.ds(pl.multiple_of((2 * k + at) * rows, rows), rows), :]
+def strips_kernel(chip, near, far, own, other, scratch):
+    x, k, w = place()
+
+    @pl.when(w % 2 == 0)
+    def _():
+        one, two = ordered(x, k, chip, near, far)
+        put(scratch, one)
+        rows = own.shape[1]
+        half = scratch[:, pl.ds(pl.multiple_of(2 * k * rows, 2 * rows), 2 * rows), :]
+        value = product((half[0], half[1]), two)
+        top, low = tuple(v[:rows] for v in value), tuple(v[rows:] for v in value)
+        put(own, pick(x == 0, top, low))
+        put(other, pick(x == 0, low, top))
+
+
+def window_kernel(chip, near, far, window):
+    x, k, w = place()
+
+    @pl.when(w == 1)
+    def _():
+        put(window, product(*ordered(x, k, chip, near, far)))
 
 
 def extend_kernel(piece, window, out):
@@ -135,18 +150,23 @@
     put(out.at[1], product(pair(block), before, NT))
 
 
-def left_kernel(before, near, across, far, far_across, out):
+def left_kernel(before, near, across, far, far_across, high, low):
     _, _, w = place()
+
+    def store(slot, value):
+        for plane in range(2):
+            high[slot, plane], low[slot, plane] = halves(value[plane])
 
     @pl.when(w == 3)
     def _():
         window = whole(near, across, far, far_across)
         for slot in range(2):
-            put(out.at[slot], product(pair(before[slot]), window, NT))
-
-    @pl.when(w != 3)
-    def _():
-        out[...] = before[...]
+            store(slot, product(pair(before[slot]), window, NT))
+
+    @pl.when((w == 1) | (w == 2))
+    def _():
+        for slot in range(2):
+            store(slot, pair(before[slot]))
 
 
 def merge_kernel(one, two, three, out):
@@ -154,30 +174,34 @@
     out[...] = jnp.where(w == 1, one[...], jnp.where(w == 2, two[...], three[...]))
 
 
-def send(out, columns, at, sems, left, offset):
-    width, copies = columns.shape[-1], []
-    high, low = halves(jnp.concatenate(offset, axis=0))
+def columns_of(high, low, slot, offset):
+    width = offset[0].shape[0] // 2
     dot = functools.partial(lax.dot_general, dimension_numbers=NT, preferred_element_type=F32)
-    for slot in range(2):
-        parts = []
-        for plane in range(2):
-            a, al = halves(left[slot, plane])
-            parts.append(dot(a, high) + (dot(a, low) + dot(al, high)))
-        real, imag = parts
-        columns[slot, 0] = real[:, :width] - imag[:, width:]
-        columns[slot, 1] = real[:, width:] + imag[:, :width]
-        copies.append(pltpu.make_async_copy(columns.at[slot], out.at[0, 0, slot, :, :, at], sems.at[slot]))
-        copies[-1].start()
-    return copies
-
-
-def near_kernel(left, near, across, out, columns, sems):
+    parts = []
+    for plane in range(2):
+        a, al = high[slot, plane], low[slot, plane]
+        parts.append(dot(a, offset[0]) + (dot(a, offset[1]) + dot(al, offset[0])))
+    real, imag = parts
+    return real[:, :width] - imag[:, width:], real[:, width:] + imag[:, :width]
+
+
+def near_kernel(high, low, early, late, out):
+    x, _, w = place()
+
+    @pl.when(w != 0)
+    def _():
+        offset = halves(jnp.concatenate(half(jnp.where(w == 3, 1 - x, x), early, late), axis=0))
+        for slot in range(2):
+            put(out.at[slot], columns_of(high, low, slot, offset))
+
+
+def far_kernel(before, near, high, low, early, late, out, far, sems):
     x, k, w = place()
-    width = columns.shape[-1]
+    width = near.shape[-1]
 
     @pl.when(w == 0)
     def _():
-        copies = [pltpu.make_async_copy(left.at[s], out.at[0, 0, s], sems.at[s]) for s in range(2)]
+        copies = [pltpu.make_async_copy(before.at[s], out.at[0, 0, s], sems.at[s, 0]) for s in range(2)]
         for copy in copies:
             copy.start()
         for copy in copies:
@@ -185,19 +209,18 @@
 
     @pl.when(w != 0)
     def _():
-        at = pl.ds(pl.multiple_of(k * width, width), width)
-        for copy in send(out, columns, at, sems, left, half(x, near, across)):
-            copy.wait()
-
-
-def far_kernel(_, left, far, far_across, out, columns, sems):
-    x, k, w = place()
-    width = columns.shape[-1]
-
-    @pl.when(w != 0)
-    def _():
-        at = pl.ds(pl.multiple_of((1 - k) * width, width), width)
-        for copy in send(out, columns, at, sems, left, half(x, far, far_across)):
+        def start(columns, slot, core, which):
+            at = pl.ds(pl.multiple_of(core * width, width), width)
+            copy = pltpu.make_async_copy(columns.at[slot], out.at[0, 0, slot, :, :, at], sems.at[slot, which])
+            copy.start()
+            return copy
+
+        copies = [start(near, slot, k, 0) for slot in range(2)]
+        offset = halves(jnp.concatenate(half(jnp.where(w == 3, 1 - x, x), early, late), axis=0))
+        for slot in range(2):
+            put(far.at[slot], columns_of(high, low, slot, offset))
+            copies.append(start(far, slot, 1 - k, 1))
+        for copy in copies:
             copy.wait()
 
 
@@ -215,6 +238,7 @@
     chips = [((t, v), (t ^ 2, v)) for t, v in spots]
     twins = [((t, v), (t, v ^ 1)) for t, v in spots]
     one_two = [((t, 1), (t, 2)) for t in range(4)]
+    two_three = [((t, 2), (t, 3)) for t in range(4)]
     one_three = [((t, 1), (t, 3)) for t in range(4)]
     tie = lax.optimization_barrier
 
@@ -223,33 +247,39 @@
     chip, plane = call(chip_kernel, [full, full[1:]], turned, turned_other, name="chip")
     near_chip = permute(plane, chips)
     far_chip = permute(near_chip, cores)
-    window, own, other = call(window_kernel, [full, strip, strip], chip, near_chip, far_chip, name="window")
-
-    one, one_other = permute(own, twins), permute(other, twins)
+    own, other = call(
+        strips_kernel, [strip, strip], chip, near_chip, far_chip, name="strips", scratch=[pltpu.VMEM(full, F32)]
+    )
+    one = permute(own, twins)
     (before,) = call(
         before_kernel, [(2, *full)], unitaries, block, turned_other, near_chip, far_chip, name="before"
     )
+    (window,) = call(window_kernel, [full], chip, near_chip, far_chip, name="window")
+    other, before, window = tie((other, before, window))
+    one_other = permute(other, twins)
     one, before = tie((one, before))
     (both,) = call(extend_kernel, [strip], one, window, name="extend")
     two = permute(both, one_two)
     (both_other,) = call(extend_kernel, [strip], one_other, window, name="extend_other")
     three_other = permute(both_other, one_three)
-    three = permute(two, twins)
+    three = permute(two, two_three)
     two_other = permute(both_other, one_two)
 
-    (across,) = call(merge_kernel, [strip], one_other, two_other, three_other, name="merge_across")
-    far_across = permute(across, cores)
-    three, across = tie((three, across))
-    (near,) = call(merge_kernel, [strip], one, two, three, name="merge_near")
-    far = permute(near, cores)
+    (early,) = call(merge_kernel, [strip], one, two, three_other, name="merge_early")
+    far_early = permute(early, cores)
     one, one_other, _ = tie((one, one_other, both_other))
-    (left,) = call(
-        left_kernel, [(2, *full)], before, one, one_other, permute(one, cores), permute(one_other, cores), name="left"
-    )
-    scratch = pltpu.VMEM((2, 2, width, width // 2), F32), pltpu.SemaphoreType.DMA((2,))
-    shape = [unitaries.shape]
-    (out,) = call(near_kernel, shape, left, near, across, name="near", scratch=scratch, hbm_out=True)
-    (out,) = call(far_kernel, shape, out, left, far, far_across, name="far", scratch=scratch, hbm_out=True, alias=0)
+    parts = [jax.ShapeDtypeStruct((2, *full), jnp.bfloat16)] * 2
+    high, low = call(
+        left_kernel, parts, before, one, one_other, permute(one, cores), permute(one_other, cores), name="left"
+    )
+    two_other, three, high, early = tie((two_other, three, high, early))
+    (late,) = call(merge_kernel, [strip], one_other, two_other, three, name="merge_late")
+    far_late = permute(late, cores)
+    half_width = (2, 2, width, width // 2)
+    (near,) = call(near_kernel, [half_width], high, low, early, late, name="near")
+    scratch = pltpu.VMEM(half_width, F32), pltpu.SemaphoreType.DMA((2, 2))
+    operands = before, near, high, low, far_early, far_late
+    (out,) = call(far_kernel, [unitaries.shape], *operands, name="far", scratch=scratch, hbm_out=True)
     return out
 
 

time: 38.2 us -> 37 us (0.969)
  starting transfers between devices: 15.9 us -> 13.1 us
  waiting for transfers between devices: 13.1 us -> 15.6 us
  Pallas kernels: 7.41 us -> 6.08 us
  local copies, waits for them, and re-layouts: 1.23 us -> 1.75 us
    ppermute x13, starting transfers between devices: 15.9 us -> 13.1 us  [permute(): return lax.ppermute(value, AXES, flat)]
    ppermute x13, waiting for transfers between devices: 13.1 us -> 15.6 us  [permute(): return lax.ppermute(value, AXES, flat)]
    pallas_call x11 -> x12, Pallas kernels: 7.41 us -> 6.08 us  [call(): pl.pallas_call(body, out_shape=shapes, in_specs=[far if i == alias else w...]
    unnamed x4, local copies, waits for them, and re-layouts: 1.23 us -> 1.75 us
  transfers between devices with their start and end apart: 13 -> 13, of which waited for: 6 -> 8; matrix products, arithmetic and copies ran while one was open for 0% -> 0% of each run, Pallas kernels for 11% -> 9%
where the time goes in v4:
time: 37 us; the launch traced here: 36.7 us
  waiting for transfers between devices  15.6 us (42%)
  starting transfers between devices  13.1 us (35%)
  Pallas kernels  6.08 us (16%)
  local copies, waits for them, and re-layouts  1.75 us (5%)
    ppermute x13, waiting for transfers between devices, permute(): return lax.ppermute(value, AXES, flat)  15.6 us
    ppermute x13, starting transfers between devices, permute(): return lax.ppermute(value, AXES, flat)  13.1 us
    pallas_call x12, Pallas kernels, call(): pl.pallas_call(body, out_shape=shapes, in_specs=[far if i == alias else w...  6.08 us
    unnamed x4, local copies, waits for them, and re-layouts  1.75 us
  transfers between devices with their start and end apart: 13, of which 8 were waited for; matrix products, arithmetic and copies ran while one was open for 0% of the time, Pallas kernels for 9%

profile of v4, /device:TPU:29, one launch (start us, length us, event | category | flops | bytes accessed | tf_op | source)
XLA Modules:
  0.0 36.7 jit_solution(5658371650611238039)
XLA Ops:
  0.0 0.0 copy-start
  0.0 1.2 %copy-done = f32[1,1,2,2,256,256]{5,4,3,2,1,0:T(8,128)S(1)} copy-done((f32[1,1,2,2,256,256]{5,4,3,2,1,0:T(8,128)S(1)}, f32[1,1,2,2,256,256]{5,4,3,2,1,0:T(8,128)}, u32[]{:S(2)}) %copy-start) | copy-done | bytes 1048600
  1.2 0.7 %block.1 = (f32[2,256,256]{2,1,0:T(8,128)S(1)}, f32[2,256,256]{2,1,0:T(8,128)S(1)}) custom-call(f32[1,1,2,2,256,256]{5,4,3,2,1,0:T(8,128)S(1)} %copy-done), custom_call_target="tpu_custom_call" | custom-call | tf_op jit(solution)/shard_map/block/pallas_call | solution.py:60
  1.9 0.7 %collective-permute-start = (f32[2,256,256]{2,1,0:T(8,128)S(1)}, f32[2,256,256]{2,1,0:T(8,128)S(1)}, u32[]{:S(2)}, u32[]{:S(2)}) collective-permute-start(f32[2,256,256]{2,1,0:T(8,128)S(1)} %get-tuple-element.24.mine), channel_id=1, source_target_pairs={{0,4},{1,5},{2,6},{3,7},{4,0},{5,1},{6,2},{7,3},{8,12},{9,13},{10,... | collective-permute-start | bytes 1572872 | tf_op jit(solution)/shard_map/ppermute | solution.py:230
  2.7 1.5 %collective-permute-done.theirs.turned = f32[2,256,256]{2,1,0:T(8,128)S(1)} collective-permute-done((f32[2,256,256]{2,1,0:T(8,128)S(1)}, f32[2,256,256]{2,1,0:T(8,128)S(1)}, u32[]{:S(2)}, u32[]{:S(2)}) %collective-permute-start) | collective-permute-done | bytes 524320 | tf_op jit(solution)/shard_map/ppermute | solution.py:230
  4.2 0.6 %chip.1 = (f32[2,256,256]{2,1,0:T(8,128)S(1)}, f32[256,256]{1,0:T(8,128)S(1)}) custom-call(f32[2,256,256]{2,1,0:T(8,128)S(1)} %get-tuple-element.24.mine, f32[2,256,256]{2,1,0:T(8,128)S(1)} %collective-permute-done.theirs.turned), custom_call_target="tpu_custom_call" | custom-call | tf_op jit(solution)/shard_map/chip/pallas_call | solution.py:60
  4.8 1.3 %collective-permute-start.1 = (f32[256,256]{1,0:T(8,128)S(1)}, f32[256,256]{1,0:T(8,128)S(1)}, u32[]{:S(2)}, u32[]{:S(2)}) collective-permute-start(f32[256,256]{1,0:T(8,128)S(1)} %get-tuple-element.26), channel_id=1, source_target_pairs={{0,8},{1,9},{2,10},{3,11},{4,12},{5,13},{6,14},{7,15},{8,0},{9,1},... | collective-permute-start | bytes 786440 | tf_op jit(solution)/shard_map/ppermute | solution.py:230
  6.1 6.3 %collective-permute-done.1.near = f32[256,256]{1,0:T(8,128)S(1)} collective-permute-done((f32[256,256]{1,0:T(8,128)S(1)}, f32[256,256]{1,0:T(8,128)S(1)}, u32[]{:S(2)}, u32[]{:S(2)}) %collective-permute-start.1) | collective-permute-done | bytes 262176 | tf_op jit(solution)/shard_map/ppermute | solution.py:230
  12.4 1.2 %collective-permute-start.2 = (f32[256,256]{1,0:T(8,128)S(1)}, f32[256,256]{1,0:T(8,128)S(1)}, u32[]{:S(2)}, u32[]{:S(2)}) collective-permute-start(f32[256,256]{1,0:T(8,128)S(1)} %collective-permute-done.1.near), channel_id=1, source_target_pairs={{0,4},{1,5},{2,6},{3,7},{4,0},{5,1},{6,2},{7,3},{8,12},{9,13},{10,... | collective-permute-start | bytes 786440 | tf_op jit(solution)/shard_map/ppermute | solution.py:230
  13.6 1.2 %collective-permute-done.2.far = f32[256,256]{1,0:T(8,128)S(1)} collective-permute-done((f32[256,256]{1,0:T(8,128)S(1)}, f32[256,256]{1,0:T(8,128)S(1)}, u32[]{:S(2)}, u32[]{:S(2)}) %collective-permute-start.2) | collective-permute-done | bytes 262176 | tf_op jit(solution)/shard_map/ppermute | solution.py:230
  14.8 0.0 copy-start.1
  14.8 0.7 %collective-permute-start.3 = (f32[2,64,256]{2,1,0:T(8,128)S(1)}, f32[2,64,256]{2,1,0:T(8,128)S(1)}, u32[]{:S(2)}, u32[]{:S(2)}) collective-permute-start(f32[2,64,256]{2,1,0:T(8,128)S(1)} %get-tuple-element.27), channel_id=1, source_target_pairs={{0,1},{1,0},{2,3},{3,2},{4,5},{5,4},{6,7},{7,6},{8,9},{9,8},{10,11... | collective-permute-start | bytes 393224 | tf_op jit(solution)/shard_map/ppermute | solution.py:230
  15.5 0.5 %copy-done.1 = f32[1,1,2,2,256,256]{5,4,3,2,1,0:T(8,128)S(1)} copy-done((f32[1,1,2,2,256,256]{5,4,3,2,1,0:T(8,128)S(1)}, f32[1,1,2,2,256,256]{5,4,3,2,1,0:T(8,128)}, u32[]{:S(2)}) %copy-start.1) | copy-done | bytes 1048600
  16.0 1.6 %before.1 = f32[2,2,256,256]{3,2,1,0:T(8,128)S(1)} custom-call(f32[1,1,2,2,256,256]{5,4,3,2,1,0:T(8,128)S(1)} %copy-done.1, f32[2,256,256]{2,1,0:T(8,128)S(1)} %get-tuple-element.29.block, f32[2,256,256]{2,1,0:T(8,128)S(1)} %collective-permute-done.theirs.turned, f32[256,256]{1,0:T(8,128)S(1)} %collective-permute-done.1.near, ...), custom_call_target="tpu_custom_call" | custom-call | tf_op jit(solution)/shard_map/before/pallas_call | solution.py:60
  17.6 0.7 %collective-permute-start.4 = (f32[2,64,256]{2,1,0:T(8,128)S(1)}, f32[2,64,256]{2,1,0:T(8,128)S(1)}, u32[]{:S(2)}, u32[]{:S(2)}) collective-permute-start(f32[2,64,256]{2,1,0:T(8,128)S(1)} %get-tuple-element.32), channel_id=1, source_target_pairs={{0,1},{1,0},{2,3},{3,2},{4,5},{5,4},{6,7},{7,6},{8,9},{9,8},{10,11... | collective-permute-start | bytes 393224 | tf_op jit(solution)/shard_map/ppermute | solution.py:230
  18.3 1.2 %collective-permute-done.3.piece.near.one = f32[2,64,256]{2,1,0:T(8,128)S(1)} collective-permute-done((f32[2,64,256]{2,1,0:T(8,128)S(1)}, f32[2,64,256]{2,1,0:T(8,128)S(1)}, u32[]{:S(2)}, u32[]{:S(2)}) %collective-permute-start.3) | collective-permute-done | bytes 131104 | tf_op jit(solution)/shard_map/ppermute | solution.py:230
  19.5 0.7 %collective-permute-start.6 = (f32[2,64,256]{2,1,0:T(8,128)S(1)}, f32[2,64,256]{2,1,0:T(8,128)S(1)}, u32[]{:S(2)}, u32[]{:S(2)}) collective-permute-start(f32[2,64,256]{2,1,0:T(8,128)S(1)} %extend.1), channel_id=1, source_target_pairs={{1,2},{5,6},{9,10},{13,14},{17,18},{21,22},{25,26},{29,30}} | collective-permute-start | bytes 393224 | tf_op jit(solution)/shard_map/ppermute | solution.py:230
  20.2 2.2 %collective-permute-done.4.piece.across.one = f32[2,64,256]{2,1,0:T(8,128)S(1)} collective-permute-done((f32[2,64,256]{2,1,0:T(8,128)S(1)}, f32[2,64,256]{2,1,0:T(8,128)S(1)}, u32[]{:S(2)}, u32[]{:S(2)}) %collective-permute-start.4) | collective-permute-done | bytes 131104 | tf_op jit(solution)/shard_map/ppermute | solution.py:230
  22.4 1.3 %collective-permute-start.10 = (f32[2,64,256]{2,1,0:T(8,128)S(1)}, f32[2,64,256]{2,1,0:T(8,128)S(1)}, u32[]{:S(2)}, u32[]{:S(2)}) collective-permute-start(f32[2,64,256]{2,1,0:T(8,128)S(1)} %extend_other.1), channel_id=1, source_target_pairs={{1,3},{5,7},{9,11},{13,15},{17,19},{21,23},{25,27},{29,31}} | collective-permute-start | bytes 393224 | tf_op jit(solution)/shard_map/ppermute | solution.py:230
  23.7 1.3 %collective-permute-start.8 = (f32[2,64,256]{2,1,0:T(8,128)S(1)}, f32[2,64,256]{2,1,0:T(8,128)S(1)}, u32[]{:S(2)}, u32[]{:S(2)}) collective-permute-start(f32[2,64,256]{2,1,0:T(8,128)S(1)} %collective-permute-done.3.piece.near.one), channel_id=1, source_target_pairs={{0,4},{1,5},{2,6},{3,7},{4,0},{5,1},{6,2},{7,3},{8,12},{9,13},{10,... | collective-permute-start | bytes 393224 | tf_op jit(solution)/shard_map/ppermute | solution.py:230
  24.9 0.1 collective-permute-start.9
  25.0 0.7 %collective-permute-start.5 = (f32[2,64,256]{2,1,0:T(8,128)S(1)}, f32[2,64,256]{2,1,0:T(8,128)S(1)}, u32[]{:S(2)}, u32[]{:S(2)}) collective-permute-start(f32[2,64,256]{2,1,0:T(8,128)S(1)} %extend_other.1), channel_id=1, source_target_pairs={{1,2},{5,6},{9,10},{13,14},{17,18},{21,22},{25,26},{29,30}} | collective-permute-start | bytes 393224 | tf_op jit(solution)/shard_map/ppermute | solution.py:230
  25.7 0.0 collective-permute-done.6.two
  25.7 1.3 %collective-permute-start.7 = (f32[2,64,256]{2,1,0:T(8,128)S(1)}, f32[2,64,256]{2,1,0:T(8,128)S(1)}, u32[]{:S(2)}, u32[]{:S(2)}) collective-permute-start(f32[2,64,256]{2,1,0:T(8,128)S(1)} %collective-permute-done.6.two), channel_id=1, source_target_pairs={{2,3},{6,7},{10,11},{14,15},{18,19},{22,23},{26,27},{30,31}} | collective-permute-start | bytes 393224 | tf_op jit(solution)/shard_map/ppermute | solution.py:230
  27.0 2.0 %collective-permute-done.10.three = f32[2,64,256]{2,1,0:T(8,128)S(1)} collective-permute-done((f32[2,64,256]{2,1,0:T(8,128)S(1)}, f32[2,64,256]{2,1,0:T(8,128)S(1)}, u32[]{:S(2)}, u32[]{:S(2)}) %collective-permute-start.10) | collective-permute-done | bytes 131104 | tf_op jit(solution)/shard_map/ppermute | solution.py:230
  29.0 2.5 %collective-permute-start.11 = (f32[2,64,256]{2,1,0:T(8,128)S(1)}, f32[2,64,256]{2,1,0:T(8,128)S(1)}, u32[]{:S(2)}, u32[]{:S(2)}) collective-permute-start(f32[2,64,256]{2,1,0:T(8,128)S(1)} %merge_early.1.early), channel_id=1, source_target_pairs={{0,4},{1,5},{2,6},{3,7},{4,0},{5,1},{6,2},{7,3},{8,12},{9,13},{10,... | collective-permute-start | bytes 393224 | tf_op jit(solution)/shard_map/ppermute | solution.py:230
  31.5 0.0 collective-permute-done.8.far
  31.5 0.0 collective-permute-done.9.far_across
  31.5 1.1 %left.1 = (bf16[2,2,256,256]{3,2,1,0:T(8,128)(2,1)S(1)}, bf16[2,2,256,256]{3,2,1,0:T(8,128)(2,1)S(1)}) custom-call(f32[2,2,256,256]{3,2,1,0:T(8,128)S(1)} %before.1, f32[2,64,256]{2,1,0:T(8,128)S(1)} %collective-permute-done.3.piece.near.one, f32[2,64,256]{2,1,0:T(8,128)S(1)} %collective-permute-done.4.piece.across.one, ...), custom_call_target="tpu_custom_call" | custom-call | tf_op jit(solution)/shard_map/left/pallas_call | solution.py:60
  32.6 0.0 collective-permute-done.5.two
  32.7 0.8 %collective-permute-done.7.three = f32[2,64,256]{2,1,0:T(8,128)S(1)} collective-permute-done((f32[2,64,256]{2,1,0:T(8,128)S(1)}, f32[2,64,256]{2,1,0:T(8,128)S(1)}, u32[]{:S(2)}, u32[]{:S(2)}) %collective-permute-start.7) | collective-permute-done | bytes 131104 | tf_op jit(solution)/shard_map/ppermute | solution.py:230
  33.5 0.7 %collective-permute-start.12 = (f32[2,64,256]{2,1,0:T(8,128)S(1)}, f32[2,64,256]{2,1,0:T(8,128)S(1)}, u32[]{:S(2)}, u32[]{:S(2)}) collective-permute-start(f32[2,64,256]{2,1,0:T(8,128)S(1)} %merge_late.1.late), channel_id=1, source_target_pairs={{0,4},{1,5},{2,6},{3,7},{4,0},{5,1},{6,2},{7,3},{8,12},{9,13},{10,... | collective-permute-start | bytes 393224 | tf_op jit(solution)/shard_map/ppermute | solution.py:230
  34.2 0.6 %near.1 = f32[2,2,256,128]{3,2,1,0:T(8,128)S(1)} custom-call(bf16[2,2,256,256]{3,2,1,0:T(8,128)(2,1)S(1)} %get-tuple-element.38.high, bf16[2,2,256,256]{3,2,1,0:T(8,128)(2,1)S(1)} %get-tuple-element.39.low, f32[2,64,256]{2,1,0:T(8,128)S(1)} %merge_early.1.early, f32[2,64,256]{2,1,0:T(8,128)S(1)} %merge_late.1.late), custom_call_target="tpu_custom_call" | custom-call | tf_op jit(solution)/shard_map/near/pallas_call | solution.py:60
  34.9 0.0 collective-permute-done.11.early
  34.9 0.4 collective-permute-done.12.late
  35.2 1.4 %far.1 = f32[1,1,2,2,256,256]{5,4,3,2,1,0:T(8,128)} custom-call(f32[2,2,256,256]{3,2,1,0:T(8,128)S(1)} %before.1, f32[2,2,256,128]{3,2,1,0:T(8,128)S(1)} %near.1, bf16[2,2,256,256]{3,2,1,0:T(8,128)(2,1)S(1)} %get-tuple-element.38.high, bf16[2,2,256,256]{3,2,1,0:T(8,128)(2,1)S(1)} %get-tuple-element.39.low, f32[2,64,256]{2,1,0:T(8,128)S(1)} %collective-permute-done.11.early, ...), custom_call_target="tpu_custom_call" | custom-call | tf_op jit(solution)/shard_map/far/pallas_call | solution.py:60
  (6 shorter events, 0.0 us)
Async XLA Ops:
  0.0 1.2 %copy-start = (f32[1,1,2,2,256,256]{5,4,3,2,1,0:T(8,128)S(1)}, f32[1,1,2,2,256,256]{5,4,3,2,1,0:T(8,128)}, u32[]{:S(2)}) copy-start(f32[1,1,2,2,256,256]{5,4,3,2,1,0:T(8,128)} %u.3) | copy-start | bytes 3145732
  1.9 2.3 %collective-permute-start = (f32[2,256,256]{2,1,0:T(8,128)S(1)}, f32[2,256,256]{2,1,0:T(8,128)S(1)}, u32[]{:S(2)}, u32[]{:S(2)}) collective-permute-start(f32[2,256,256]{2,1,0:T(8,128)S(1)} %get-tuple-element.24.mine), channel_id=1, source_target_pairs={{0,4},{1,5},{2,6},{3,7},{4,0},{5,1},{6,2},{7,3},{8,12},{9,13},{10,... | collective-permute-start | bytes 1572872 | tf_op jit(solution)/shard_map/ppermute | solution.py:230
  4.8 7.6 %collective-permute-start.1 = (f32[256,256]{1,0:T(8,128)S(1)}, f32[256,256]{1,0:T(8,128)S(1)}, u32[]{:S(2)}, u32[]{:S(2)}) collective-permute-start(f32[256,256]{1,0:T(8,128)S(1)} %get-tuple-element.26), channel_id=1, source_target_pairs={{0,8},{1,9},{2,10},{3,11},{4,12},{5,13},{6,14},{7,15},{8,0},{9,1},... | collective-permute-start | bytes 786440 | tf_op jit(solution)/shard_map/ppermute | solution.py:230
  12.4 2.4 %collective-permute-start.2 = (f32[256,256]{1,0:T(8,128)S(1)}, f32[256,256]{1,0:T(8,128)S(1)}, u32[]{:S(2)}, u32[]{:S(2)}) collective-permute-start(f32[256,256]{1,0:T(8,128)S(1)} %collective-permute-done.1.near), channel_id=1, source_target_pairs={{0,4},{1,5},{2,6},{3,7},{4,0},{5,1},{6,2},{7,3},{8,12},{9,13},{10,... | collective-permute-start | bytes 786440 | tf_op jit(solution)/shard_map/ppermute | solution.py:230
  14.8 1.2 %copy-start.1 = (f32[1,1,2,2,256,256]{5,4,3,2,1,0:T(8,128)S(1)}, f32[1,1,2,2,256,256]{5,4,3,2,1,0:T(8,128)}, u32[]{:S(2)}) copy-start(f32[1,1,2,2,256,256]{5,4,3,2,1,0:T(8,128)} %u.3) | copy-start | bytes 3145732
  14.8 4.7 %collective-permute-start.3 = (f32[2,64,256]{2,1,0:T(8,128)S(1)}, f32[2,64,256]{2,1,0:T(8,128)S(1)}, u32[]{:S(2)}, u32[]{:S(2)}) collective-permute-start(f32[2,64,256]{2,1,0:T(8,128)S(1)} %get-tuple-element.27), channel_id=1, source_target_pairs={{0,1},{1,0},{2,3},{3,2},{4,5},{5,4},{6,7},{7,6},{8,9},{9,8},{10,11... | collective-permute-start | bytes 393224 | tf_op jit(solution)/shard_map/ppermute | solution.py:230
  17.6 4.8 %collective-permute-start.4 = (f32[2,64,256]{2,1,0:T(8,128)S(1)}, f32[2,64,256]{2,1,0:T(8,128)S(1)}, u32[]{:S(2)}, u32[]{:S(2)}) collective-permute-start(f32[2,64,256]{2,1,0:T(8,128)S(1)} %get-tuple-element.32), channel_id=1, source_target_pairs={{0,1},{1,0},{2,3},{3,2},{4,5},{5,4},{6,7},{7,6},{8,9},{9,8},{10,11... | collective-permute-start | bytes 393224 | tf_op jit(solution)/shard_map/ppermute | solution.py:230
  19.5 6.2 %collective-permute-start.6 = (f32[2,64,256]{2,1,0:T(8,128)S(1)}, f32[2,64,256]{2,1,0:T(8,128)S(1)}, u32[]{:S(2)}, u32[]{:S(2)}) collective-permute-start(f32[2,64,256]{2,1,0:T(8,128)S(1)} %extend.1), channel_id=1, source_target_pairs={{1,2},{5,6},{9,10},{13,14},{17,18},{21,22},{25,26},{29,30}} | collective-permute-start | bytes 393224 | tf_op jit(solution)/shard_map/ppermute | solution.py:230
  22.4 6.6 %collective-permute-start.10 = (f32[2,64,256]{2,1,0:T(8,128)S(1)}, f32[2,64,256]{2,1,0:T(8,128)S(1)}, u32[]{:S(2)}, u32[]{:S(2)}) collective-permute-start(f32[2,64,256]{2,1,0:T(8,128)S(1)} %extend_other.1), channel_id=1, source_target_pairs={{1,3},{5,7},{9,11},{13,15},{17,19},{21,23},{25,27},{29,31}} | collective-permute-start | bytes 393224 | tf_op jit(solution)/shard_map/ppermute | solution.py:230
  23.7 7.9 %collective-permute-start.8 = (f32[2,64,256]{2,1,0:T(8,128)S(1)}, f32[2,64,256]{2,1,0:T(8,128)S(1)}, u32[]{:S(2)}, u32[]{:S(2)}) collective-permute-start(f32[2,64,256]{2,1,0:T(8,128)S(1)} %collective-permute-done.3.piece.near.one), channel_id=1, source_target_pairs={{0,4},{1,5},{2,6},{3,7},{4,0},{5,1},{6,2},{7,3},{8,12},{9,13},{10,... | collective-permute-start | bytes 393224 | tf_op jit(solution)/shard_map/ppermute | solution.py:230
  24.9 6.6 %collective-permute-start.9 = (f32[2,64,256]{2,1,0:T(8,128)S(1)}, f32[2,64,256]{2,1,0:T(8,128)S(1)}, u32[]{:S(2)}, u32[]{:S(2)}) collective-permute-start(f32[2,64,256]{2,1,0:T(8,128)S(1)} %collective-permute-done.4.piece.across.one), channel_id=1, source_target_pairs={{0,4},{1,5},{2,6},{3,7},{4,0},{5,1},{6,2},{7,3},{8,12},{9,13},{10,... | collective-permute-start | bytes 393224 | tf_op jit(solution)/shard_map/ppermute | solution.py:230
  25.0 7.6 %collective-permute-start.5 = (f32[2,64,256]{2,1,0:T(8,128)S(1)}, f32[2,64,256]{2,1,0:T(8,128)S(1)}, u32[]{:S(2)}, u32[]{:S(2)}) collective-permute-start(f32[2,64,256]{2,1,0:T(8,128)S(1)} %extend_other.1), channel_id=1, source_target_pairs={{1,2},{5,6},{9,10},{13,14},{17,18},{21,22},{25,26},{29,30}} | collective-permute-start | bytes 393224 | tf_op jit(solution)/shard_map/ppermute | solution.py:230
  25.7 7.8 %collective-permute-start.7 = (f32[2,64,256]{2,1,0:T(8,128)S(1)}, f32[2,64,256]{2,1,0:T(8,128)S(1)}, u32[]{:S(2)}, u32[]{:S(2)}) collective-permute-start(f32[2,64,256]{2,1,0:T(8,128)S(1)} %collective-permute-done.6.two), channel_id=1, source_target_pairs={{2,3},{6,7},{10,11},{14,15},{18,19},{22,23},{26,27},{30,31}} | collective-permute-start | bytes 393224 | tf_op jit(solution)/shard_map/ppermute | solution.py:230
  29.0 5.9 %collective-permute-start.11 = (f32[2,64,256]{2,1,0:T(8,128)S(1)}, f32[2,64,256]{2,1,0:T(8,128)S(1)}, u32[]{:S(2)}, u32[]{:S(2)}) collective-permute-start(f32[2,64,256]{2,1,0:T(8,128)S(1)} %merge_early.1.early), channel_id=1, source_target_pairs={{0,4},{1,5},{2,6},{3,7},{4,0},{5,1},{6,2},{7,3},{8,12},{9,13},{10,... | collective-permute-start | bytes 393224 | tf_op jit(solution)/shard_map/ppermute | solution.py:230
  33.5 1.7 %collective-permute-start.12 = (f32[2,64,256]{2,1,0:T(8,128)S(1)}, f32[2,64,256]{2,1,0:T(8,128)S(1)}, u32[]{:S(2)}, u32[]{:S(2)}) collective-permute-start(f32[2,64,256]{2,1,0:T(8,128)S(1)} %merge_late.1.late), channel_id=1, source_target_pairs={{0,4},{1,5},{2,6},{3,7},{4,0},{5,1},{6,2},{7,3},{8,12},{9,13},{10,... | collective-permute-start | bytes 393224 | tf_op jit(solution)/shard_map/ppermute | solution.py:230

commit v5 on v4

--- a/solution.py
+++ b/solution.py
@@ -118,8 +118,12 @@
         put(window, product(*ordered(x, k, chip, near, far)))
 
 
-def extend_kernel(piece, window, out):
+def extend_kernel(piece, window, own, out):
     _, _, w = place()
+
+    @pl.when(w == 2)
+    def _():
+        out[...] = own[...]
 
     @pl.when(w == 1)
     def _():
@@ -238,7 +242,9 @@
     chips = [((t, v), (t ^ 2, v)) for t, v in spots]
     twins = [((t, v), (t, v ^ 1)) for t, v in spots]
     one_two = [((t, 1), (t, 2)) for t in range(4)]
+    zero_one = [((t, 0), (t, 1)) for t in range(4)]
     two_three = [((t, 2), (t, 3)) for t in range(4)]
+    onward = [((t, v), (t, (v + 1) % 4)) for t, v in spots]
     one_three = [((t, 1), (t, 3)) for t in range(4)]
     tie = lax.optimization_barrier
 
@@ -251,29 +257,30 @@
         strips_kernel, [strip, strip], chip, near_chip, far_chip, name="strips", scratch=[pltpu.VMEM(full, F32)]
     )
     one = permute(own, twins)
-    (before,) = call(
-        before_kernel, [(2, *full)], unitaries, block, turned_other, near_chip, far_chip, name="before"
-    )
     (window,) = call(window_kernel, [full], chip, near_chip, far_chip, name="window")
-    other, before, window = tie((other, before, window))
-    one_other = permute(other, twins)
-    one, before = tie((one, before))
-    (both,) = call(extend_kernel, [strip], one, window, name="extend")
-    two = permute(both, one_two)
-    (both_other,) = call(extend_kernel, [strip], one_other, window, name="extend_other")
+    other, window = tie((other, window))
+    one_other = permute(other, zero_one)
+    (both,) = call(extend_kernel, [strip], one, window, other, name="extend")
+    two = permute(both, onward)
+    (both_other,) = call(extend_kernel, [strip], one_other, window, other, name="extend_other")
     three_other = permute(both_other, one_three)
     three = permute(two, two_three)
     two_other = permute(both_other, one_two)
-
+    own, _ = tie((one, two))
+    strips = own, two, permute(own, cores), permute(two, cores)
+    far_chip, _ = tie((far_chip, two))
+    (before,) = call(
+        before_kernel, [(2, *full)], unitaries, block, turned_other, near_chip, far_chip, name="before"
+    )
+    three_other, before = tie((three_other, before))
     (early,) = call(merge_kernel, [strip], one, two, three_other, name="merge_early")
     far_early = permute(early, cores)
-    one, one_other, _ = tie((one, one_other, both_other))
     parts = [jax.ShapeDtypeStruct((2, *full), jnp.bfloat16)] * 2
-    high, low = call(
-        left_kernel, parts, before, one, one_other, permute(one, cores), permute(one_other, cores), name="left"
-    )
-    two_other, three, high, early = tie((two_other, three, high, early))
-    (late,) = call(merge_kernel, [strip], one_other, two_other, three, name="merge_late")
+    high, low = call(left_kernel, parts, before, *strips, name="left")
+    two_other, early = tie((two_other, early))
+    (other,) = call(merge_kernel, [strip], one_other, two_other, two_other, name="merge_other")
+    three, other, high = tie((three, other, high))
+    (late,) = call(merge_kernel, [strip], other, other, three, name="merge_late")
     far_late = permute(late, cores)
     half_width = (2, 2, width, width // 2)
     (near,) = call(near_kernel, [half_width], high, low, early, late, name="near")

time: 37 us -> 36.2 us (0.978)
  waiting for transfers between devices: 15.6 us -> 14.5 us
  starting transfers between devices: 13.1 us -> 14 us
  local copies, waits for them, and re-layouts: 1.75 us -> 1.23 us
    ppermute x13, waiting for transfers between devices: 15.6 us -> 14.5 us  [permute(): return lax.ppermute(value, AXES, flat)]
    ppermute x13, starting transfers between devices: 13.1 us -> 14 us  [permute(): return lax.ppermute(value, AXES, flat)]
    unnamed x4, local copies, waits for them, and re-layouts: 1.75 us -> 1.23 us
    pallas_call x12 -> x13, Pallas kernels: 6.08 us -> 6.11 us  [call(): pl.pallas_call(body, out_shape=shapes, in_specs=[far if i == alias else w...]
  transfers between devices with their start and end apart: 13 -> 13, of which waited for: 8 -> 7; matrix products, arithmetic and copies ran while one was open for 0% -> 0% of each run, Pallas kernels for 9% -> 9%
where the time goes in v5:
time: 36.2 us; the launch traced here: 36 us
  waiting for transfers between devices  14.5 us (40%)
  starting transfers between devices  14 us (39%)
  Pallas kernels  6.11 us (17%)
  local copies, waits for them, and re-layouts  1.23 us (3%)
    ppermute x13, waiting for transfers between devices, permute(): return lax.ppermute(value, AXES, flat)  14.5 us
    ppermute x13, starting transfers between devices, permute(): return lax.ppermute(value, AXES, flat)  14 us
    pallas_call x13, Pallas kernels, call(): pl.pallas_call(body, out_shape=shapes, in_specs=[far if i == alias else w...  6.11 us
    unnamed x4, local copies, waits for them, and re-layouts  1.23 us
  transfers between devices with their start and end apart: 13, of which 7 were waited for; matrix products, arithmetic and copies ran while one was open for 0% of the time, Pallas kernels for 9%

profile of v5, /device:TPU:29, one launch (start us, length us, event | category | flops | bytes accessed | tf_op | source)
XLA Modules:
  0.0 36.0 jit_solution(9810338399216270146)
XLA Ops:
  0.0 0.0 copy-start
  0.0 1.2 %copy-done = f32[1,1,2,2,256,256]{5,4,3,2,1,0:T(8,128)S(1)} copy-done((f32[1,1,2,2,256,256]{5,4,3,2,1,0:T(8,128)S(1)}, f32[1,1,2,2,256,256]{5,4,3,2,1,0:T(8,128)}, u32[]{:S(2)}) %copy-start) | copy-done | bytes 1048600
  1.2 0.7 %block.1 = (f32[2,256,256]{2,1,0:T(8,128)S(1)}, f32[2,256,256]{2,1,0:T(8,128)S(1)}) custom-call(f32[1,1,2,2,256,256]{5,4,3,2,1,0:T(8,128)S(1)} %copy-done), custom_call_target="tpu_custom_call" | custom-call | tf_op jit(solution)/shard_map/block/pallas_call | solution.py:60
  1.9 0.7 %collective-permute-start = (f32[2,256,256]{2,1,0:T(8,128)S(1)}, f32[2,256,256]{2,1,0:T(8,128)S(1)}, u32[]{:S(2)}, u32[]{:S(2)}) collective-permute-start(f32[2,256,256]{2,1,0:T(8,128)S(1)} %get-tuple-element.24.mine), channel_id=1, source_target_pairs={{0,4},{1,5},{2,6},{3,7},{4,0},{5,1},{6,2},{7,3},{8,12},{9,13},{10,... | collective-permute-start | bytes 1572872 | tf_op jit(solution)/shard_map/ppermute | solution.py:234
  2.7 1.5 %collective-permute-done.theirs.turned = f32[2,256,256]{2,1,0:T(8,128)S(1)} collective-permute-done((f32[2,256,256]{2,1,0:T(8,128)S(1)}, f32[2,256,256]{2,1,0:T(8,128)S(1)}, u32[]{:S(2)}, u32[]{:S(2)}) %collective-permute-start) | collective-permute-done | bytes 524320 | tf_op jit(solution)/shard_map/ppermute | solution.py:234
  4.2 0.6 %chip.1 = (f32[2,256,256]{2,1,0:T(8,128)S(1)}, f32[256,256]{1,0:T(8,128)S(1)}) custom-call(f32[2,256,256]{2,1,0:T(8,128)S(1)} %get-tuple-element.24.mine, f32[2,256,256]{2,1,0:T(8,128)S(1)} %collective-permute-done.theirs.turned), custom_call_target="tpu_custom_call" | custom-call | tf_op jit(solution)/shard_map/chip/pallas_call | solution.py:60
  4.8 1.3 %collective-permute-start.1 = (f32[256,256]{1,0:T(8,128)S(1)}, f32[256,256]{1,0:T(8,128)S(1)}, u32[]{:S(2)}, u32[]{:S(2)}) collective-permute-start(f32[256,256]{1,0:T(8,128)S(1)} %get-tuple-element.26), channel_id=1, source_target_pairs={{0,8},{1,9},{2,10},{3,11},{4,12},{5,13},{6,14},{7,15},{8,0},{9,1},... | collective-permute-start | bytes 786440 | tf_op jit(solution)/shard_map/ppermute | solution.py:234
  6.1 6.3 %collective-permute-done.1.near = f32[256,256]{1,0:T(8,128)S(1)} collective-permute-done((f32[256,256]{1,0:T(8,128)S(1)}, f32[256,256]{1,0:T(8,128)S(1)}, u32[]{:S(2)}, u32[]{:S(2)}) %collective-permute-start.1) | collective-permute-done | bytes 262176 | tf_op jit(solution)/shard_map/ppermute | solution.py:234
  12.4 1.2 %collective-permute-start.2 = (f32[256,256]{1,0:T(8,128)S(1)}, f32[256,256]{1,0:T(8,128)S(1)}, u32[]{:S(2)}, u32[]{:S(2)}) collective-permute-start(f32[256,256]{1,0:T(8,128)S(1)} %collective-permute-done.1.near), channel_id=1, source_target_pairs={{0,4},{1,5},{2,6},{3,7},{4,0},{5,1},{6,2},{7,3},{8,12},{9,13},{10,... | collective-permute-start | bytes 786440 | tf_op jit(solution)/shard_map/ppermute | solution.py:234
  13.6 1.2 %collective-permute-done.2.far = f32[256,256]{1,0:T(8,128)S(1)} collective-permute-done((f32[256,256]{1,0:T(8,128)S(1)}, f32[256,256]{1,0:T(8,128)S(1)}, u32[]{:S(2)}, u32[]{:S(2)}) %collective-permute-start.2) | collective-permute-done | bytes 262176 | tf_op jit(solution)/shard_map/ppermute | solution.py:234
  14.8 0.7 %collective-permute-start.5 = (f32[2,64,256]{2,1,0:T(8,128)S(1)}, f32[2,64,256]{2,1,0:T(8,128)S(1)}, u32[]{:S(2)}, u32[]{:S(2)}) collective-permute-start(f32[2,64,256]{2,1,0:T(8,128)S(1)} %get-tuple-element.31), channel_id=1, source_target_pairs={{0,1},{1,0},{2,3},{3,2},{4,5},{5,4},{6,7},{7,6},{8,9},{9,8},{10,11... | collective-permute-start | bytes 393224 | tf_op jit(solution)/shard_map/ppermute | solution.py:234
  15.5 0.0 copy-start.1
  15.5 0.8 %collective-permute-start.3 = (f32[2,64,256]{2,1,0:T(8,128)S(1)}, f32[2,64,256]{2,1,0:T(8,128)S(1)}, u32[]{:S(2)}, u32[]{:S(2)}) collective-permute-start(f32[2,64,256]{2,1,0:T(8,128)S(1)} %get-tuple-element.28.own), channel_id=1, source_target_pairs={{0,1},{4,5},{8,9},{12,13},{16,17},{20,21},{24,25},{28,29}} | collective-permute-start | bytes 393224 | tf_op jit(solution)/shard_map/ppermute | solution.py:234
  16.3 3.2 %collective-permute-done.5.piece.one.near = f32[2,64,256]{2,1,0:T(8,128)S(1)} collective-permute-done((f32[2,64,256]{2,1,0:T(8,128)S(1)}, f32[2,64,256]{2,1,0:T(8,128)S(1)}, u32[]{:S(2)}, u32[]{:S(2)}) %collective-permute-start.5) | collective-permute-done | bytes 131104 | tf_op jit(solution)/shard_map/ppermute | solution.py:234
  19.5 0.5 %collective-permute-start.6 = (f32[2,64,256]{2,1,0:T(8,128)S(1)}, f32[2,64,256]{2,1,0:T(8,128)S(1)}, u32[]{:S(2)}, u32[]{:S(2)}) collective-permute-start(f32[2,64,256]{2,1,0:T(8,128)S(1)} %extend.1), channel_id=1, source_target_pairs={{0,1},{1,2},{2,3},{3,0},{4,5},{5,6},{6,7},{7,4},{8,9},{9,10},{10,1... | collective-permute-start | bytes 393224 | tf_op jit(solution)/shard_map/ppermute | solution.py:234
  20.0 0.0 collective-permute-done.3.piece.one
  20.0 1.3 %collective-permute-start.4 = (f32[2,64,256]{2,1,0:T(8,128)S(1)}, f32[2,64,256]{2,1,0:T(8,128)S(1)}, u32[]{:S(2)}, u32[]{:S(2)}) collective-permute-start(f32[2,64,256]{2,1,0:T(8,128)S(1)} %extend_other.1), channel_id=1, source_target_pairs={{1,3},{5,7},{9,11},{13,15},{17,19},{21,23},{25,27},{29,31}} | collective-permute-start | bytes 393224 | tf_op jit(solution)/shard_map/ppermute | solution.py:234
  21.3 0.7 %collective-permute-start.8 = (f32[2,64,256]{2,1,0:T(8,128)S(1)}, f32[2,64,256]{2,1,0:T(8,128)S(1)}, u32[]{:S(2)}, u32[]{:S(2)}) collective-permute-start(f32[2,64,256]{2,1,0:T(8,128)S(1)} %extend_other.1), channel_id=1, source_target_pairs={{1,2},{5,6},{9,10},{13,14},{17,18},{21,22},{25,26},{29,30}} | collective-permute-start | bytes 393224 | tf_op jit(solution)/shard_map/ppermute | solution.py:234
  21.9 1.4 %collective-permute-done.6.two.across = f32[2,64,256]{2,1,0:T(8,128)S(1)} collective-permute-done((f32[2,64,256]{2,1,0:T(8,128)S(1)}, f32[2,64,256]{2,1,0:T(8,128)S(1)}, u32[]{:S(2)}, u32[]{:S(2)}) %collective-permute-start.6) | collective-permute-done | bytes 131104 | tf_op jit(solution)/shard_map/ppermute | solution.py:234
  23.3 2.4 %collective-permute-start.9 = (f32[2,64,256]{2,1,0:T(8,128)S(1)}, f32[2,64,256]{2,1,0:T(8,128)S(1)}, u32[]{:S(2)}, u32[]{:S(2)}) collective-permute-start(f32[2,64,256]{2,1,0:T(8,128)S(1)} %collective-permute-done.5.piece.one.near), channel_id=1, source_target_pairs={{0,4},{1,5},{2,6},{3,7},{4,0},{5,1},{6,2},{7,3},{8,12},{9,13},{10,... | collective-permute-start | bytes 393224 | tf_op jit(solution)/shard_map/ppermute | solution.py:234
  25.7 0.0 collective-permute-start.10
  25.7 1.3 %collective-permute-start.7 = (f32[2,64,256]{2,1,0:T(8,128)S(1)}, f32[2,64,256]{2,1,0:T(8,128)S(1)}, u32[]{:S(2)}, u32[]{:S(2)}) collective-permute-start(f32[2,64,256]{2,1,0:T(8,128)S(1)} %collective-permute-done.6.two.across), channel_id=1, source_target_pairs={{2,3},{6,7},{10,11},{14,15},{18,19},{22,23},{26,27},{30,31}} | collective-permute-start | bytes 393224 | tf_op jit(solution)/shard_map/ppermute | solution.py:234
  27.0 0.0 copy-done.1
  27.0 1.6 %before.1 = f32[2,2,256,256]{3,2,1,0:T(8,128)S(1)} custom-call(f32[1,1,2,2,256,256]{5,4,3,2,1,0:T(8,128)S(1)} %copy-done.1, f32[2,256,256]{2,1,0:T(8,128)S(1)} %get-tuple-element.30.block, f32[2,256,256]{2,1,0:T(8,128)S(1)} %collective-permute-done.theirs.turned, f32[256,256]{1,0:T(8,128)S(1)} %collective-permute-done.1.near, ...), custom_call_target="tpu_custom_call" | custom-call | tf_op jit(solution)/shard_map/before/pallas_call | solution.py:60
  28.6 0.0 collective-permute-done.4.three
  28.6 1.8 %collective-permute-start.11 = (f32[2,64,256]{2,1,0:T(8,128)S(1)}, f32[2,64,256]{2,1,0:T(8,128)S(1)}, u32[]{:S(2)}, u32[]{:S(2)}) collective-permute-start(f32[2,64,256]{2,1,0:T(8,128)S(1)} %merge_early.1.early), channel_id=1, source_target_pairs={{0,4},{1,5},{2,6},{3,7},{4,0},{5,1},{6,2},{7,3},{8,12},{9,13},{10,... | collective-permute-start | bytes 393224 | tf_op jit(solution)/shard_map/ppermute | solution.py:234
  30.5 0.0 collective-permute-done.8.two.three
  30.5 0.0 collective-permute-done.9.far
  30.5 0.0 collective-permute-done.10.far_across
  30.5 1.1 %left.1 = (bf16[2,2,256,256]{3,2,1,0:T(8,128)(2,1)S(1)}, bf16[2,2,256,256]{3,2,1,0:T(8,128)(2,1)S(1)}) custom-call(f32[2,2,256,256]{3,2,1,0:T(8,128)S(1)} %before.1, f32[2,64,256]{2,1,0:T(8,128)S(1)} %collective-permute-done.5.piece.one.near, f32[2,64,256]{2,1,0:T(8,128)S(1)} %collective-permute-done.6.two.across, ...), custom_call_target="tpu_custom_call" | custom-call | tf_op jit(solution)/shard_map/left/pallas_call | solution.py:60
  31.6 0.5 %collective-permute-done.7.three = f32[2,64,256]{2,1,0:T(8,128)S(1)} collective-permute-done((f32[2,64,256]{2,1,0:T(8,128)S(1)}, f32[2,64,256]{2,1,0:T(8,128)S(1)}, u32[]{:S(2)}, u32[]{:S(2)}) %collective-permute-start.7) | collective-permute-done | bytes 131104 | tf_op jit(solution)/shard_map/ppermute | solution.py:234
  32.1 1.4 %collective-permute-start.12 = (f32[2,64,256]{2,1,0:T(8,128)S(1)}, f32[2,64,256]{2,1,0:T(8,128)S(1)}, u32[]{:S(2)}, u32[]{:S(2)}) collective-permute-start(f32[2,64,256]{2,1,0:T(8,128)S(1)} %merge_late.1.late), channel_id=1, source_target_pairs={{0,4},{1,5},{2,6},{3,7},{4,0},{5,1},{6,2},{7,3},{8,12},{9,13},{10,... | collective-permute-start | bytes 393224 | tf_op jit(solution)/shard_map/ppermute | solution.py:234
  33.6 0.6 %near.1 = f32[2,2,256,128]{3,2,1,0:T(8,128)S(1)} custom-call(bf16[2,2,256,256]{3,2,1,0:T(8,128)(2,1)S(1)} %get-tuple-element.38.high, bf16[2,2,256,256]{3,2,1,0:T(8,128)(2,1)S(1)} %get-tuple-element.39.low, f32[2,64,256]{2,1,0:T(8,128)S(1)} %merge_early.1.early, f32[2,64,256]{2,1,0:T(8,128)S(1)} %merge_late.1.late), custom_call_target="tpu_custom_call" | custom-call | tf_op jit(solution)/shard_map/near/pallas_call | solution.py:60
  34.2 0.0 collective-permute-done.11.early
  34.2 0.4 %collective-permute-done.12.late = f32[2,64,256]{2,1,0:T(8,128)S(1)} collective-permute-done((f32[2,64,256]{2,1,0:T(8,128)S(1)}, f32[2,64,256]{2,1,0:T(8,128)S(1)}, u32[]{:S(2)}, u32[]{:S(2)}) %collective-permute-start.12) | collective-permute-done | bytes 131104 | tf_op jit(solution)/shard_map/ppermute | solution.py:234
  34.6 1.4 %far.1 = f32[1,1,2,2,256,256]{5,4,3,2,1,0:T(8,128)} custom-call(f32[2,2,256,256]{3,2,1,0:T(8,128)S(1)} %before.1, f32[2,2,256,128]{3,2,1,0:T(8,128)S(1)} %near.1, bf16[2,2,256,256]{3,2,1,0:T(8,128)(2,1)S(1)} %get-tuple-element.38.high, bf16[2,2,256,256]{3,2,1,0:T(8,128)(2,1)S(1)} %get-tuple-element.39.low, f32[2,64,256]{2,1,0:T(8,128)S(1)} %collective-permute-done.11.early, ...), custom_call_target="tpu_custom_call" | custom-call | tf_op jit(solution)/shard_map/far/pallas_call | solution.py:60
  (7 shorter events, 0.1 us)
Async XLA Ops:
  0.0 1.2 %copy-start = (f32[1,1,2,2,256,256]{5,4,3,2,1,0:T(8,128)S(1)}, f32[1,1,2,2,256,256]{5,4,3,2,1,0:T(8,128)}, u32[]{:S(2)}) copy-start(f32[1,1,2,2,256,256]{5,4,3,2,1,0:T(8,128)} %u.3) | copy-start | bytes 3145732
  1.9 2.3 %collective-permute-start = (f32[2,256,256]{2,1,0:T(8,128)S(1)}, f32[2,256,256]{2,1,0:T(8,128)S(1)}, u32[]{:S(2)}, u32[]{:S(2)}) collective-permute-start(f32[2,256,256]{2,1,0:T(8,128)S(1)} %get-tuple-element.24.mine), channel_id=1, source_target_pairs={{0,4},{1,5},{2,6},{3,7},{4,0},{5,1},{6,2},{7,3},{8,12},{9,13},{10,... | collective-permute-start | bytes 1572872 | tf_op jit(solution)/shard_map/ppermute | solution.py:234
  4.8 7.6 %collective-permute-start.1 = (f32[256,256]{1,0:T(8,128)S(1)}, f32[256,256]{1,0:T(8,128)S(1)}, u32[]{:S(2)}, u32[]{:S(2)}) collective-permute-start(f32[256,256]{1,0:T(8,128)S(1)} %get-tuple-element.26), channel_id=1, source_target_pairs={{0,8},{1,9},{2,10},{3,11},{4,12},{5,13},{6,14},{7,15},{8,0},{9,1},... | collective-permute-start | bytes 786440 | tf_op jit(solution)/shard_map/ppermute | solution.py:234
  12.4 2.4 %collective-permute-start.2 = (f32[256,256]{1,0:T(8,128)S(1)}, f32[256,256]{1,0:T(8,128)S(1)}, u32[]{:S(2)}, u32[]{:S(2)}) collective-permute-start(f32[256,256]{1,0:T(8,128)S(1)} %collective-permute-done.1.near), channel_id=1, source_target_pairs={{0,4},{1,5},{2,6},{3,7},{4,0},{5,1},{6,2},{7,3},{8,12},{9,13},{10,... | collective-permute-start | bytes 786440 | tf_op jit(solution)/shard_map/ppermute | solution.py:234
  14.8 4.7 %collective-permute-start.5 = (f32[2,64,256]{2,1,0:T(8,128)S(1)}, f32[2,64,256]{2,1,0:T(8,128)S(1)}, u32[]{:S(2)}, u32[]{:S(2)}) collective-permute-start(f32[2,64,256]{2,1,0:T(8,128)S(1)} %get-tuple-element.31), channel_id=1, source_target_pairs={{0,1},{1,0},{2,3},{3,2},{4,5},{5,4},{6,7},{7,6},{8,9},{9,8},{10,11... | collective-permute-start | bytes 393224 | tf_op jit(solution)/shard_map/ppermute | solution.py:234
  15.5 11.5 %copy-start.1 = (f32[1,1,2,2,256,256]{5,4,3,2,1,0:T(8,128)S(1)}, f32[1,1,2,2,256,256]{5,4,3,2,1,0:T(8,128)}, u32[]{:S(2)}) copy-start(f32[1,1,2,2,256,256]{5,4,3,2,1,0:T(8,128)} %u.3) | copy-start | bytes 3145732
  15.5 4.5 %collective-permute-start.3 = (f32[2,64,256]{2,1,0:T(8,128)S(1)}, f32[2,64,256]{2,1,0:T(8,128)S(1)}, u32[]{:S(2)}, u32[]{:S(2)}) collective-permute-start(f32[2,64,256]{2,1,0:T(8,128)S(1)} %get-tuple-element.28.own), channel_id=1, source_target_pairs={{0,1},{4,5},{8,9},{12,13},{16,17},{20,21},{24,25},{28,29}} | collective-permute-start | bytes 393224 | tf_op jit(solution)/shard_map/ppermute | solution.py:234
  19.5 3.8 %collective-permute-start.6 = (f32[2,64,256]{2,1,0:T(8,128)S(1)}, f32[2,64,256]{2,1,0:T(8,128)S(1)}, u32[]{:S(2)}, u32[]{:S(2)}) collective-permute-start(f32[2,64,256]{2,1,0:T(8,128)S(1)} %extend.1), channel_id=1, source_target_pairs={{0,1},{1,2},{2,3},{3,0},{4,5},{5,6},{6,7},{7,4},{8,9},{9,10},{10,1... | collective-permute-start | bytes 393224 | tf_op jit(solution)/shard_map/ppermute | solution.py:234
  20.0 8.6 %collective-permute-start.4 = (f32[2,64,256]{2,1,0:T(8,128)S(1)}, f32[2,64,256]{2,1,0:T(8,128)S(1)}, u32[]{:S(2)}, u32[]{:S(2)}) collective-permute-start(f32[2,64,256]{2,1,0:T(8,128)S(1)} %extend_other.1), channel_id=1, source_target_pairs={{1,3},{5,7},{9,11},{13,15},{17,19},{21,23},{25,27},{29,31}} | collective-permute-start | bytes 393224 | tf_op jit(solution)/shard_map/ppermute | solution.py:234
  21.3 9.2 %collective-permute-start.8 = (f32[2,64,256]{2,1,0:T(8,128)S(1)}, f32[2,64,256]{2,1,0:T(8,128)S(1)}, u32[]{:S(2)}, u32[]{:S(2)}) collective-permute-start(f32[2,64,256]{2,1,0:T(8,128)S(1)} %extend_other.1), channel_id=1, source_target_pairs={{1,2},{5,6},{9,10},{13,14},{17,18},{21,22},{25,26},{29,30}} | collective-permute-start | bytes 393224 | tf_op jit(solution)/shard_map/ppermute | solution.py:234
  23.3 7.2 %collective-permute-start.9 = (f32[2,64,256]{2,1,0:T(8,128)S(1)}, f32[2,64,256]{2,1,0:T(8,128)S(1)}, u32[]{:S(2)}, u32[]{:S(2)}) collective-permute-start(f32[2,64,256]{2,1,0:T(8,128)S(1)} %collective-permute-done.5.piece.one.near), channel_id=1, source_target_pairs={{0,4},{1,5},{2,6},{3,7},{4,0},{5,1},{6,2},{7,3},{8,12},{9,13},{10,... | collective-permute-start | bytes 393224 | tf_op jit(solution)/shard_map/ppermute | solution.py:234
  25.7 4.8 %collective-permute-start.10 = (f32[2,64,256]{2,1,0:T(8,128)S(1)}, f32[2,64,256]{2,1,0:T(8,128)S(1)}, u32[]{:S(2)}, u32[]{:S(2)}) collective-permute-start(f32[2,64,256]{2,1,0:T(8,128)S(1)} %collective-permute-done.6.two.across), channel_id=1, source_target_pairs={{0,4},{1,5},{2,6},{3,7},{4,0},{5,1},{6,2},{7,3},{8,12},{9,13},{10,... | collective-permute-start | bytes 393224 | tf_op jit(solution)/shard_map/ppermute | solution.py:234
  25.7 6.4 %collective-permute-start.7 = (f32[2,64,256]{2,1,0:T(8,128)S(1)}, f32[2,64,256]{2,1,0:T(8,128)S(1)}, u32[]{:S(2)}, u32[]{:S(2)}) collective-permute-start(f32[2,64,256]{2,1,0:T(8,128)S(1)} %collective-permute-done.6.two.across), channel_id=1, source_target_pairs={{2,3},{6,7},{10,11},{14,15},{18,19},{22,23},{26,27},{30,31}} | collective-permute-start | bytes 393224 | tf_op jit(solution)/shard_map/ppermute | solution.py:234
  28.6 5.6 %collective-permute-start.11 = (f32[2,64,256]{2,1,0:T(8,128)S(1)}, f32[2,64,256]{2,1,0:T(8,128)S(1)}, u32[]{:S(2)}, u32[]{:S(2)}) collective-permute-start(f32[2,64,256]{2,1,0:T(8,128)S(1)} %merge_early.1.early), channel_id=1, source_target_pairs={{0,4},{1,5},{2,6},{3,7},{4,0},{5,1},{6,2},{7,3},{8,12},{9,13},{10,... | collective-permute-start | bytes 393224 | tf_op jit(solution)/shard_map/ppermute | solution.py:234
  32.1 2.4 %collective-permute-start.12 = (f32[2,64,256]{2,1,0:T(8,128)S(1)}, f32[2,64,256]{2,1,0:T(8,128)S(1)}, u32[]{:S(2)}, u32[]{:S(2)}) collective-permute-start(f32[2,64,256]{2,1,0:T(8,128)S(1)} %merge_late.1.late), channel_id=1, source_target_pairs={{0,4},{1,5},{2,6},{3,7},{4,0},{5,1},{6,2},{7,3},{8,12},{9,13},{10,... | collective-permute-start | bytes 393224 | tf_op jit(solution)/shard_map/ppermute | solution.py:234

commit v6 on v5

--- a/solution.py
+++ b/solution.py
@@ -154,23 +154,30 @@
     put(out.at[1], product(pair(block), before, NT))
 
 
-def left_kernel(before, near, across, far, far_across, high, low):
-    _, _, w = place()
-
-    def store(slot, value):
-        for plane in range(2):
-            high[slot, plane], low[slot, plane] = halves(value[plane])
+def left_kernel(before, near, across, high, low, *, mine):
+    x, k, w = place()
+    width = high.shape[-1]
 
     @pl.when(w == 3)
     def _():
-        window = whole(near, across, far, far_across)
-        for slot in range(2):
-            store(slot, product(pair(before[slot]), window, NT))
+        strips = half(x, near, across)
+        for slot in range(2):
+            value = columns_of(*parts_of(before, slot), 0, halves(jnp.concatenate(strips, axis=0)))
+            for plane in range(2):
+                high[slot, plane], low[slot, plane] = halves(value[plane])
 
     @pl.when((w == 1) | (w == 2))
     def _():
-        for slot in range(2):
-            store(slot, pair(before[slot]))
+        core = k if mine else 1 - k
+        for slot in range(2):
+            for plane in range(2):
+                value = before[slot, plane, :, pl.ds(pl.multiple_of(core * width, width), width)]
+                high[slot, plane], low[slot, plane] = halves(value)
+
+
+def parts_of(ref, slot):
+    planes = [halves(ref[slot, plane]) for plane in range(2)]
+    return tuple({(0, plane): planes[plane][part] for plane in range(2)} for part in range(2))
 
 
 def merge_kernel(one, two, three, out):
@@ -189,14 +196,26 @@
     return real[:, :width] - imag[:, width:], real[:, width:] + imag[:, :width]
 
 
-def near_kernel(high, low, early, late, out):
-    x, _, w = place()
+def joined(k, mine, theirs):
+    def plane(slot, index):
+        a, b = mine[slot, index], theirs[slot, index]
+        return jnp.concatenate([jnp.where(k == 0, a, b), jnp.where(k == 0, b, a)], axis=1)
+
+    return {(slot, index): plane(slot, index) for slot in range(2) for index in range(2)}
+
+
+def near_kernel(high, low, far_high, far_low, early, late, out, whole_high, whole_low):
+    x, k, w = place()
 
     @pl.when(w != 0)
     def _():
+        both_high, both_low = joined(k, high, far_high), joined(k, low, far_low)
+        for slot in range(2):
+            for plane in range(2):
+                whole_high[slot, plane], whole_low[slot, plane] = both_high[slot, plane], both_low[slot, plane]
         offset = halves(jnp.concatenate(half(jnp.where(w == 3, 1 - x, x), early, late), axis=0))
         for slot in range(2):
-            put(out.at[slot], columns_of(high, low, slot, offset))
+            put(out.at[slot], columns_of(both_high, both_low, slot, offset))
 
 
 def far_kernel(before, near, high, low, early, late, out, far, sems):
@@ -266,24 +285,26 @@
     three_other = permute(both_other, one_three)
     three = permute(two, two_three)
     two_other = permute(both_other, one_two)
-    own, _ = tie((one, two))
-    strips = own, two, permute(own, cores), permute(two, cores)
+    own, past = tie((one, two))
+    far_own, far_past = permute(own, cores), permute(past, cores)
     far_chip, _ = tie((far_chip, two))
     (before,) = call(
         before_kernel, [(2, *full)], unitaries, block, turned_other, near_chip, far_chip, name="before"
     )
     three_other, before = tie((three_other, before))
+    parts = [jax.ShapeDtypeStruct((2, 2, width, width // 2), jnp.bfloat16)] * 2
+    high, low = call(functools.partial(left_kernel, mine=True), parts, before, own, past, name="left_near")
+    three_other, high = tie((three_other, high))
     (early,) = call(merge_kernel, [strip], one, two, three_other, name="merge_early")
     far_early = permute(early, cores)
-    parts = [jax.ShapeDtypeStruct((2, *full), jnp.bfloat16)] * 2
-    high, low = call(left_kernel, parts, before, *strips, name="left")
     two_other, early = tie((two_other, early))
     (other,) = call(merge_kernel, [strip], one_other, two_other, two_other, name="merge_other")
-    three, other, high = tie((three, other, high))
+    three, other = tie((three, other))
     (late,) = call(merge_kernel, [strip], other, other, three, name="merge_late")
     far_late = permute(late, cores)
-    half_width = (2, 2, width, width // 2)
-    (near,) = call(near_kernel, [half_width], high, low, early, late, name="near")
+    theirs = call(functools.partial(left_kernel, mine=False), parts, before, far_own, far_past, name="left_far")
+    half_width, both = (2, 2, width, width // 2), jax.ShapeDtypeStruct((2, *full), jnp.bfloat16)
+    near, high, low = call(near_kernel, [half_width, both, both], high, low, *theirs, early, late, name="near")
     scratch = pltpu.VMEM(half_width, F32), pltpu.SemaphoreType.DMA((2, 2))
     operands = before, near, high, low, far_early, far_late
     (out,) = call(far_kernel, [unitaries.shape], *operands, name="far", scratch=scratch, hbm_out=True)

time: 36.2 us -> 35.6 us (0.983)
  starting transfers between devices: 14 us -> 13.4 us
    ppermute x13, starting transfers between devices: 14 us -> 13.4 us  [permute(): return lax.ppermute(value, AXES, flat)]
    pallas_call x13 -> x14, Pallas kernels: 6.11 us -> 6.31 us  [call(): pl.pallas_call(body, out_shape=shapes, in_specs=[far if i == alias else w...]
  transfers between devices with their start and end apart: 13 -> 13, of which waited for: 7 -> 6; matrix products, arithmetic and copies ran while one was open for 0% -> 0% of each run, Pallas kernels for 9% -> 10%
where the time goes in v6:
time: 35.6 us; the launch traced here: 35.4 us
  waiting for transfers between devices  14.3 us (40%)
  starting transfers between devices  13.4 us (38%)
  Pallas kernels  6.31 us (18%)
  local copies, waits for them, and re-layouts  1.23 us (3%)
    ppermute x13, waiting for transfers between devices, permute(): return lax.ppermute(value, AXES, flat)  14.3 us
    ppermute x13, starting transfers between devices, permute(): return lax.ppermute(value, AXES, flat)  13.4 us
    pallas_call x14, Pallas kernels, call(): pl.pallas_call(body, out_shape=shapes, in_specs=[far if i == alias else w...  6.31 us
    unnamed x4, local copies, waits for them, and re-layouts  1.23 us
  transfers between devices with their start and end apart: 13, of which 6 were waited for; matrix products, arithmetic and copies ran while one was open for 0% of the time, Pallas kernels for 10%

profile of v6, /device:TPU:29, one launch (start us, length us, event | category | flops | bytes accessed | tf_op | source)
XLA Modules:
  0.0 35.4 jit_solution(15488834663651593623)
XLA Ops:
  0.0 0.0 copy-start
  0.0 1.2 %copy-done = f32[1,1,2,2,256,256]{5,4,3,2,1,0:T(8,128)S(1)} copy-done((f32[1,1,2,2,256,256]{5,4,3,2,1,0:T(8,128)S(1)}, f32[1,1,2,2,256,256]{5,4,3,2,1,0:T(8,128)}, u32[]{:S(2)}) %copy-start) | copy-done | bytes 1048600
  1.2 0.7 %block.1 = (f32[2,256,256]{2,1,0:T(8,128)S(1)}, f32[2,256,256]{2,1,0:T(8,128)S(1)}) custom-call(f32[1,1,2,2,256,256]{5,4,3,2,1,0:T(8,128)S(1)} %copy-done), custom_call_target="tpu_custom_call" | custom-call | tf_op jit(solution)/shard_map/block/pallas_call | solution.py:60
  1.9 0.7 %collective-permute-start = (f32[2,256,256]{2,1,0:T(8,128)S(1)}, f32[2,256,256]{2,1,0:T(8,128)S(1)}, u32[]{:S(2)}, u32[]{:S(2)}) collective-permute-start(f32[2,256,256]{2,1,0:T(8,128)S(1)} %get-tuple-element.31.mine), channel_id=1, source_target_pairs={{0,4},{1,5},{2,6},{3,7},{4,0},{5,1},{6,2},{7,3},{8,12},{9,13},{10,... | collective-permute-start | bytes 1572872 | tf_op jit(solution)/shard_map/ppermute | solution.py:253
  2.7 1.5 %collective-permute-done.theirs.turned = f32[2,256,256]{2,1,0:T(8,128)S(1)} collective-permute-done((f32[2,256,256]{2,1,0:T(8,128)S(1)}, f32[2,256,256]{2,1,0:T(8,128)S(1)}, u32[]{:S(2)}, u32[]{:S(2)}) %collective-permute-start) | collective-permute-done | bytes 524320 | tf_op jit(solution)/shard_map/ppermute | solution.py:253
  4.2 0.6 %chip.1 = (f32[2,256,256]{2,1,0:T(8,128)S(1)}, f32[256,256]{1,0:T(8,128)S(1)}) custom-call(f32[2,256,256]{2,1,0:T(8,128)S(1)} %get-tuple-element.31.mine, f32[2,256,256]{2,1,0:T(8,128)S(1)} %collective-permute-done.theirs.turned), custom_call_target="tpu_custom_call" | custom-call | tf_op jit(solution)/shard_map/chip/pallas_call | solution.py:60
  4.8 1.3 %collective-permute-start.1 = (f32[256,256]{1,0:T(8,128)S(1)}, f32[256,256]{1,0:T(8,128)S(1)}, u32[]{:S(2)}, u32[]{:S(2)}) collective-permute-start(f32[256,256]{1,0:T(8,128)S(1)} %get-tuple-element.33), channel_id=1, source_target_pairs={{0,8},{1,9},{2,10},{3,11},{4,12},{5,13},{6,14},{7,15},{8,0},{9,1},... | collective-permute-start | bytes 786440 | tf_op jit(solution)/shard_map/ppermute | solution.py:253
  6.1 6.3 %collective-permute-done.1.near = f32[256,256]{1,0:T(8,128)S(1)} collective-permute-done((f32[256,256]{1,0:T(8,128)S(1)}, f32[256,256]{1,0:T(8,128)S(1)}, u32[]{:S(2)}, u32[]{:S(2)}) %collective-permute-start.1) | collective-permute-done | bytes 262176 | tf_op jit(solution)/shard_map/ppermute | solution.py:253
  12.4 1.2 %collective-permute-start.2 = (f32[256,256]{1,0:T(8,128)S(1)}, f32[256,256]{1,0:T(8,128)S(1)}, u32[]{:S(2)}, u32[]{:S(2)}) collective-permute-start(f32[256,256]{1,0:T(8,128)S(1)} %collective-permute-done.1.near), channel_id=1, source_target_pairs={{0,4},{1,5},{2,6},{3,7},{4,0},{5,1},{6,2},{7,3},{8,12},{9,13},{10,... | collective-permute-start | bytes 786440 | tf_op jit(solution)/shard_map/ppermute | solution.py:253
  13.6 1.2 %collective-permute-done.2.far = f32[256,256]{1,0:T(8,128)S(1)} collective-permute-done((f32[256,256]{1,0:T(8,128)S(1)}, f32[256,256]{1,0:T(8,128)S(1)}, u32[]{:S(2)}, u32[]{:S(2)}) %collective-permute-start.2) | collective-permute-done | bytes 262176 | tf_op jit(solution)/shard_map/ppermute | solution.py:253
  14.8 0.7 %collective-permute-start.5 = (f32[2,64,256]{2,1,0:T(8,128)S(1)}, f32[2,64,256]{2,1,0:T(8,128)S(1)}, u32[]{:S(2)}, u32[]{:S(2)}) collective-permute-start(f32[2,64,256]{2,1,0:T(8,128)S(1)} %get-tuple-element.38), channel_id=1, source_target_pairs={{0,1},{1,0},{2,3},{3,2},{4,5},{5,4},{6,7},{7,6},{8,9},{9,8},{10,11... | collective-permute-start | bytes 393224 | tf_op jit(solution)/shard_map/ppermute | solution.py:253
  15.5 0.0 copy-start.1
  15.5 0.8 %collective-permute-start.3 = (f32[2,64,256]{2,1,0:T(8,128)S(1)}, f32[2,64,256]{2,1,0:T(8,128)S(1)}, u32[]{:S(2)}, u32[]{:S(2)}) collective-permute-start(f32[2,64,256]{2,1,0:T(8,128)S(1)} %get-tuple-element.35.own), channel_id=1, source_target_pairs={{0,1},{4,5},{8,9},{12,13},{16,17},{20,21},{24,25},{28,29}} | collective-permute-start | bytes 393224 | tf_op jit(solution)/shard_map/ppermute | solution.py:253
  16.3 3.2 %collective-permute-done.5.piece.near.one = f32[2,64,256]{2,1,0:T(8,128)S(1)} collective-permute-done((f32[2,64,256]{2,1,0:T(8,128)S(1)}, f32[2,64,256]{2,1,0:T(8,128)S(1)}, u32[]{:S(2)}, u32[]{:S(2)}) %collective-permute-start.5) | collective-permute-done | bytes 131104 | tf_op jit(solution)/shard_map/ppermute | solution.py:253
  19.5 0.5 %collective-permute-start.6 = (f32[2,64,256]{2,1,0:T(8,128)S(1)}, f32[2,64,256]{2,1,0:T(8,128)S(1)}, u32[]{:S(2)}, u32[]{:S(2)}) collective-permute-start(f32[2,64,256]{2,1,0:T(8,128)S(1)} %extend.1), channel_id=1, source_target_pairs={{0,1},{1,2},{2,3},{3,0},{4,5},{5,6},{6,7},{7,4},{8,9},{9,10},{10,1... | collective-permute-start | bytes 393224 | tf_op jit(solution)/shard_map/ppermute | solution.py:253
  20.0 0.0 collective-permute-done.3.piece.one
  20.0 1.3 %collective-permute-start.4 = (f32[2,64,256]{2,1,0:T(8,128)S(1)}, f32[2,64,256]{2,1,0:T(8,128)S(1)}, u32[]{:S(2)}, u32[]{:S(2)}) collective-permute-start(f32[2,64,256]{2,1,0:T(8,128)S(1)} %extend_other.1), channel_id=1, source_target_pairs={{1,3},{5,7},{9,11},{13,15},{17,19},{21,23},{25,27},{29,31}} | collective-permute-start | bytes 393224 | tf_op jit(solution)/shard_map/ppermute | solution.py:253
  21.3 0.7 %collective-permute-start.9 = (f32[2,64,256]{2,1,0:T(8,128)S(1)}, f32[2,64,256]{2,1,0:T(8,128)S(1)}, u32[]{:S(2)}, u32[]{:S(2)}) collective-permute-start(f32[2,64,256]{2,1,0:T(8,128)S(1)} %extend_other.1), channel_id=1, source_target_pairs={{1,2},{5,6},{9,10},{13,14},{17,18},{21,22},{25,26},{29,30}} | collective-permute-start | bytes 393224 | tf_op jit(solution)/shard_map/ppermute | solution.py:253
  21.9 1.4 %collective-permute-done.6.across.two = f32[2,64,256]{2,1,0:T(8,128)S(1)} collective-permute-done((f32[2,64,256]{2,1,0:T(8,128)S(1)}, f32[2,64,256]{2,1,0:T(8,128)S(1)}, u32[]{:S(2)}, u32[]{:S(2)}) %collective-permute-start.6) | collective-permute-done | bytes 131104 | tf_op jit(solution)/shard_map/ppermute | solution.py:253
  23.3 1.3 %collective-permute-start.10 = (f32[2,64,256]{2,1,0:T(8,128)S(1)}, f32[2,64,256]{2,1,0:T(8,128)S(1)}, u32[]{:S(2)}, u32[]{:S(2)}) collective-permute-start(f32[2,64,256]{2,1,0:T(8,128)S(1)} %collective-permute-done.6.across.two), channel_id=1, source_target_pairs={{2,3},{6,7},{10,11},{14,15},{18,19},{22,23},{26,27},{30,31}} | collective-permute-start | bytes 393224 | tf_op jit(solution)/shard_map/ppermute | solution.py:253
  24.6 0.0 copy-done.1
  24.6 1.6 %before.1 = f32[2,2,256,256]{3,2,1,0:T(8,128)S(1)} custom-call(f32[1,1,2,2,256,256]{5,4,3,2,1,0:T(8,128)S(1)} %copy-done.1, f32[2,256,256]{2,1,0:T(8,128)S(1)} %get-tuple-element.37.block, f32[2,256,256]{2,1,0:T(8,128)S(1)} %collective-permute-done.theirs.turned, f32[256,256]{1,0:T(8,128)S(1)} %collective-permute-done.1.near, ...), custom_call_target="tpu_custom_call" | custom-call | tf_op jit(solution)/shard_map/before/pallas_call | solution.py:60
  26.2 0.7 %collective-permute-done.4.three = f32[2,64,256]{2,1,0:T(8,128)S(1)} collective-permute-done((f32[2,64,256]{2,1,0:T(8,128)S(1)}, f32[2,64,256]{2,1,0:T(8,128)S(1)}, u32[]{:S(2)}, u32[]{:S(2)}) %collective-permute-start.4) | collective-permute-done | bytes 131104 | tf_op jit(solution)/shard_map/ppermute | solution.py:253
  26.9 3.6 %collective-permute-start.7 = (f32[2,64,256]{2,1,0:T(8,128)S(1)}, f32[2,64,256]{2,1,0:T(8,128)S(1)}, u32[]{:S(2)}, u32[]{:S(2)}) collective-permute-start(f32[2,64,256]{2,1,0:T(8,128)S(1)} %collective-permute-done.5.piece.near.one), channel_id=1, source_target_pairs={{0,4},{1,5},{2,6},{3,7},{4,0},{5,1},{6,2},{7,3},{8,12},{9,13},{10,... | collective-permute-start | bytes 393224 | tf_op jit(solution)/shard_map/ppermute | solution.py:253
  30.5 0.0 collective-permute-start.8
  30.5 0.6 %left_near.1 = (bf16[2,2,256,128]{3,2,1,0:T(8,128)(2,1)S(1)}, bf16[2,2,256,128]{3,2,1,0:T(8,128)(2,1)S(1)}) custom-call(f32[2,2,256,256]{3,2,1,0:T(8,128)S(1)} %before.1, f32[2,64,256]{2,1,0:T(8,128)S(1)} %collective-permute-done.5.piece.near.one, f32[2,64,256]{2,1,0:T(8,128)S(1)} %collective-permute-done.6.across.two), custom_call_target="tpu_custom_call" | custom-call | tf_op jit(solution)/shard_map/left_near/pallas_call | solution.py:60
  31.1 0.6 %collective-permute-start.11 = (f32[2,64,256]{2,1,0:T(8,128)S(1)}, f32[2,64,256]{2,1,0:T(8,128)S(1)}, u32[]{:S(2)}, u32[]{:S(2)}) collective-permute-start(f32[2,64,256]{2,1,0:T(8,128)S(1)} %merge_early.1.early), channel_id=1, source_target_pairs={{0,4},{1,5},{2,6},{3,7},{4,0},{5,1},{6,2},{7,3},{8,12},{9,13},{10,... | collective-permute-start | bytes 393224 | tf_op jit(solution)/shard_map/ppermute | solution.py:253
  31.7 0.0 collective-permute-done.9.two.three
  31.7 0.0 collective-permute-done.10.three
  31.8 0.8 %collective-permute-start.12 = (f32[2,64,256]{2,1,0:T(8,128)S(1)}, f32[2,64,256]{2,1,0:T(8,128)S(1)}, u32[]{:S(2)}, u32[]{:S(2)}) collective-permute-start(f32[2,64,256]{2,1,0:T(8,128)S(1)} %merge_late.1.late), channel_id=1, source_target_pairs={{0,4},{1,5},{2,6},{3,7},{4,0},{5,1},{6,2},{7,3},{8,12},{9,13},{10,... | collective-permute-start | bytes 393224 | tf_op jit(solution)/shard_map/ppermute | solution.py:253
  32.6 0.0 collective-permute-done.7.near
  32.6 0.0 collective-permute-done.8.across
  32.6 0.6 %left_far.1 = (bf16[2,2,256,128]{3,2,1,0:T(8,128)(2,1)S(1)}, bf16[2,2,256,128]{3,2,1,0:T(8,128)(2,1)S(1)}) custom-call(f32[2,2,256,256]{3,2,1,0:T(8,128)S(1)} %before.1, f32[2,64,256]{2,1,0:T(8,128)S(1)} %collective-permute-done.7.near, f32[2,64,256]{2,1,0:T(8,128)S(1)} %collective-permute-done.8.across), custom_call_target="tpu_custom_call" | custom-call | tf_op jit(solution)/shard_map/left_far/pallas_call | solution.py:60
  33.3 0.6 %near.1 = (f32[2,2,256,128]{3,2,1,0:T(8,128)S(1)}, bf16[2,2,256,256]{3,2,1,0:T(8,128)(2,1)S(1)}, bf16[2,2,256,256]{3,2,1,0:T(8,128)(2,1)S(1)}) custom-call(bf16[2,2,256,128]{3,2,1,0:T(8,128)(2,1)S(1)} %get-tuple-element.45.high, bf16[2,2,256,128]{3,2,1,0:T(8,128)(2,1)S(1)} %get-tuple-element.46.low, bf16[2,2,256,128]{3,2,1,0:T(8,128)(2,1)S(1)} %get-tuple-element.47.far_high, ...), custom_call_target="tpu_custom_call" | custom-call | tf_op jit(solution)/shard_map/near/pallas_call | solution.py:60
  33.9 0.0 collective-permute-done.11.early
  33.9 0.0 collective-permute-done.12.late
  33.9 1.4 %far.1 = f32[1,1,2,2,256,256]{5,4,3,2,1,0:T(8,128)} custom-call(f32[2,2,256,256]{3,2,1,0:T(8,128)S(1)} %before.1, f32[2,2,256,128]{3,2,1,0:T(8,128)S(1)} %get-tuple-element.54.near, bf16[2,2,256,256]{3,2,1,0:T(8,128)(2,1)S(1)} %get-tuple-element.55.high, bf16[2,2,256,256]{3,2,1,0:T(8,128)(2,1)S(1)} %get-tuple-element.56.low, ...), custom_call_target="tpu_custom_call" | custom-call | tf_op jit(solution)/shard_map/far/pallas_call | solution.py:60
  (7 shorter events, 0.1 us)
Async XLA Ops:
  0.0 1.2 %copy-start = (f32[1,1,2,2,256,256]{5,4,3,2,1,0:T(8,128)S(1)}, f32[1,1,2,2,256,256]{5,4,3,2,1,0:T(8,128)}, u32[]{:S(2)}) copy-start(f32[1,1,2,2,256,256]{5,4,3,2,1,0:T(8,128)} %u.3) | copy-start | bytes 3145732
  1.9 2.3 %collective-permute-start = (f32[2,256,256]{2,1,0:T(8,128)S(1)}, f32[2,256,256]{2,1,0:T(8,128)S(1)}, u32[]{:S(2)}, u32[]{:S(2)}) collective-permute-start(f32[2,256,256]{2,1,0:T(8,128)S(1)} %get-tuple-element.31.mine), channel_id=1, source_target_pairs={{0,4},{1,5},{2,6},{3,7},{4,0},{5,1},{6,2},{7,3},{8,12},{9,13},{10,... | collective-permute-start | bytes 1572872 | tf_op jit(solution)/shard_map/ppermute | solution.py:253
  4.8 7.6 %collective-permute-start.1 = (f32[256,256]{1,0:T(8,128)S(1)}, f32[256,256]{1,0:T(8,128)S(1)}, u32[]{:S(2)}, u32[]{:S(2)}) collective-permute-start(f32[256,256]{1,0:T(8,128)S(1)} %get-tuple-element.33), channel_id=1, source_target_pairs={{0,8},{1,9},{2,10},{3,11},{4,12},{5,13},{6,14},{7,15},{8,0},{9,1},... | collective-permute-start | bytes 786440 | tf_op jit(solution)/shard_map/ppermute | solution.py:253
  12.4 2.4 %collective-permute-start.2 = (f32[256,256]{1,0:T(8,128)S(1)}, f32[256,256]{1,0:T(8,128)S(1)}, u32[]{:S(2)}, u32[]{:S(2)}) collective-permute-start(f32[256,256]{1,0:T(8,128)S(1)} %collective-permute-done.1.near), channel_id=1, source_target_pairs={{0,4},{1,5},{2,6},{3,7},{4,0},{5,1},{6,2},{7,3},{8,12},{9,13},{10,... | collective-permute-start | bytes 786440 | tf_op jit(solution)/shard_map/ppermute | solution.py:253
  14.8 4.7 %collective-permute-start.5 = (f32[2,64,256]{2,1,0:T(8,128)S(1)}, f32[2,64,256]{2,1,0:T(8,128)S(1)}, u32[]{:S(2)}, u32[]{:S(2)}) collective-permute-start(f32[2,64,256]{2,1,0:T(8,128)S(1)} %get-tuple-element.38), channel_id=1, source_target_pairs={{0,1},{1,0},{2,3},{3,2},{4,5},{5,4},{6,7},{7,6},{8,9},{9,8},{10,11... | collective-permute-start | bytes 393224 | tf_op jit(solution)/shard_map/ppermute | solution.py:253
  15.5 9.1 %copy-start.1 = (f32[1,1,2,2,256,256]{5,4,3,2,1,0:T(8,128)S(1)}, f32[1,1,2,2,256,256]{5,4,3,2,1,0:T(8,128)}, u32[]{:S(2)}) copy-start(f32[1,1,2,2,256,256]{5,4,3,2,1,0:T(8,128)} %u.3) | copy-start | bytes 3145732
  15.5 4.5 %collective-permute-start.3 = (f32[2,64,256]{2,1,0:T(8,128)S(1)}, f32[2,64,256]{2,1,0:T(8,128)S(1)}, u32[]{:S(2)}, u32[]{:S(2)}) collective-permute-start(f32[2,64,256]{2,1,0:T(8,128)S(1)} %get-tuple-element.35.own), channel_id=1, source_target_pairs={{0,1},{4,5},{8,9},{12,13},{16,17},{20,21},{24,25},{28,29}} | collective-permute-start | bytes 393224 | tf_op jit(solution)/shard_map/ppermute | solution.py:253
  19.5 3.8 %collective-permute-start.6 = (f32[2,64,256]{2,1,0:T(8,128)S(1)}, f32[2,64,256]{2,1,0:T(8,128)S(1)}, u32[]{:S(2)}, u32[]{:S(2)}) collective-permute-start(f32[2,64,256]{2,1,0:T(8,128)S(1)} %extend.1), channel_id=1, source_target_pairs={{0,1},{1,2},{2,3},{3,0},{4,5},{5,6},{6,7},{7,4},{8,9},{9,10},{10,1... | collective-permute-start | bytes 393224 | tf_op jit(solution)/shard_map/ppermute | solution.py:253
  20.0 6.9 %collective-permute-start.4 = (f32[2,64,256]{2,1,0:T(8,128)S(1)}, f32[2,64,256]{2,1,0:T(8,128)S(1)}, u32[]{:S(2)}, u32[]{:S(2)}) collective-permute-start(f32[2,64,256]{2,1,0:T(8,128)S(1)} %extend_other.1), channel_id=1, source_target_pairs={{1,3},{5,7},{9,11},{13,15},{17,19},{21,23},{25,27},{29,31}} | collective-permute-start | bytes 393224 | tf_op jit(solution)/shard_map/ppermute | solution.py:253
  21.3 10.4 %collective-permute-start.9 = (f32[2,64,256]{2,1,0:T(8,128)S(1)}, f32[2,64,256]{2,1,0:T(8,128)S(1)}, u32[]{:S(2)}, u32[]{:S(2)}) collective-permute-start(f32[2,64,256]{2,1,0:T(8,128)S(1)} %extend_other.1), channel_id=1, source_target_pairs={{1,2},{5,6},{9,10},{13,14},{17,18},{21,22},{25,26},{29,30}} | collective-permute-start | bytes 393224 | tf_op jit(solution)/shard_map/ppermute | solution.py:253
  23.3 8.4 %collective-permute-start.10 = (f32[2,64,256]{2,1,0:T(8,128)S(1)}, f32[2,64,256]{2,1,0:T(8,128)S(1)}, u32[]{:S(2)}, u32[]{:S(2)}) collective-permute-start(f32[2,64,256]{2,1,0:T(8,128)S(1)} %collective-permute-done.6.across.two), channel_id=1, source_target_pairs={{2,3},{6,7},{10,11},{14,15},{18,19},{22,23},{26,27},{30,31}} | collective-permute-start | bytes 393224 | tf_op jit(solution)/shard_map/ppermute | solution.py:253
  26.9 5.8 %collective-permute-start.7 = (f32[2,64,256]{2,1,0:T(8,128)S(1)}, f32[2,64,256]{2,1,0:T(8,128)S(1)}, u32[]{:S(2)}, u32[]{:S(2)}) collective-permute-start(f32[2,64,256]{2,1,0:T(8,128)S(1)} %collective-permute-done.5.piece.near.one), channel_id=1, source_target_pairs={{0,4},{1,5},{2,6},{3,7},{4,0},{5,1},{6,2},{7,3},{8,12},{9,13},{10,... | collective-permute-start | bytes 393224 | tf_op jit(solution)/shard_map/ppermute | solution.py:253
  30.5 2.2 %collective-permute-start.8 = (f32[2,64,256]{2,1,0:T(8,128)S(1)}, f32[2,64,256]{2,1,0:T(8,128)S(1)}, u32[]{:S(2)}, u32[]{:S(2)}) collective-permute-start(f32[2,64,256]{2,1,0:T(8,128)S(1)} %collective-permute-done.6.across.two), channel_id=1, source_target_pairs={{0,4},{1,5},{2,6},{3,7},{4,0},{5,1},{6,2},{7,3},{8,12},{9,13},{10,... | collective-permute-start | bytes 393224 | tf_op jit(solution)/shard_map/ppermute | solution.py:253
  31.1 2.8 %collective-permute-start.11 = (f32[2,64,256]{2,1,0:T(8,128)S(1)}, f32[2,64,256]{2,1,0:T(8,128)S(1)}, u32[]{:S(2)}, u32[]{:S(2)}) collective-permute-start(f32[2,64,256]{2,1,0:T(8,128)S(1)} %merge_early.1.early), channel_id=1, source_target_pairs={{0,4},{1,5},{2,6},{3,7},{4,0},{5,1},{6,2},{7,3},{8,12},{9,13},{10,... | collective-permute-start | bytes 393224 | tf_op jit(solution)/shard_map/ppermute | solution.py:253
  31.8 2.1 %collective-permute-start.12 = (f32[2,64,256]{2,1,0:T(8,128)S(1)}, f32[2,64,256]{2,1,0:T(8,128)S(1)}, u32[]{:S(2)}, u32[]{:S(2)}) collective-permute-start(f32[2,64,256]{2,1,0:T(8,128)S(1)} %merge_late.1.late), channel_id=1, source_target_pairs={{0,4},{1,5},{2,6},{3,7},{4,0},{5,1},{6,2},{7,3},{8,12},{9,13},{10,... | collective-permute-start | bytes 393224 | tf_op jit(solution)/shard_map/ppermute | solution.py:253

commit v7 on v6

--- a/solution.py
+++ b/solution.py
@@ -145,39 +145,39 @@
     return stack(pick(k == 0, mine, theirs), pick(k == 0, theirs, mine))
 
 
-def before_kernel(u, block, turned, near, far, out):
+def before_kernel(u, block, turned, near, far, out, high, low):
     x, k, _ = place()
     one = identity(block.shape[-1])
     other = pick(k == 0, (near[...], far[...]), (far[...], near[...]))
     before = product(pick(x == 1, other, one), pick(k == 1, pair(turned), one))
-    put(out.at[0], product(pair(u[0, 0, 0]), before, NT))
-    put(out.at[1], product(pair(block), before, NT))
-
-
-def left_kernel(before, near, across, high, low, *, mine):
-    x, k, w = place()
-    width = high.shape[-1]
+    for slot, left in enumerate((pair(u[0, 0, 0]), pair(block))):
+        value = product(left, before, NT)
+        put(out.at[slot], value)
+        for plane in range(2):
+            high[slot, plane], low[slot, plane] = halves(value[plane])
+
+
+def left_half(before, near, across, core, high, low):
+    x, _, w = place()
+    width = before[0].shape[-1] // 2
 
     @pl.when(w == 3)
     def _():
-        strips = half(x, near, across)
+        strips = halves(jnp.concatenate(half(x, near, across), axis=0))
         for slot in range(2):
-            value = columns_of(*parts_of(before, slot), 0, halves(jnp.concatenate(strips, axis=0)))
+            value = columns_of(*before, slot, strips)
             for plane in range(2):
                 high[slot, plane], low[slot, plane] = halves(value[plane])
 
     @pl.when((w == 1) | (w == 2))
     def _():
-        core = k if mine else 1 - k
-        for slot in range(2):
-            for plane in range(2):
-                value = before[slot, plane, :, pl.ds(pl.multiple_of(core * width, width), width)]
-                high[slot, plane], low[slot, plane] = halves(value)
-
-
-def parts_of(ref, slot):
-    planes = [halves(ref[slot, plane]) for plane in range(2)]
-    return tuple({(0, plane): planes[plane][part] for plane in range(2)} for part in range(2))
+        at = pl.ds(pl.multiple_of(core * width, width), width)
+        high[...], low[...] = (part[:, :, :, at] for part in before)
+
+
+def left_kernel(before_high, before_low, near, across, high, low):
+    _, k, _ = place()
+    left_half((before_high, before_low), near, across, k, high, low)
 
 
 def merge_kernel(one, two, three, out):
@@ -204,8 +204,11 @@
     return {(slot, index): plane(slot, index) for slot in range(2) for index in range(2)}
 
 
-def near_kernel(high, low, far_high, far_low, early, late, out, whole_high, whole_low):
+def near_kernel(
+    before_high, before_low, far_own, far_past, high, low, early, late, out, whole_high, whole_low, far_high, far_low
+):
     x, k, w = place()
+    left_half((before_high, before_low), far_own, far_past, 1 - k, far_high, far_low)
 
     @pl.when(w != 0)
     def _():
@@ -277,7 +280,6 @@
     )
     one = permute(own, twins)
     (window,) = call(window_kernel, [full], chip, near_chip, far_chip, name="window")
-    other, window = tie((other, window))
     one_other = permute(other, zero_one)
     (both,) = call(extend_kernel, [strip], one, window, other, name="extend")
     two = permute(both, onward)
@@ -288,12 +290,12 @@
     own, past = tie((one, two))
     far_own, far_past = permute(own, cores), permute(past, cores)
     far_chip, _ = tie((far_chip, two))
-    (before,) = call(
-        before_kernel, [(2, *full)], unitaries, block, turned_other, near_chip, far_chip, name="before"
-    )
+    both = jax.ShapeDtypeStruct((2, *full), jnp.bfloat16)
+    operands = unitaries, block, turned_other, near_chip, far_chip
+    before, *before_parts = call(before_kernel, [(2, *full), both, both], *operands, name="before")
     three_other, before = tie((three_other, before))
     parts = [jax.ShapeDtypeStruct((2, 2, width, width // 2), jnp.bfloat16)] * 2
-    high, low = call(functools.partial(left_kernel, mine=True), parts, before, own, past, name="left_near")
+    high, low = call(left_kernel, parts, *before_parts, own, past, name="left")
     three_other, high = tie((three_other, high))
     (early,) = call(merge_kernel, [strip], one, two, three_other, name="merge_early")
     far_early = permute(early, cores)
@@ -302,9 +304,10 @@
     three, other = tie((three, other))
     (late,) = call(merge_kernel, [strip], other, other, three, name="merge_late")
     far_late = permute(late, cores)
-    theirs = call(functools.partial(left_kernel, mine=False), parts, before, far_own, far_past, name="left_far")
-    half_width, both = (2, 2, width, width // 2), jax.ShapeDtypeStruct((2, *full), jnp.bfloat16)
-    near, high, low = call(near_kernel, [half_width, both, both], high, low, *theirs, early, late, name="near")
+    half_width = (2, 2, width, width // 2)
+    operands = *before_parts, far_own, far_past, high, low, early, late
+    scratch = [pltpu.VMEM(half_width, jnp.bfloat16)] * 2
+    near, high, low = call(near_kernel, [half_width, both, both], *operands, name="near", scratch=scratch)
     scratch = pltpu.VMEM(half_width, F32), pltpu.SemaphoreType.DMA((2, 2))
     operands = before, near, high, low, far_early, far_late
     (out,) = call(far_kernel, [unitaries.shape], *operands, name="far", scratch=scratch, hbm_out=True)

time: 35.6 us -> 35.5 us (level)
  waiting for transfers between devices: 14.3 us -> 13.7 us
  starting transfers between devices: 13.4 us -> 13.9 us
    ppermute x13, waiting for transfers between devices: 14.3 us -> 13.7 us  [permute(): return lax.ppermute(value, AXES, flat)]
    ppermute x13, starting transfers between devices: 13.4 us -> 13.9 us  [permute(): return lax.ppermute(value, AXES, flat)]
    pallas_call x14 -> x13, Pallas kernels: 6.31 us -> 6.34 us  [call(): pl.pallas_call(body, out_shape=shapes, in_specs=[far if i == alias else w...]
  transfers between devices with their start and end apart: 13 -> 13, of which waited for: 6 -> 5; matrix products, arithmetic and copies ran while one was open for 0% -> 0% of each run, Pallas kernels for 10% -> 10%
where the time goes in v7:
time: 35.5 us; the launch traced here: 35.3 us
  starting transfers between devices  13.9 us (39%)
  waiting for transfers between devices  13.7 us (39%)
  Pallas kernels  6.34 us (18%)
  local copies, waits for them, and re-layouts  1.23 us (3%)
    ppermute x13, starting transfers between devices, permute(): return lax.ppermute(value, AXES, flat)  13.9 us
    ppermute x13, waiting for transfers between devices, permute(): return lax.ppermute(value, AXES, flat)  13.7 us
    pallas_call x13, Pallas kernels, call(): pl.pallas_call(body, out_shape=shapes, in_specs=[far if i == alias else w...  6.34 us
    unnamed x4, local copies, waits for them, and re-layouts  1.23 us
  transfers between devices with their start and end apart: 13, of which 5 were waited for; matrix products, arithmetic and copies ran while one was open for 0% of the time, Pallas kernels for 10%

profile of v7, /device:TPU:29, one launch (start us, length us, event | category | flops | bytes accessed | tf_op | source)
XLA Modules:
  0.0 35.3 jit_solution(3377083983700137806)
XLA Ops:
  0.0 0.0 copy-start
  0.0 1.2 %copy-done = f32[1,1,2,2,256,256]{5,4,3,2,1,0:T(8,128)S(1)} copy-done((f32[1,1,2,2,256,256]{5,4,3,2,1,0:T(8,128)S(1)}, f32[1,1,2,2,256,256]{5,4,3,2,1,0:T(8,128)}, u32[]{:S(2)}) %copy-start) | copy-done | bytes 1048600
  1.2 0.7 %block.1 = (f32[2,256,256]{2,1,0:T(8,128)S(1)}, f32[2,256,256]{2,1,0:T(8,128)S(1)}) custom-call(f32[1,1,2,2,256,256]{5,4,3,2,1,0:T(8,128)S(1)} %copy-done), custom_call_target="tpu_custom_call" | custom-call | tf_op jit(solution)/shard_map/block/pallas_call | solution.py:60
  1.9 0.7 %collective-permute-start = (f32[2,256,256]{2,1,0:T(8,128)S(1)}, f32[2,256,256]{2,1,0:T(8,128)S(1)}, u32[]{:S(2)}, u32[]{:S(2)}) collective-permute-start(f32[2,256,256]{2,1,0:T(8,128)S(1)} %get-tuple-element.30.mine), channel_id=1, source_target_pairs={{0,4},{1,5},{2,6},{3,7},{4,0},{5,1},{6,2},{7,3},{8,12},{9,13},{10,... | collective-permute-start | bytes 1572872 | tf_op jit(solution)/shard_map/ppermute | solution.py:256
  2.7 1.5 %collective-permute-done.theirs.turned = f32[2,256,256]{2,1,0:T(8,128)S(1)} collective-permute-done((f32[2,256,256]{2,1,0:T(8,128)S(1)}, f32[2,256,256]{2,1,0:T(8,128)S(1)}, u32[]{:S(2)}, u32[]{:S(2)}) %collective-permute-start) | collective-permute-done | bytes 524320 | tf_op jit(solution)/shard_map/ppermute | solution.py:256
  4.2 0.6 %chip.1 = (f32[2,256,256]{2,1,0:T(8,128)S(1)}, f32[256,256]{1,0:T(8,128)S(1)}) custom-call(f32[2,256,256]{2,1,0:T(8,128)S(1)} %get-tuple-element.30.mine, f32[2,256,256]{2,1,0:T(8,128)S(1)} %collective-permute-done.theirs.turned), custom_call_target="tpu_custom_call" | custom-call | tf_op jit(solution)/shard_map/chip/pallas_call | solution.py:60
  4.8 1.3 %collective-permute-start.1 = (f32[256,256]{1,0:T(8,128)S(1)}, f32[256,256]{1,0:T(8,128)S(1)}, u32[]{:S(2)}, u32[]{:S(2)}) collective-permute-start(f32[256,256]{1,0:T(8,128)S(1)} %get-tuple-element.32), channel_id=1, source_target_pairs={{0,8},{1,9},{2,10},{3,11},{4,12},{5,13},{6,14},{7,15},{8,0},{9,1},... | collective-permute-start | bytes 786440 | tf_op jit(solution)/shard_map/ppermute | solution.py:256
  6.1 6.3 %collective-permute-done.1.near = f32[256,256]{1,0:T(8,128)S(1)} collective-permute-done((f32[256,256]{1,0:T(8,128)S(1)}, f32[256,256]{1,0:T(8,128)S(1)}, u32[]{:S(2)}, u32[]{:S(2)}) %collective-permute-start.1) | collective-permute-done | bytes 262176 | tf_op jit(solution)/shard_map/ppermute | solution.py:256
  12.4 1.2 %collective-permute-start.2 = (f32[256,256]{1,0:T(8,128)S(1)}, f32[256,256]{1,0:T(8,128)S(1)}, u32[]{:S(2)}, u32[]{:S(2)}) collective-permute-start(f32[256,256]{1,0:T(8,128)S(1)} %collective-permute-done.1.near), channel_id=1, source_target_pairs={{0,4},{1,5},{2,6},{3,7},{4,0},{5,1},{6,2},{7,3},{8,12},{9,13},{10,... | collective-permute-start | bytes 786440 | tf_op jit(solution)/shard_map/ppermute | solution.py:256
  13.6 1.2 %collective-permute-done.2.far = f32[256,256]{1,0:T(8,128)S(1)} collective-permute-done((f32[256,256]{1,0:T(8,128)S(1)}, f32[256,256]{1,0:T(8,128)S(1)}, u32[]{:S(2)}, u32[]{:S(2)}) %collective-permute-start.2) | collective-permute-done | bytes 262176 | tf_op jit(solution)/shard_map/ppermute | solution.py:256
  14.8 0.7 %collective-permute-start.5 = (f32[2,64,256]{2,1,0:T(8,128)S(1)}, f32[2,64,256]{2,1,0:T(8,128)S(1)}, u32[]{:S(2)}, u32[]{:S(2)}) collective-permute-start(f32[2,64,256]{2,1,0:T(8,128)S(1)} %get-tuple-element.35), channel_id=1, source_target_pairs={{0,1},{1,0},{2,3},{3,2},{4,5},{5,4},{6,7},{7,6},{8,9},{9,8},{10,11... | collective-permute-start | bytes 393224 | tf_op jit(solution)/shard_map/ppermute | solution.py:256
  15.5 0.7 %collective-permute-start.3 = (f32[2,64,256]{2,1,0:T(8,128)S(1)}, f32[2,64,256]{2,1,0:T(8,128)S(1)}, u32[]{:S(2)}, u32[]{:S(2)}) collective-permute-start(f32[2,64,256]{2,1,0:T(8,128)S(1)} %get-tuple-element.33.own), channel_id=1, source_target_pairs={{0,1},{4,5},{8,9},{12,13},{16,17},{20,21},{24,25},{28,29}} | collective-permute-start | bytes 393224 | tf_op jit(solution)/shard_map/ppermute | solution.py:256
  16.2 0.0 copy-start.1
  16.2 3.3 %collective-permute-done.5.piece.near.one = f32[2,64,256]{2,1,0:T(8,128)S(1)} collective-permute-done((f32[2,64,256]{2,1,0:T(8,128)S(1)}, f32[2,64,256]{2,1,0:T(8,128)S(1)}, u32[]{:S(2)}, u32[]{:S(2)}) %collective-permute-start.5) | collective-permute-done | bytes 131104 | tf_op jit(solution)/shard_map/ppermute | solution.py:256
  19.5 0.5 %collective-permute-start.6 = (f32[2,64,256]{2,1,0:T(8,128)S(1)}, f32[2,64,256]{2,1,0:T(8,128)S(1)}, u32[]{:S(2)}, u32[]{:S(2)}) collective-permute-start(f32[2,64,256]{2,1,0:T(8,128)S(1)} %extend.1), channel_id=1, source_target_pairs={{0,1},{1,2},{2,3},{3,0},{4,5},{5,6},{6,7},{7,4},{8,9},{9,10},{10,1... | collective-permute-start | bytes 393224 | tf_op jit(solution)/shard_map/ppermute | solution.py:256
  20.0 0.0 collective-permute-done.3.piece.one
  20.0 1.3 %collective-permute-start.4 = (f32[2,64,256]{2,1,0:T(8,128)S(1)}, f32[2,64,256]{2,1,0:T(8,128)S(1)}, u32[]{:S(2)}, u32[]{:S(2)}) collective-permute-start(f32[2,64,256]{2,1,0:T(8,128)S(1)} %extend_other.1), channel_id=1, source_target_pairs={{1,3},{5,7},{9,11},{13,15},{17,19},{21,23},{25,27},{29,31}} | collective-permute-start | bytes 393224 | tf_op jit(solution)/shard_map/ppermute | solution.py:256
  21.3 0.7 %collective-permute-start.9 = (f32[2,64,256]{2,1,0:T(8,128)S(1)}, f32[2,64,256]{2,1,0:T(8,128)S(1)}, u32[]{:S(2)}, u32[]{:S(2)}) collective-permute-start(f32[2,64,256]{2,1,0:T(8,128)S(1)} %extend_other.1), channel_id=1, source_target_pairs={{1,2},{5,6},{9,10},{13,14},{17,18},{21,22},{25,26},{29,30}} | collective-permute-start | bytes 393224 | tf_op jit(solution)/shard_map/ppermute | solution.py:256
  21.9 1.4 %collective-permute-done.6.across.two = f32[2,64,256]{2,1,0:T(8,128)S(1)} collective-permute-done((f32[2,64,256]{2,1,0:T(8,128)S(1)}, f32[2,64,256]{2,1,0:T(8,128)S(1)}, u32[]{:S(2)}, u32[]{:S(2)}) %collective-permute-start.6) | collective-permute-done | bytes 131104 | tf_op jit(solution)/shard_map/ppermute | solution.py:256
  23.3 1.3 %collective-permute-start.10 = (f32[2,64,256]{2,1,0:T(8,128)S(1)}, f32[2,64,256]{2,1,0:T(8,128)S(1)}, u32[]{:S(2)}, u32[]{:S(2)}) collective-permute-start(f32[2,64,256]{2,1,0:T(8,128)S(1)} %collective-permute-done.6.across.two), channel_id=1, source_target_pairs={{2,3},{6,7},{10,11},{14,15},{18,19},{22,23},{26,27},{30,31}} | collective-permute-start | bytes 393224 | tf_op jit(solution)/shard_map/ppermute | solution.py:256
  24.6 2.4 %collective-permute-start.7 = (f32[2,64,256]{2,1,0:T(8,128)S(1)}, f32[2,64,256]{2,1,0:T(8,128)S(1)}, u32[]{:S(2)}, u32[]{:S(2)}) collective-permute-start(f32[2,64,256]{2,1,0:T(8,128)S(1)} %collective-permute-done.5.piece.near.one), channel_id=1, source_target_pairs={{0,4},{1,5},{2,6},{3,7},{4,0},{5,1},{6,2},{7,3},{8,12},{9,13},{10,... | collective-permute-start | bytes 393224 | tf_op jit(solution)/shard_map/ppermute | solution.py:256
  27.0 0.1 collective-permute-start.8
  27.1 0.0 copy-done.1
  27.1 1.6 %before.1 = (f32[2,2,256,256]{3,2,1,0:T(8,128)S(1)}, bf16[2,2,256,256]{3,2,1,0:T(8,128)(2,1)S(1)}, bf16[2,2,256,256]{3,2,1,0:T(8,128)(2,1)S(1)}) custom-call(f32[1,1,2,2,256,256]{5,4,3,2,1,0:T(8,128)S(1)} %copy-done.1, f32[2,256,256]{2,1,0:T(8,128)S(1)} %get-tuple-element.34.block, f32[2,256,256]{2,1,0:T(8,128)S(1)} %collective-permute-done.theirs.turned, ...), custom_call_target="tpu_custom_call" | custom-call | tf_op jit(solution)/shard_map/before/pallas_call | solution.py:60
  28.7 0.0 collective-permute-done.4.three
  28.7 0.6 %left.1 = (bf16[2,2,256,128]{3,2,1,0:T(8,128)(2,1)S(1)}, bf16[2,2,256,128]{3,2,1,0:T(8,128)(2,1)S(1)}) custom-call(bf16[2,2,256,256]{3,2,1,0:T(8,128)(2,1)S(1)} %get-tuple-element.39.before_high, bf16[2,2,256,256]{3,2,1,0:T(8,128)(2,1)S(1)} %get-tuple-element.40.before_low, f32[2,64,256]{2,1,0:T(8,128)S(1)} %collective-permute-done.5.piece.near.one, ...), custom_call_target="tpu_custom_call" | custom-call | tf_op jit(solution)/shard_map/left/pallas_call | solution.py:60
  29.4 1.8 %collective-permute-start.11 = (f32[2,64,256]{2,1,0:T(8,128)S(1)}, f32[2,64,256]{2,1,0:T(8,128)S(1)}, u32[]{:S(2)}, u32[]{:S(2)}) collective-permute-start(f32[2,64,256]{2,1,0:T(8,128)S(1)} %merge_early.1.early), channel_id=1, source_target_pairs={{0,4},{1,5},{2,6},{3,7},{4,0},{5,1},{6,2},{7,3},{8,12},{9,13},{10,... | collective-permute-start | bytes 393224 | tf_op jit(solution)/shard_map/ppermute | solution.py:256
  31.2 0.0 collective-permute-done.9.two.three
  31.2 0.0 collective-permute-done.10.three
  31.3 1.4 %collective-permute-start.12 = (f32[2,64,256]{2,1,0:T(8,128)S(1)}, f32[2,64,256]{2,1,0:T(8,128)S(1)}, u32[]{:S(2)}, u32[]{:S(2)}) collective-permute-start(f32[2,64,256]{2,1,0:T(8,128)S(1)} %merge_late.1.late), channel_id=1, source_target_pairs={{0,4},{1,5},{2,6},{3,7},{4,0},{5,1},{6,2},{7,3},{8,12},{9,13},{10,... | collective-permute-start | bytes 393224 | tf_op jit(solution)/shard_map/ppermute | solution.py:256
  32.6 0.0 collective-permute-done.7.far_own
  32.6 0.0 collective-permute-done.8.far_past
  32.6 1.2 %near.1 = (f32[2,2,256,128]{3,2,1,0:T(8,128)S(1)}, bf16[2,2,256,256]{3,2,1,0:T(8,128)(2,1)S(1)}, bf16[2,2,256,256]{3,2,1,0:T(8,128)(2,1)S(1)}) custom-call(bf16[2,2,256,256]{3,2,1,0:T(8,128)(2,1)S(1)} %get-tuple-element.39.before_high, bf16[2,2,256,256]{3,2,1,0:T(8,128)(2,1)S(1)} %get-tuple-element.40.before_low, ...), custom_call_target="tpu_custom_call" | custom-call | tf_op jit(solution)/shard_map/near/pallas_call | solution.py:60
  33.9 0.0 collective-permute-done.11.early
  33.9 0.0 collective-permute-done.12.late
  33.9 1.4 %far.1 = f32[1,1,2,2,256,256]{5,4,3,2,1,0:T(8,128)} custom-call(f32[2,2,256,256]{3,2,1,0:T(8,128)S(1)} %get-tuple-element.38.before, f32[2,2,256,128]{3,2,1,0:T(8,128)S(1)} %get-tuple-element.52.near, bf16[2,2,256,256]{3,2,1,0:T(8,128)(2,1)S(1)} %get-tuple-element.53.high, bf16[2,2,256,256]{3,2,1,0:T(8,128)(2,1)S(1)} %get-tuple-element.54.low, ...), custom_call_target="tpu_custom_call" | custom-call | tf_op jit(solution)/shard_map/far/pallas_call | solution.py:60
  (7 shorter events, 0.1 us)
Async XLA Ops:
  0.0 1.2 %copy-start = (f32[1,1,2,2,256,256]{5,4,3,2,1,0:T(8,128)S(1)}, f32[1,1,2,2,256,256]{5,4,3,2,1,0:T(8,128)}, u32[]{:S(2)}) copy-start(f32[1,1,2,2,256,256]{5,4,3,2,1,0:T(8,128)} %u.3) | copy-start | bytes 3145732
  1.9 2.3 %collective-permute-start = (f32[2,256,256]{2,1,0:T(8,128)S(1)}, f32[2,256,256]{2,1,0:T(8,128)S(1)}, u32[]{:S(2)}, u32[]{:S(2)}) collective-permute-start(f32[2,256,256]{2,1,0:T(8,128)S(1)} %get-tuple-element.30.mine), channel_id=1, source_target_pairs={{0,4},{1,5},{2,6},{3,7},{4,0},{5,1},{6,2},{7,3},{8,12},{9,13},{10,... | collective-permute-start | bytes 1572872 | tf_op jit(solution)/shard_map/ppermute | solution.py:256
  4.8 7.6 %collective-permute-start.1 = (f32[256,256]{1,0:T(8,128)S(1)}, f32[256,256]{1,0:T(8,128)S(1)}, u32[]{:S(2)}, u32[]{:S(2)}) collective-permute-start(f32[256,256]{1,0:T(8,128)S(1)} %get-tuple-element.32), channel_id=1, source_target_pairs={{0,8},{1,9},{2,10},{3,11},{4,12},{5,13},{6,14},{7,15},{8,0},{9,1},... | collective-permute-start | bytes 786440 | tf_op jit(solution)/shard_map/ppermute | solution.py:256
  12.4 2.4 %collective-permute-start.2 = (f32[256,256]{1,0:T(8,128)S(1)}, f32[256,256]{1,0:T(8,128)S(1)}, u32[]{:S(2)}, u32[]{:S(2)}) collective-permute-start(f32[256,256]{1,0:T(8,128)S(1)} %collective-permute-done.1.near), channel_id=1, source_target_pairs={{0,4},{1,5},{2,6},{3,7},{4,0},{5,1},{6,2},{7,3},{8,12},{9,13},{10,... | collective-permute-start | bytes 786440 | tf_op jit(solution)/shard_map/ppermute | solution.py:256
  14.8 4.7 %collective-permute-start.5 = (f32[2,64,256]{2,1,0:T(8,128)S(1)}, f32[2,64,256]{2,1,0:T(8,128)S(1)}, u32[]{:S(2)}, u32[]{:S(2)}) collective-permute-start(f32[2,64,256]{2,1,0:T(8,128)S(1)} %get-tuple-element.35), channel_id=1, source_target_pairs={{0,1},{1,0},{2,3},{3,2},{4,5},{5,4},{6,7},{7,6},{8,9},{9,8},{10,11... | collective-permute-start | bytes 393224 | tf_op jit(solution)/shard_map/ppermute | solution.py:256
  15.5 4.5 %collective-permute-start.3 = (f32[2,64,256]{2,1,0:T(8,128)S(1)}, f32[2,64,256]{2,1,0:T(8,128)S(1)}, u32[]{:S(2)}, u32[]{:S(2)}) collective-permute-start(f32[2,64,256]{2,1,0:T(8,128)S(1)} %get-tuple-element.33.own), channel_id=1, source_target_pairs={{0,1},{4,5},{8,9},{12,13},{16,17},{20,21},{24,25},{28,29}} | collective-permute-start | bytes 393224 | tf_op jit(solution)/shard_map/ppermute | solution.py:256
  16.2 10.9 %copy-start.1 = (f32[1,1,2,2,256,256]{5,4,3,2,1,0:T(8,128)S(1)}, f32[1,1,2,2,256,256]{5,4,3,2,1,0:T(8,128)}, u32[]{:S(2)}) copy-start(f32[1,1,2,2,256,256]{5,4,3,2,1,0:T(8,128)} %u.3) | copy-start | bytes 3145732
  19.5 3.8 %collective-permute-start.6 = (f32[2,64,256]{2,1,0:T(8,128)S(1)}, f32[2,64,256]{2,1,0:T(8,128)S(1)}, u32[]{:S(2)}, u32[]{:S(2)}) collective-permute-start(f32[2,64,256]{2,1,0:T(8,128)S(1)} %extend.1), channel_id=1, source_target_pairs={{0,1},{1,2},{2,3},{3,0},{4,5},{5,6},{6,7},{7,4},{8,9},{9,10},{10,1... | collective-permute-start | bytes 393224 | tf_op jit(solution)/shard_map/ppermute | solution.py:256
  20.0 8.8 %collective-permute-start.4 = (f32[2,64,256]{2,1,0:T(8,128)S(1)}, f32[2,64,256]{2,1,0:T(8,128)S(1)}, u32[]{:S(2)}, u32[]{:S(2)}) collective-permute-start(f32[2,64,256]{2,1,0:T(8,128)S(1)} %extend_other.1), channel_id=1, source_target_pairs={{1,3},{5,7},{9,11},{13,15},{17,19},{21,23},{25,27},{29,31}} | collective-permute-start | bytes 393224 | tf_op jit(solution)/shard_map/ppermute | solution.py:256
  21.3 9.9 %collective-permute-start.9 = (f32[2,64,256]{2,1,0:T(8,128)S(1)}, f32[2,64,256]{2,1,0:T(8,128)S(1)}, u32[]{:S(2)}, u32[]{:S(2)}) collective-permute-start(f32[2,64,256]{2,1,0:T(8,128)S(1)} %extend_other.1), channel_id=1, source_target_pairs={{1,2},{5,6},{9,10},{13,14},{17,18},{21,22},{25,26},{29,30}} | collective-permute-start | bytes 393224 | tf_op jit(solution)/shard_map/ppermute | solution.py:256
  23.3 7.9 %collective-permute-start.10 = (f32[2,64,256]{2,1,0:T(8,128)S(1)}, f32[2,64,256]{2,1,0:T(8,128)S(1)}, u32[]{:S(2)}, u32[]{:S(2)}) collective-permute-start(f32[2,64,256]{2,1,0:T(8,128)S(1)} %collective-permute-done.6.across.two), channel_id=1, source_target_pairs={{2,3},{6,7},{10,11},{14,15},{18,19},{22,23},{26,27},{30,31}} | collective-permute-start | bytes 393224 | tf_op jit(solution)/shard_map/ppermute | solution.py:256
  24.6 8.0 %collective-permute-start.7 = (f32[2,64,256]{2,1,0:T(8,128)S(1)}, f32[2,64,256]{2,1,0:T(8,128)S(1)}, u32[]{:S(2)}, u32[]{:S(2)}) collective-permute-start(f32[2,64,256]{2,1,0:T(8,128)S(1)} %collective-permute-done.5.piece.near.one), channel_id=1, source_target_pairs={{0,4},{1,5},{2,6},{3,7},{4,0},{5,1},{6,2},{7,3},{8,12},{9,13},{10,... | collective-permute-start | bytes 393224 | tf_op jit(solution)/shard_map/ppermute | solution.py:256
  27.0 5.6 %collective-permute-start.8 = (f32[2,64,256]{2,1,0:T(8,128)S(1)}, f32[2,64,256]{2,1,0:T(8,128)S(1)}, u32[]{:S(2)}, u32[]{:S(2)}) collective-permute-start(f32[2,64,256]{2,1,0:T(8,128)S(1)} %collective-permute-done.6.across.two), channel_id=1, source_target_pairs={{0,4},{1,5},{2,6},{3,7},{4,0},{5,1},{6,2},{7,3},{8,12},{9,13},{10,... | collective-permute-start | bytes 393224 | tf_op jit(solution)/shard_map/ppermute | solution.py:256
  29.4 4.5 %collective-permute-start.11 = (f32[2,64,256]{2,1,0:T(8,128)S(1)}, f32[2,64,256]{2,1,0:T(8,128)S(1)}, u32[]{:S(2)}, u32[]{:S(2)}) collective-permute-start(f32[2,64,256]{2,1,0:T(8,128)S(1)} %merge_early.1.early), channel_id=1, source_target_pairs={{0,4},{1,5},{2,6},{3,7},{4,0},{5,1},{6,2},{7,3},{8,12},{9,13},{10,... | collective-permute-start | bytes 393224 | tf_op jit(solution)/shard_map/ppermute | solution.py:256
  31.3 2.6 %collective-permute-start.12 = (f32[2,64,256]{2,1,0:T(8,128)S(1)}, f32[2,64,256]{2,1,0:T(8,128)S(1)}, u32[]{:S(2)}, u32[]{:S(2)}) collective-permute-start(f32[2,64,256]{2,1,0:T(8,128)S(1)} %merge_late.1.late), channel_id=1, source_target_pairs={{0,4},{1,5},{2,6},{3,7},{4,0},{5,1},{6,2},{7,3},{8,12},{9,13},{10,... | collective-permute-start | bytes 393224 | tf_op jit(solution)/shard_map/ppermute | solution.py:256

commit v8 on v7

--- a/solution.py
+++ b/solution.py
@@ -32,6 +32,12 @@
         real(lr, lrl, rr, rrl) - real(li, lil, ri, ril),
         real(lr, lrl, ri, ril) + real(li, lil, rr, rrl),
     )
+
+
+def real_product(left, right):
+    (a, al), (b, bl) = halves(left), halves(right)
+    dot = functools.partial(jnp.dot, preferred_element_type=F32)
+    return dot(a, b) + (dot(a, bl) + dot(al, b))
 
 
 def pick(condition, yes, no):
@@ -80,13 +86,32 @@
     put(turned, (b[0].T, b[1].T))
 
 
-def chip_kernel(mine, theirs, chip, plane):
+def plane_kernel(mine, theirs, plane):
     _, k, _ = place()
-    first = pick(k == 0, pair(mine), pair(theirs))
-    second = pick(k == 0, pair(theirs), pair(mine))
-    value = product(first, second)
-    put(chip, value)
-    plane[...] = jnp.where(k == 0, value[0], value[1])
+
+    @pl.when(k == 0)
+    def _():
+        (lr, li), (rr, ri) = pair(mine), pair(theirs)
+        plane[...] = real_product(lr, rr) - real_product(li, ri)
+
+    @pl.when(k == 1)
+    def _():
+        (lr, li), (rr, ri) = pair(theirs), pair(mine)
+        plane[...] = real_product(lr, ri) + real_product(li, rr)
+
+
+def chip_kernel(mine, theirs, plane, chip):
+    _, k, _ = place()
+
+    @pl.when(k == 0)
+    def _():
+        (lr, li), (rr, ri) = pair(mine), pair(theirs)
+        put(chip, (plane[...], real_product(lr, ri) + real_product(li, rr)))
+
+    @pl.when(k == 1)
+    def _():
+        (lr, li), (rr, ri) = pair(theirs), pair(mine)
+        put(chip, (real_product(lr, rr) - real_product(li, ri), plane[...]))
 
 
 def ordered(x, k, chip, near, far):
@@ -272,8 +297,10 @@
 
     block, turned = call(block_kernel, [full, full], unitaries, name="block")
     turned_other = permute(turned, cores)
-    chip, plane = call(chip_kernel, [full, full[1:]], turned, turned_other, name="chip")
+    (plane,) = call(plane_kernel, [full[1:]], turned, turned_other, name="plane")
     near_chip = permute(plane, chips)
+    (chip,) = call(chip_kernel, [full], turned, turned_other, plane, name="chip")
+    near_chip, chip = tie((near_chip, chip))
     far_chip = permute(near_chip, cores)
     own, other = call(
         strips_kernel, [strip, strip], chip, near_chip, far_chip, name="strips", scratch=[pltpu.VMEM(full, F32)]

time: 35.5 us -> 35.3 us (level)
  waiting for transfers between devices: 13.7 us -> 13.3 us
    ppermute x13, waiting for transfers between devices: 13.7 us -> 13.3 us  [permute(): return lax.ppermute(value, AXES, flat)]
    pallas_call x13 -> x14, Pallas kernels: 6.34 us -> 6.51 us  [call(): pl.pallas_call(body, out_shape=shapes, in_specs=[far if i == alias else w...]
  transfers between devices with their start and end apart: 13 -> 13, of which waited for: 5 -> 5; matrix products, arithmetic and copies ran while one was open for 0% -> 0% of each run, Pallas kernels for 10% -> 11%
where the time goes in v8:
time: 35.3 us; the launch traced here: 35.1 us
  starting transfers between devices  13.9 us (39%)
  waiting for transfers between devices  13.3 us (38%)
  Pallas kernels  6.51 us (18%)
  local copies, waits for them, and re-layouts  1.23 us (3%)
    ppermute x13, starting transfers between devices, permute(): return lax.ppermute(value, AXES, flat)  13.9 us
    ppermute x13, waiting for transfers between devices, permute(): return lax.ppermute(value, AXES, flat)  13.3 us
    pallas_call x14, Pallas kernels, call(): pl.pallas_call(body, out_shape=shapes, in_specs=[far if i == alias else w...  6.51 us
    unnamed x4, local copies, waits for them, and re-layouts  1.23 us
  transfers between devices with their start and end apart: 13, of which 5 were waited for; matrix products, arithmetic and copies ran while one was open for 0% of the time, Pallas kernels for 11%

profile of v8, /device:TPU:29, one launch (start us, length us, event | category | flops | bytes accessed | tf_op | source)
XLA Modules:
  0.0 35.1 jit_solution(16999325113638403542)
XLA Ops:
  0.0 0.0 copy-start
  0.0 1.2 %copy-done = f32[1,1,2,2,256,256]{5,4,3,2,1,0:T(8,128)S(1)} copy-done((f32[1,1,2,2,256,256]{5,4,3,2,1,0:T(8,128)S(1)}, f32[1,1,2,2,256,256]{5,4,3,2,1,0:T(8,128)}, u32[]{:S(2)}) %copy-start) | copy-done | bytes 1048600
  1.2 0.7 %block.1 = (f32[2,256,256]{2,1,0:T(8,128)S(1)}, f32[2,256,256]{2,1,0:T(8,128)S(1)}) custom-call(f32[1,1,2,2,256,256]{5,4,3,2,1,0:T(8,128)S(1)} %copy-done), custom_call_target="tpu_custom_call" | custom-call | tf_op jit(solution)/shard_map/block/pallas_call | solution.py:66
  1.9 0.7 %collective-permute-start = (f32[2,256,256]{2,1,0:T(8,128)S(1)}, f32[2,256,256]{2,1,0:T(8,128)S(1)}, u32[]{:S(2)}, u32[]{:S(2)}) collective-permute-start(f32[2,256,256]{2,1,0:T(8,128)S(1)} %get-tuple-element.30.mine), channel_id=1, source_target_pairs={{0,4},{1,5},{2,6},{3,7},{4,0},{5,1},{6,2},{7,3},{8,12},{9,13},{10,... | collective-permute-start | bytes 1572872 | tf_op jit(solution)/shard_map/ppermute | solution.py:281
  2.7 1.5 %collective-permute-done.theirs.turned = f32[2,256,256]{2,1,0:T(8,128)S(1)} collective-permute-done((f32[2,256,256]{2,1,0:T(8,128)S(1)}, f32[2,256,256]{2,1,0:T(8,128)S(1)}, u32[]{:S(2)}, u32[]{:S(2)}) %collective-permute-start) | collective-permute-done | bytes 524320 | tf_op jit(solution)/shard_map/ppermute | solution.py:281
  4.2 0.4 %plane.1 = f32[256,256]{1,0:T(8,128)S(1)} custom-call(f32[2,256,256]{2,1,0:T(8,128)S(1)} %get-tuple-element.30.mine, f32[2,256,256]{2,1,0:T(8,128)S(1)} %collective-permute-done.theirs.turned), custom_call_target="tpu_custom_call" | custom-call | tf_op jit(solution)/shard_map/plane/pallas_call | solution.py:66
  4.6 1.3 %collective-permute-start.1 = (f32[256,256]{1,0:T(8,128)S(1)}, f32[256,256]{1,0:T(8,128)S(1)}, u32[]{:S(2)}, u32[]{:S(2)}) collective-permute-start(f32[256,256]{1,0:T(8,128)S(1)} %plane.1), channel_id=1, source_target_pairs={{0,8},{1,9},{2,10},{3,11},{4,12},{5,13},{6,14},{7,15},{8,0},{9,1},... | collective-permute-start | bytes 786440 | tf_op jit(solution)/shard_map/ppermute | solution.py:281
  5.9 0.4 %chip.1 = f32[2,256,256]{2,1,0:T(8,128)S(1)} custom-call(f32[2,256,256]{2,1,0:T(8,128)S(1)} %get-tuple-element.30.mine, f32[2,256,256]{2,1,0:T(8,128)S(1)} %collective-permute-done.theirs.turned, f32[256,256]{1,0:T(8,128)S(1)} %plane.1), custom_call_target="tpu_custom_call" | custom-call | tf_op jit(solution)/shard_map/chip/pallas_call | solution.py:66
  6.3 5.9 %collective-permute-done.1.near = f32[256,256]{1,0:T(8,128)S(1)} collective-permute-done((f32[256,256]{1,0:T(8,128)S(1)}, f32[256,256]{1,0:T(8,128)S(1)}, u32[]{:S(2)}, u32[]{:S(2)}) %collective-permute-start.1) | collective-permute-done | bytes 262176 | tf_op jit(solution)/shard_map/ppermute | solution.py:281
  12.2 1.2 %collective-permute-start.2 = (f32[256,256]{1,0:T(8,128)S(1)}, f32[256,256]{1,0:T(8,128)S(1)}, u32[]{:S(2)}, u32[]{:S(2)}) collective-permute-start(f32[256,256]{1,0:T(8,128)S(1)} %collective-permute-done.1.near), channel_id=1, source_target_pairs={{0,4},{1,5},{2,6},{3,7},{4,0},{5,1},{6,2},{7,3},{8,12},{9,13},{10,... | collective-permute-start | bytes 786440 | tf_op jit(solution)/shard_map/ppermute | solution.py:281
  13.4 1.2 %collective-permute-done.2.far = f32[256,256]{1,0:T(8,128)S(1)} collective-permute-done((f32[256,256]{1,0:T(8,128)S(1)}, f32[256,256]{1,0:T(8,128)S(1)}, u32[]{:S(2)}, u32[]{:S(2)}) %collective-permute-start.2) | collective-permute-done | bytes 262176 | tf_op jit(solution)/shard_map/ppermute | solution.py:281
  14.6 0.7 %collective-permute-start.5 = (f32[2,64,256]{2,1,0:T(8,128)S(1)}, f32[2,64,256]{2,1,0:T(8,128)S(1)}, u32[]{:S(2)}, u32[]{:S(2)}) collective-permute-start(f32[2,64,256]{2,1,0:T(8,128)S(1)} %get-tuple-element.35), channel_id=1, source_target_pairs={{0,1},{1,0},{2,3},{3,2},{4,5},{5,4},{6,7},{7,6},{8,9},{9,8},{10,11... | collective-permute-start | bytes 393224 | tf_op jit(solution)/shard_map/ppermute | solution.py:281
  15.3 0.7 %collective-permute-start.3 = (f32[2,64,256]{2,1,0:T(8,128)S(1)}, f32[2,64,256]{2,1,0:T(8,128)S(1)}, u32[]{:S(2)}, u32[]{:S(2)}) collective-permute-start(f32[2,64,256]{2,1,0:T(8,128)S(1)} %get-tuple-element.33.own), channel_id=1, source_target_pairs={{0,1},{4,5},{8,9},{12,13},{16,17},{20,21},{24,25},{28,29}} | collective-permute-start | bytes 393224 | tf_op jit(solution)/shard_map/ppermute | solution.py:281
  16.0 0.0 copy-start.1
  16.0 3.3 %collective-permute-done.5.piece.near.one = f32[2,64,256]{2,1,0:T(8,128)S(1)} collective-permute-done((f32[2,64,256]{2,1,0:T(8,128)S(1)}, f32[2,64,256]{2,1,0:T(8,128)S(1)}, u32[]{:S(2)}, u32[]{:S(2)}) %collective-permute-start.5) | collective-permute-done | bytes 131104 | tf_op jit(solution)/shard_map/ppermute | solution.py:281
  19.3 0.5 %collective-permute-start.6 = (f32[2,64,256]{2,1,0:T(8,128)S(1)}, f32[2,64,256]{2,1,0:T(8,128)S(1)}, u32[]{:S(2)}, u32[]{:S(2)}) collective-permute-start(f32[2,64,256]{2,1,0:T(8,128)S(1)} %extend.1), channel_id=1, source_target_pairs={{0,1},{1,2},{2,3},{3,0},{4,5},{5,6},{6,7},{7,4},{8,9},{9,10},{10,1... | collective-permute-start | bytes 393224 | tf_op jit(solution)/shard_map/ppermute | solution.py:281
  19.7 0.0 collective-permute-done.3.piece.one
  19.8 1.3 %collective-permute-start.4 = (f32[2,64,256]{2,1,0:T(8,128)S(1)}, f32[2,64,256]{2,1,0:T(8,128)S(1)}, u32[]{:S(2)}, u32[]{:S(2)}) collective-permute-start(f32[2,64,256]{2,1,0:T(8,128)S(1)} %extend_other.1), channel_id=1, source_target_pairs={{1,3},{5,7},{9,11},{13,15},{17,19},{21,23},{25,27},{29,31}} | collective-permute-start | bytes 393224 | tf_op jit(solution)/shard_map/ppermute | solution.py:281
  21.0 0.7 %collective-permute-start.9 = (f32[2,64,256]{2,1,0:T(8,128)S(1)}, f32[2,64,256]{2,1,0:T(8,128)S(1)}, u32[]{:S(2)}, u32[]{:S(2)}) collective-permute-start(f32[2,64,256]{2,1,0:T(8,128)S(1)} %extend_other.1), channel_id=1, source_target_pairs={{1,2},{5,6},{9,10},{13,14},{17,18},{21,22},{25,26},{29,30}} | collective-permute-start | bytes 393224 | tf_op jit(solution)/shard_map/ppermute | solution.py:281
  21.7 1.4 %collective-permute-done.6.across.two = f32[2,64,256]{2,1,0:T(8,128)S(1)} collective-permute-done((f32[2,64,256]{2,1,0:T(8,128)S(1)}, f32[2,64,256]{2,1,0:T(8,128)S(1)}, u32[]{:S(2)}, u32[]{:S(2)}) %collective-permute-start.6) | collective-permute-done | bytes 131104 | tf_op jit(solution)/shard_map/ppermute | solution.py:281
  23.1 1.3 %collective-permute-start.10 = (f32[2,64,256]{2,1,0:T(8,128)S(1)}, f32[2,64,256]{2,1,0:T(8,128)S(1)}, u32[]{:S(2)}, u32[]{:S(2)}) collective-permute-start(f32[2,64,256]{2,1,0:T(8,128)S(1)} %collective-permute-done.6.across.two), channel_id=1, source_target_pairs={{2,3},{6,7},{10,11},{14,15},{18,19},{22,23},{26,27},{30,31}} | collective-permute-start | bytes 393224 | tf_op jit(solution)/shard_map/ppermute | solution.py:281
  24.4 2.4 %collective-permute-start.7 = (f32[2,64,256]{2,1,0:T(8,128)S(1)}, f32[2,64,256]{2,1,0:T(8,128)S(1)}, u32[]{:S(2)}, u32[]{:S(2)}) collective-permute-start(f32[2,64,256]{2,1,0:T(8,128)S(1)} %collective-permute-done.5.piece.near.one), channel_id=1, source_target_pairs={{0,4},{1,5},{2,6},{3,7},{4,0},{5,1},{6,2},{7,3},{8,12},{9,13},{10,... | collective-permute-start | bytes 393224 | tf_op jit(solution)/shard_map/ppermute | solution.py:281
  26.8 0.1 collective-permute-start.8
  26.9 0.0 copy-done.1
  26.9 1.6 %before.1 = (f32[2,2,256,256]{3,2,1,0:T(8,128)S(1)}, bf16[2,2,256,256]{3,2,1,0:T(8,128)(2,1)S(1)}, bf16[2,2,256,256]{3,2,1,0:T(8,128)(2,1)S(1)}) custom-call(f32[1,1,2,2,256,256]{5,4,3,2,1,0:T(8,128)S(1)} %copy-done.1, f32[2,256,256]{2,1,0:T(8,128)S(1)} %get-tuple-element.34.block, f32[2,256,256]{2,1,0:T(8,128)S(1)} %collective-permute-done.theirs.turned, ...), custom_call_target="tpu_custom_call" | custom-call | tf_op jit(solution)/shard_map/before/pallas_call | solution.py:66
  28.5 0.0 collective-permute-done.4.three
  28.5 0.6 %left.1 = (bf16[2,2,256,128]{3,2,1,0:T(8,128)(2,1)S(1)}, bf16[2,2,256,128]{3,2,1,0:T(8,128)(2,1)S(1)}) custom-call(bf16[2,2,256,256]{3,2,1,0:T(8,128)(2,1)S(1)} %get-tuple-element.39.before_high, bf16[2,2,256,256]{3,2,1,0:T(8,128)(2,1)S(1)} %get-tuple-element.40.before_low, f32[2,64,256]{2,1,0:T(8,128)S(1)} %collective-permute-done.5.piece.near.one, ...), custom_call_target="tpu_custom_call" | custom-call | tf_op jit(solution)/shard_map/left/pallas_call | solution.py:66
  29.2 1.8 %collective-permute-start.11 = (f32[2,64,256]{2,1,0:T(8,128)S(1)}, f32[2,64,256]{2,1,0:T(8,128)S(1)}, u32[]{:S(2)}, u32[]{:S(2)}) collective-permute-start(f32[2,64,256]{2,1,0:T(8,128)S(1)} %merge_early.1.early), channel_id=1, source_target_pairs={{0,4},{1,5},{2,6},{3,7},{4,0},{5,1},{6,2},{7,3},{8,12},{9,13},{10,... | collective-permute-start | bytes 393224 | tf_op jit(solution)/shard_map/ppermute | solution.py:281
  31.0 0.0 collective-permute-done.9.two.three
  31.0 0.0 collective-permute-done.10.three
  31.0 1.4 %collective-permute-start.12 = (f32[2,64,256]{2,1,0:T(8,128)S(1)}, f32[2,64,256]{2,1,0:T(8,128)S(1)}, u32[]{:S(2)}, u32[]{:S(2)}) collective-permute-start(f32[2,64,256]{2,1,0:T(8,128)S(1)} %merge_late.1.late), channel_id=1, source_target_pairs={{0,4},{1,5},{2,6},{3,7},{4,0},{5,1},{6,2},{7,3},{8,12},{9,13},{10,... | collective-permute-start | bytes 393224 | tf_op jit(solution)/shard_map/ppermute | solution.py:281
  32.4 0.0 collective-permute-done.7.far_own
  32.4 0.0 collective-permute-done.8.far_past
  32.4 1.2 %near.1 = (f32[2,2,256,128]{3,2,1,0:T(8,128)S(1)}, bf16[2,2,256,256]{3,2,1,0:T(8,128)(2,1)S(1)}, bf16[2,2,256,256]{3,2,1,0:T(8,128)(2,1)S(1)}) custom-call(bf16[2,2,256,256]{3,2,1,0:T(8,128)(2,1)S(1)} %get-tuple-element.39.before_high, bf16[2,2,256,256]{3,2,1,0:T(8,128)(2,1)S(1)} %get-tuple-element.40.before_low, ...), custom_call_target="tpu_custom_call" | custom-call | tf_op jit(solution)/shard_map/near/pallas_call | solution.py:66
  33.7 0.0 collective-permute-done.11.early
  33.7 0.0 collective-permute-done.12.late
  33.7 1.4 %far.1 = f32[1,1,2,2,256,256]{5,4,3,2,1,0:T(8,128)} custom-call(f32[2,2,256,256]{3,2,1,0:T(8,128)S(1)} %get-tuple-element.38.before, f32[2,2,256,128]{3,2,1,0:T(8,128)S(1)} %get-tuple-element.52.near, bf16[2,2,256,256]{3,2,1,0:T(8,128)(2,1)S(1)} %get-tuple-element.53.high, bf16[2,2,256,256]{3,2,1,0:T(8,128)(2,1)S(1)} %get-tuple-element.54.low, ...), custom_call_target="tpu_custom_call" | custom-call | tf_op jit(solution)/shard_map/far/pallas_call | solution.py:66
  (7 shorter events, 0.1 us)
Async XLA Ops:
  0.0 1.2 %copy-start = (f32[1,1,2,2,256,256]{5,4,3,2,1,0:T(8,128)S(1)}, f32[1,1,2,2,256,256]{5,4,3,2,1,0:T(8,128)}, u32[]{:S(2)}) copy-start(f32[1,1,2,2,256,256]{5,4,3,2,1,0:T(8,128)} %u.3) | copy-start | bytes 3145732
  1.9 2.3 %collective-permute-start = (f32[2,256,256]{2,1,0:T(8,128)S(1)}, f32[2,256,256]{2,1,0:T(8,128)S(1)}, u32[]{:S(2)}, u32[]{:S(2)}) collective-permute-start(f32[2,256,256]{2,1,0:T(8,128)S(1)} %get-tuple-element.30.mine), channel_id=1, source_target_pairs={{0,4},{1,5},{2,6},{3,7},{4,0},{5,1},{6,2},{7,3},{8,12},{9,13},{10,... | collective-permute-start | bytes 1572872 | tf_op jit(solution)/shard_map/ppermute | solution.py:281
  4.6 7.6 %collective-permute-start.1 = (f32[256,256]{1,0:T(8,128)S(1)}, f32[256,256]{1,0:T(8,128)S(1)}, u32[]{:S(2)}, u32[]{:S(2)}) collective-permute-start(f32[256,256]{1,0:T(8,128)S(1)} %plane.1), channel_id=1, source_target_pairs={{0,8},{1,9},{2,10},{3,11},{4,12},{5,13},{6,14},{7,15},{8,0},{9,1},... | collective-permute-start | bytes 786440 | tf_op jit(solution)/shard_map/ppermute | solution.py:281
  12.2 2.4 %collective-permute-start.2 = (f32[256,256]{1,0:T(8,128)S(1)}, f32[256,256]{1,0:T(8,128)S(1)}, u32[]{:S(2)}, u32[]{:S(2)}) collective-permute-start(f32[256,256]{1,0:T(8,128)S(1)} %collective-permute-done.1.near), channel_id=1, source_target_pairs={{0,4},{1,5},{2,6},{3,7},{4,0},{5,1},{6,2},{7,3},{8,12},{9,13},{10,... | collective-permute-start | bytes 786440 | tf_op jit(solution)/shard_map/ppermute | solution.py:281
  14.6 4.7 %collective-permute-start.5 = (f32[2,64,256]{2,1,0:T(8,128)S(1)}, f32[2,64,256]{2,1,0:T(8,128)S(1)}, u32[]{:S(2)}, u32[]{:S(2)}) collective-permute-start(f32[2,64,256]{2,1,0:T(8,128)S(1)} %get-tuple-element.35), channel_id=1, source_target_pairs={{0,1},{1,0},{2,3},{3,2},{4,5},{5,4},{6,7},{7,6},{8,9},{9,8},{10,11... | collective-permute-start | bytes 393224 | tf_op jit(solution)/shard_map/ppermute | solution.py:281
  15.3 4.5 %collective-permute-start.3 = (f32[2,64,256]{2,1,0:T(8,128)S(1)}, f32[2,64,256]{2,1,0:T(8,128)S(1)}, u32[]{:S(2)}, u32[]{:S(2)}) collective-permute-start(f32[2,64,256]{2,1,0:T(8,128)S(1)} %get-tuple-element.33.own), channel_id=1, source_target_pairs={{0,1},{4,5},{8,9},{12,13},{16,17},{20,21},{24,25},{28,29}} | collective-permute-start | bytes 393224 | tf_op jit(solution)/shard_map/ppermute | solution.py:281
  16.0 10.9 %copy-start.1 = (f32[1,1,2,2,256,256]{5,4,3,2,1,0:T(8,128)S(1)}, f32[1,1,2,2,256,256]{5,4,3,2,1,0:T(8,128)}, u32[]{:S(2)}) copy-start(f32[1,1,2,2,256,256]{5,4,3,2,1,0:T(8,128)} %u.3) | copy-start | bytes 3145732
  19.3 3.8 %collective-permute-start.6 = (f32[2,64,256]{2,1,0:T(8,128)S(1)}, f32[2,64,256]{2,1,0:T(8,128)S(1)}, u32[]{:S(2)}, u32[]{:S(2)}) collective-permute-start(f32[2,64,256]{2,1,0:T(8,128)S(1)} %extend.1), channel_id=1, source_target_pairs={{0,1},{1,2},{2,3},{3,0},{4,5},{5,6},{6,7},{7,4},{8,9},{9,10},{10,1... | collective-permute-start | bytes 393224 | tf_op jit(solution)/shard_map/ppermute | solution.py:281
  19.8 8.8 %collective-permute-start.4 = (f32[2,64,256]{2,1,0:T(8,128)S(1)}, f32[2,64,256]{2,1,0:T(8,128)S(1)}, u32[]{:S(2)}, u32[]{:S(2)}) collective-permute-start(f32[2,64,256]{2,1,0:T(8,128)S(1)} %extend_other.1), channel_id=1, source_target_pairs={{1,3},{5,7},{9,11},{13,15},{17,19},{21,23},{25,27},{29,31}} | collective-permute-start | bytes 393224 | tf_op jit(solution)/shard_map/ppermute | solution.py:281
  21.0 9.9 %collective-permute-start.9 = (f32[2,64,256]{2,1,0:T(8,128)S(1)}, f32[2,64,256]{2,1,0:T(8,128)S(1)}, u32[]{:S(2)}, u32[]{:S(2)}) collective-permute-start(f32[2,64,256]{2,1,0:T(8,128)S(1)} %extend_other.1), channel_id=1, source_target_pairs={{1,2},{5,6},{9,10},{13,14},{17,18},{21,22},{25,26},{29,30}} | collective-permute-start | bytes 393224 | tf_op jit(solution)/shard_map/ppermute | solution.py:281
  23.1 7.9 %collective-permute-start.10 = (f32[2,64,256]{2,1,0:T(8,128)S(1)}, f32[2,64,256]{2,1,0:T(8,128)S(1)}, u32[]{:S(2)}, u32[]{:S(2)}) collective-permute-start(f32[2,64,256]{2,1,0:T(8,128)S(1)} %collective-permute-done.6.across.two), channel_id=1, source_target_pairs={{2,3},{6,7},{10,11},{14,15},{18,19},{22,23},{26,27},{30,31}} | collective-permute-start | bytes 393224 | tf_op jit(solution)/shard_map/ppermute | solution.py:281
  24.4 8.0 %collective-permute-start.7 = (f32[2,64,256]{2,1,0:T(8,128)S(1)}, f32[2,64,256]{2,1,0:T(8,128)S(1)}, u32[]{:S(2)}, u32[]{:S(2)}) collective-permute-start(f32[2,64,256]{2,1,0:T(8,128)S(1)} %collective-permute-done.5.piece.near.one), channel_id=1, source_target_pairs={{0,4},{1,5},{2,6},{3,7},{4,0},{5,1},{6,2},{7,3},{8,12},{9,13},{10,... | collective-permute-start | bytes 393224 | tf_op jit(solution)/shard_map/ppermute | solution.py:281
  26.8 5.6 %collective-permute-start.8 = (f32[2,64,256]{2,1,0:T(8,128)S(1)}, f32[2,64,256]{2,1,0:T(8,128)S(1)}, u32[]{:S(2)}, u32[]{:S(2)}) collective-permute-start(f32[2,64,256]{2,1,0:T(8,128)S(1)} %collective-permute-done.6.across.two), channel_id=1, source_target_pairs={{0,4},{1,5},{2,6},{3,7},{4,0},{5,1},{6,2},{7,3},{8,12},{9,13},{10,... | collective-permute-start | bytes 393224 | tf_op jit(solution)/shard_map/ppermute | solution.py:281
  29.2 4.5 %collective-permute-start.11 = (f32[2,64,256]{2,1,0:T(8,128)S(1)}, f32[2,64,256]{2,1,0:T(8,128)S(1)}, u32[]{:S(2)}, u32[]{:S(2)}) collective-permute-start(f32[2,64,256]{2,1,0:T(8,128)S(1)} %merge_early.1.early), channel_id=1, source_target_pairs={{0,4},{1,5},{2,6},{3,7},{4,0},{5,1},{6,2},{7,3},{8,12},{9,13},{10,... | collective-permute-start | bytes 393224 | tf_op jit(solution)/shard_map/ppermute | solution.py:281
  31.0 2.6 %collective-permute-start.12 = (f32[2,64,256]{2,1,0:T(8,128)S(1)}, f32[2,64,256]{2,1,0:T(8,128)S(1)}, u32[]{:S(2)}, u32[]{:S(2)}) collective-permute-start(f32[2,64,256]{2,1,0:T(8,128)S(1)} %merge_late.1.late), channel_id=1, source_target_pairs={{0,4},{1,5},{2,6},{3,7},{4,0},{5,1},{6,2},{7,3},{8,12},{9,13},{10,... | collective-permute-start | bytes 393224 | tf_op jit(solution)/shard_map/ppermute | solution.py:281

commit v9 on v8

--- a/solution.py
+++ b/solution.py
@@ -160,7 +160,7 @@
 
 
 def half(x, near, across):
-    near, across = pair(near), pair(across)
+    near, across = (tuple(p[...] for p in s) if isinstance(s, tuple) else pair(s) for s in (near, across))
     return stack(pick(x == 0, near, across), pick(x == 0, across, near))
 
 
@@ -205,6 +205,14 @@
     left_half((before_high, before_low), near, across, k, high, low)
 
 
+def planes_kernel(one, two, *outs):
+    rows = jnp.concatenate([one[0], one[1], two[0], two[1]], axis=0)
+    start = 0
+    for out in outs:
+        out[...] = rows[start : start + out.shape[0]]
+        start += out.shape[0]
+
+
 def merge_kernel(one, two, three, out):
     _, _, w = place()
     out[...] = jnp.where(w == 1, one[...], jnp.where(w == 2, two[...], three[...]))
@@ -229,11 +237,16 @@
     return {(slot, index): plane(slot, index) for slot in range(2) for index in range(2)}
 
 
-def near_kernel(
-    before_high, before_low, far_own, far_past, high, low, early, late, out, whole_high, whole_low, far_high, far_low
-):
+def left_far_kernel(before_high, before_low, *refs):
+    _, k, _ = place()
+    *pieces, high, low = refs
+    rows = jnp.concatenate([piece[...] for piece in pieces], axis=0)
+    a, b, c, d = (rows[i * rows.shape[0] // 4 : (i + 1) * rows.shape[0] // 4] for i in range(4))
+    left_half((before_high, before_low), (a, b), (c, d), 1 - k, high, low)
+
+
+def near_kernel(high, low, far_high, far_low, early, late, out, whole_high, whole_low):
     x, k, w = place()
-    left_half((before_high, before_low), far_own, far_past, 1 - k, far_high, far_low)
 
     @pl.when(w != 0)
     def _():
@@ -312,14 +325,17 @@
     two = permute(both, onward)
     (both_other,) = call(extend_kernel, [strip], one_other, window, other, name="extend_other")
     three_other = permute(both_other, one_three)
+    far_chip, _ = tie((far_chip, both_other))
+    both = jax.ShapeDtypeStruct((2, *full), jnp.bfloat16)
+    operands = unitaries, block, turned_other, near_chip, far_chip
+    before, *before_parts = call(before_kernel, [(2, *full), both, both], *operands, name="before")
+    two, before = tie((two, before))
     three = permute(two, two_three)
     two_other = permute(both_other, one_two)
     own, past = tie((one, two))
-    far_own, far_past = permute(own, cores), permute(past, cores)
-    far_chip, _ = tie((far_chip, two))
-    both = jax.ShapeDtypeStruct((2, *full), jnp.bfloat16)
-    operands = unitaries, block, turned_other, near_chip, far_chip
-    before, *before_parts = call(before_kernel, [(2, *full), both, both], *operands, name="before")
+    thirds = [(3 * width // 8, width)] + [(5 * width // 16, width)] * 2
+    planes = call(planes_kernel, thirds, own, past, name="planes")
+    far_strips = [permute(plane, cores) for plane in planes]
     three_other, before = tie((three_other, before))
     parts = [jax.ShapeDtypeStruct((2, 2, width, width // 2), jnp.bfloat16)] * 2
     high, low = call(left_kernel, parts, *before_parts, own, past, name="left")
@@ -328,13 +344,13 @@
     far_early = permute(early, cores)
     two_other, early = tie((two_other, early))
     (other,) = call(merge_kernel, [strip], one_other, two_other, two_other, name="merge_other")
-    three, other = tie((three, other))
+    far_high, far_low = call(left_far_kernel, parts, *before_parts, *far_strips, name="left_far")
+    three, other, far_high = tie((three, other, far_high))
     (late,) = call(merge_kernel, [strip], other, other, three, name="merge_late")
     far_late = permute(late, cores)
     half_width = (2, 2, width, width // 2)
-    operands = *before_parts, far_own, far_past, high, low, early, late
-    scratch = [pltpu.VMEM(half_width, jnp.bfloat16)] * 2
-    near, high, low = call(near_kernel, [half_width, both, both], *operands, name="near", scratch=scratch)
+    operands = high, low, far_high, far_low, early, late
+    near, high, low = call(near_kernel, [half_width, both, both], *operands, name="near")
     scratch = pltpu.VMEM(half_width, F32), pltpu.SemaphoreType.DMA((2, 2))
     operands = before, near, high, low, far_early, far_late
     (out,) = call(far_kernel, [unitaries.shape], *operands, name="far", scratch=scratch, hbm_out=True)

time: 35.3 us -> 35 us (level)
  waiting for transfers between devices: 13.3 us -> 12.4 us
  starting transfers between devices: 13.9 us -> 14.4 us
    ppermute x13 -> x14, waiting for transfers between devices: 13.3 us -> 12.4 us  [permute(): return lax.ppermute(value, AXES, flat)]
    ppermute x13 -> x14, starting transfers between devices: 13.9 us -> 14.4 us  [permute(): return lax.ppermute(value, AXES, flat)]
    pallas_call x14 -> x16, Pallas kernels: 6.51 us -> 6.5 us  [call(): pl.pallas_call(body, out_shape=shapes, in_specs=[far if i == alias else w...]
  transfers between devices with their start and end apart: 13 -> 14, of which waited for: 5 -> 6; matrix products, arithmetic and copies ran while one was open for 0% -> 0% of each run, Pallas kernels for 11% -> 11%
where the time goes in v9:
time: 35 us; the launch traced here: 34.8 us
  starting transfers between devices  14.4 us (41%)
  waiting for transfers between devices  12.4 us (35%)
  Pallas kernels  6.5 us (19%)
  local copies, waits for them, and re-layouts  1.23 us (4%)
    ppermute x14, starting transfers between devices, permute(): return lax.ppermute(value, AXES, flat)  14.4 us
    ppermute x14, waiting for transfers between devices, permute(): return lax.ppermute(value, AXES, flat)  12.4 us
    pallas_call x16, Pallas kernels, call(): pl.pallas_call(body, out_shape=shapes, in_specs=[far if i == alias else w...  6.5 us
    unnamed x4, local copies, waits for them, and re-layouts  1.23 us
  transfers between devices with their start and end apart: 14, of which 6 were waited for; matrix products, arithmetic and copies ran while one was open for 0% of the time, Pallas kernels for 11%

profile of v9, /device:TPU:29, one launch (start us, length us, event | category | flops | bytes accessed | tf_op | source)
XLA Modules:
  0.0 34.8 jit_solution(3458732308089194165)
XLA Ops:
  0.0 0.0 copy-start
  0.0 1.2 %copy-done = f32[1,1,2,2,256,256]{5,4,3,2,1,0:T(8,128)S(1)} copy-done((f32[1,1,2,2,256,256]{5,4,3,2,1,0:T(8,128)S(1)}, f32[1,1,2,2,256,256]{5,4,3,2,1,0:T(8,128)}, u32[]{:S(2)}) %copy-start) | copy-done | bytes 1048600
  1.2 0.7 %block.1 = (f32[2,256,256]{2,1,0:T(8,128)S(1)}, f32[2,256,256]{2,1,0:T(8,128)S(1)}) custom-call(f32[1,1,2,2,256,256]{5,4,3,2,1,0:T(8,128)S(1)} %copy-done), custom_call_target="tpu_custom_call" | custom-call | tf_op jit(solution)/shard_map/block/pallas_call | solution.py:66
  1.9 0.7 %collective-permute-start = (f32[2,256,256]{2,1,0:T(8,128)S(1)}, f32[2,256,256]{2,1,0:T(8,128)S(1)}, u32[]{:S(2)}, u32[]{:S(2)}) collective-permute-start(f32[2,256,256]{2,1,0:T(8,128)S(1)} %get-tuple-element.38.mine), channel_id=1, source_target_pairs={{0,4},{1,5},{2,6},{3,7},{4,0},{5,1},{6,2},{7,3},{8,12},{9,13},{10,... | collective-permute-start | bytes 1572872 | tf_op jit(solution)/shard_map/ppermute | solution.py:294
  2.7 1.5 %collective-permute-done.theirs.turned = f32[2,256,256]{2,1,0:T(8,128)S(1)} collective-permute-done((f32[2,256,256]{2,1,0:T(8,128)S(1)}, f32[2,256,256]{2,1,0:T(8,128)S(1)}, u32[]{:S(2)}, u32[]{:S(2)}) %collective-permute-start) | collective-permute-done | bytes 524320 | tf_op jit(solution)/shard_map/ppermute | solution.py:294
  4.2 0.4 %plane.1 = f32[256,256]{1,0:T(8,128)S(1)} custom-call(f32[2,256,256]{2,1,0:T(8,128)S(1)} %get-tuple-element.38.mine, f32[2,256,256]{2,1,0:T(8,128)S(1)} %collective-permute-done.theirs.turned), custom_call_target="tpu_custom_call" | custom-call | tf_op jit(solution)/shard_map/plane/pallas_call | solution.py:66
  4.6 1.3 %collective-permute-start.1 = (f32[256,256]{1,0:T(8,128)S(1)}, f32[256,256]{1,0:T(8,128)S(1)}, u32[]{:S(2)}, u32[]{:S(2)}) collective-permute-start(f32[256,256]{1,0:T(8,128)S(1)} %plane.1), channel_id=1, source_target_pairs={{0,8},{1,9},{2,10},{3,11},{4,12},{5,13},{6,14},{7,15},{8,0},{9,1},... | collective-permute-start | bytes 786440 | tf_op jit(solution)/shard_map/ppermute | solution.py:294
  5.9 0.4 %chip.1 = f32[2,256,256]{2,1,0:T(8,128)S(1)} custom-call(f32[2,256,256]{2,1,0:T(8,128)S(1)} %get-tuple-element.38.mine, f32[2,256,256]{2,1,0:T(8,128)S(1)} %collective-permute-done.theirs.turned, f32[256,256]{1,0:T(8,128)S(1)} %plane.1), custom_call_target="tpu_custom_call" | custom-call | tf_op jit(solution)/shard_map/chip/pallas_call | solution.py:66
  6.3 5.9 %collective-permute-done.1.near = f32[256,256]{1,0:T(8,128)S(1)} collective-permute-done((f32[256,256]{1,0:T(8,128)S(1)}, f32[256,256]{1,0:T(8,128)S(1)}, u32[]{:S(2)}, u32[]{:S(2)}) %collective-permute-start.1) | collective-permute-done | bytes 262176 | tf_op jit(solution)/shard_map/ppermute | solution.py:294
  12.2 1.2 %collective-permute-start.2 = (f32[256,256]{1,0:T(8,128)S(1)}, f32[256,256]{1,0:T(8,128)S(1)}, u32[]{:S(2)}, u32[]{:S(2)}) collective-permute-start(f32[256,256]{1,0:T(8,128)S(1)} %collective-permute-done.1.near), channel_id=1, source_target_pairs={{0,4},{1,5},{2,6},{3,7},{4,0},{5,1},{6,2},{7,3},{8,12},{9,13},{10,... | collective-permute-start | bytes 786440 | tf_op jit(solution)/shard_map/ppermute | solution.py:294
  13.4 1.2 %collective-permute-done.2.far = f32[256,256]{1,0:T(8,128)S(1)} collective-permute-done((f32[256,256]{1,0:T(8,128)S(1)}, f32[256,256]{1,0:T(8,128)S(1)}, u32[]{:S(2)}, u32[]{:S(2)}) %collective-permute-start.2) | collective-permute-done | bytes 262176 | tf_op jit(solution)/shard_map/ppermute | solution.py:294
  14.6 0.7 %collective-permute-start.5 = (f32[2,64,256]{2,1,0:T(8,128)S(1)}, f32[2,64,256]{2,1,0:T(8,128)S(1)}, u32[]{:S(2)}, u32[]{:S(2)}) collective-permute-start(f32[2,64,256]{2,1,0:T(8,128)S(1)} %get-tuple-element.42), channel_id=1, source_target_pairs={{0,1},{1,0},{2,3},{3,2},{4,5},{5,4},{6,7},{7,6},{8,9},{9,8},{10,11... | collective-permute-start | bytes 393224 | tf_op jit(solution)/shard_map/ppermute | solution.py:294
  15.3 0.7 %collective-permute-start.3 = (f32[2,64,256]{2,1,0:T(8,128)S(1)}, f32[2,64,256]{2,1,0:T(8,128)S(1)}, u32[]{:S(2)}, u32[]{:S(2)}) collective-permute-start(f32[2,64,256]{2,1,0:T(8,128)S(1)} %get-tuple-element.41.own), channel_id=1, source_target_pairs={{0,1},{4,5},{8,9},{12,13},{16,17},{20,21},{24,25},{28,29}} | collective-permute-start | bytes 393224 | tf_op jit(solution)/shard_map/ppermute | solution.py:294
  16.0 0.0 copy-start.1
  16.0 3.3 %collective-permute-done.5.piece.near.one = f32[2,64,256]{2,1,0:T(8,128)S(1)} collective-permute-done((f32[2,64,256]{2,1,0:T(8,128)S(1)}, f32[2,64,256]{2,1,0:T(8,128)S(1)}, u32[]{:S(2)}, u32[]{:S(2)}) %collective-permute-start.5) | collective-permute-done | bytes 131104 | tf_op jit(solution)/shard_map/ppermute | solution.py:294
  19.3 0.5 %collective-permute-start.6 = (f32[2,64,256]{2,1,0:T(8,128)S(1)}, f32[2,64,256]{2,1,0:T(8,128)S(1)}, u32[]{:S(2)}, u32[]{:S(2)}) collective-permute-start(f32[2,64,256]{2,1,0:T(8,128)S(1)} %extend.1), channel_id=1, source_target_pairs={{0,1},{1,2},{2,3},{3,0},{4,5},{5,6},{6,7},{7,4},{8,9},{9,10},{10,1... | collective-permute-start | bytes 393224 | tf_op jit(solution)/shard_map/ppermute | solution.py:294
  19.7 0.0 collective-permute-done.3.piece.one
  19.8 1.3 %collective-permute-start.4 = (f32[2,64,256]{2,1,0:T(8,128)S(1)}, f32[2,64,256]{2,1,0:T(8,128)S(1)}, u32[]{:S(2)}, u32[]{:S(2)}) collective-permute-start(f32[2,64,256]{2,1,0:T(8,128)S(1)} %extend_other.1), channel_id=1, source_target_pairs={{1,3},{5,7},{9,11},{13,15},{17,19},{21,23},{25,27},{29,31}} | collective-permute-start | bytes 393224 | tf_op jit(solution)/shard_map/ppermute | solution.py:294
  21.0 0.7 %collective-permute-start.8 = (f32[2,64,256]{2,1,0:T(8,128)S(1)}, f32[2,64,256]{2,1,0:T(8,128)S(1)}, u32[]{:S(2)}, u32[]{:S(2)}) collective-permute-start(f32[2,64,256]{2,1,0:T(8,128)S(1)} %extend_other.1), channel_id=1, source_target_pairs={{1,2},{5,6},{9,10},{13,14},{17,18},{21,22},{25,26},{29,30}} | collective-permute-start | bytes 393224 | tf_op jit(solution)/shard_map/ppermute | solution.py:294
  21.7 0.0 copy-done.1
  21.7 1.6 %before.1 = (f32[2,2,256,256]{3,2,1,0:T(8,128)S(1)}, bf16[2,2,256,256]{3,2,1,0:T(8,128)(2,1)S(1)}, bf16[2,2,256,256]{3,2,1,0:T(8,128)(2,1)S(1)}) custom-call(f32[1,1,2,2,256,256]{5,4,3,2,1,0:T(8,128)S(1)} %copy-done.1, f32[2,256,256]{2,1,0:T(8,128)S(1)} %get-tuple-element.43.block, f32[2,256,256]{2,1,0:T(8,128)S(1)} %collective-permute-done.theirs.turned, ...), custom_call_target="tpu_custom_call" | custom-call | tf_op jit(solution)/shard_map/before/pallas_call | solution.py:66
  23.3 0.0 collective-permute-done.6.across.two
  23.4 1.3 %collective-permute-start.7 = (f32[2,64,256]{2,1,0:T(8,128)S(1)}, f32[2,64,256]{2,1,0:T(8,128)S(1)}, u32[]{:S(2)}, u32[]{:S(2)}) collective-permute-start(f32[2,64,256]{2,1,0:T(8,128)S(1)} %collective-permute-done.6.across.two), channel_id=1, source_target_pairs={{2,3},{6,7},{10,11},{14,15},{18,19},{22,23},{26,27},{30,31}} | collective-permute-start | bytes 393224 | tf_op jit(solution)/shard_map/ppermute | solution.py:294
  24.7 2.2 %collective-permute-start.9 = (f32[96,256]{1,0:T(8,128)S(1)}, f32[96,256]{1,0:T(8,128)S(1)}, u32[]{:S(2)}, u32[]{:S(2)}) collective-permute-start(f32[96,256]{1,0:T(8,128)S(1)} %get-tuple-element.59), channel_id=1, source_target_pairs={{0,4},{1,5},{2,6},{3,7},{4,0},{5,1},{6,2},{7,3},{8,12},{9,13},{10,... | collective-permute-start | bytes 294920 | tf_op jit(solution)/shard_map/ppermute | solution.py:294
  26.8 0.1 collective-permute-start.10
  26.9 0.0 collective-permute-done.4.three
  26.9 3.3 %collective-permute-start.11 = (f32[80,256]{1,0:T(8,128)S(1)}, f32[80,256]{1,0:T(8,128)S(1)}, u32[]{:S(2)}, u32[]{:S(2)}) collective-permute-start(f32[80,256]{1,0:T(8,128)S(1)} %get-tuple-element.61), channel_id=1, source_target_pairs={{0,4},{1,5},{2,6},{3,7},{4,0},{5,1},{6,2},{7,3},{8,12},{9,13},{10,... | collective-permute-start | bytes 245768 | tf_op jit(solution)/shard_map/ppermute | solution.py:294
  30.3 0.6 %left.1 = (bf16[2,2,256,128]{3,2,1,0:T(8,128)(2,1)S(1)}, bf16[2,2,256,128]{3,2,1,0:T(8,128)(2,1)S(1)}) custom-call(bf16[2,2,256,256]{3,2,1,0:T(8,128)(2,1)S(1)} %get-tuple-element.49.before_high, bf16[2,2,256,256]{3,2,1,0:T(8,128)(2,1)S(1)} %get-tuple-element.50.before_low, f32[2,64,256]{2,1,0:T(8,128)S(1)} %collective-permute-done.5.piece.near.one, ...), custom_call_target="tpu_custom_call" | custom-call | tf_op jit(solution)/shard_map/left/pallas_call | solution.py:66
  30.9 0.0 collective-permute-done.8.two.three
  30.9 0.1 collective-permute-start.12
  31.0 0.0 collective-permute-done.10.refs_1_
  31.0 0.1 collective-permute-done.11.refs_2_
  31.2 0.0 collective-permute-done.9.refs_0_
  31.2 0.6 %left_far.1 = (bf16[2,2,256,128]{3,2,1,0:T(8,128)(2,1)S(1)}, bf16[2,2,256,128]{3,2,1,0:T(8,128)(2,1)S(1)}) custom-call(bf16[2,2,256,256]{3,2,1,0:T(8,128)(2,1)S(1)} %get-tuple-element.49.before_high, bf16[2,2,256,256]{3,2,1,0:T(8,128)(2,1)S(1)} %get-tuple-element.50.before_low, f32[96,256]{1,0:T(8,128)S(1)} %collective-permute-done.9.refs_0_, ...), custom_call_target="tpu_custom_call" | custom-call | tf_op jit(solution)/shard_map/left_far/pallas_call | solution.py:66
  31.8 0.0 collective-permute-done.7.three
  31.9 0.5 %collective-permute-start.13 = (f32[2,64,256]{2,1,0:T(8,128)S(1)}, f32[2,64,256]{2,1,0:T(8,128)S(1)}, u32[]{:S(2)}, u32[]{:S(2)}) collective-permute-start(f32[2,64,256]{2,1,0:T(8,128)S(1)} %merge_late.1.late), channel_id=1, source_target_pairs={{0,4},{1,5},{2,6},{3,7},{4,0},{5,1},{6,2},{7,3},{8,12},{9,13},{10,... | collective-permute-start | bytes 393224 | tf_op jit(solution)/shard_map/ppermute | solution.py:294
  32.4 0.6 %near.1 = (f32[2,2,256,128]{3,2,1,0:T(8,128)S(1)}, bf16[2,2,256,256]{3,2,1,0:T(8,128)(2,1)S(1)}, bf16[2,2,256,256]{3,2,1,0:T(8,128)(2,1)S(1)}) custom-call(bf16[2,2,256,128]{3,2,1,0:T(8,128)(2,1)S(1)} %get-tuple-element.55.high, bf16[2,2,256,128]{3,2,1,0:T(8,128)(2,1)S(1)} %get-tuple-element.56.low, bf16[2,2,256,128]{3,2,1,0:T(8,128)(2,1)S(1)} %get-tuple-element.63.far_high, ...), custom_call_target="tpu_custom_call" | custom-call | tf_op jit(solution)/shard_map/near/pallas_call | solution.py:66
  33.0 0.0 collective-permute-done.12.early
  33.0 0.3 collective-permute-done.13.late
  33.4 1.4 %far.1 = f32[1,1,2,2,256,256]{5,4,3,2,1,0:T(8,128)} custom-call(f32[2,2,256,256]{3,2,1,0:T(8,128)S(1)} %get-tuple-element.47.before, f32[2,2,256,128]{3,2,1,0:T(8,128)S(1)} %get-tuple-element.68.near, bf16[2,2,256,256]{3,2,1,0:T(8,128)(2,1)S(1)} %get-tuple-element.69.high, bf16[2,2,256,256]{3,2,1,0:T(8,128)(2,1)S(1)} %get-tuple-element.70.low, ...), custom_call_target="tpu_custom_call" | custom-call | tf_op jit(solution)/shard_map/far/pallas_call | solution.py:66
  (8 shorter events, 0.1 us)
Async XLA Ops:
  0.0 1.2 %copy-start = (f32[1,1,2,2,256,256]{5,4,3,2,1,0:T(8,128)S(1)}, f32[1,1,2,2,256,256]{5,4,3,2,1,0:T(8,128)}, u32[]{:S(2)}) copy-start(f32[1,1,2,2,256,256]{5,4,3,2,1,0:T(8,128)} %u.3) | copy-start | bytes 3145732
  1.9 2.3 %collective-permute-start = (f32[2,256,256]{2,1,0:T(8,128)S(1)}, f32[2,256,256]{2,1,0:T(8,128)S(1)}, u32[]{:S(2)}, u32[]{:S(2)}) collective-permute-start(f32[2,256,256]{2,1,0:T(8,128)S(1)} %get-tuple-element.38.mine), channel_id=1, source_target_pairs={{0,4},{1,5},{2,6},{3,7},{4,0},{5,1},{6,2},{7,3},{8,12},{9,13},{10,... | collective-permute-start | bytes 1572872 | tf_op jit(solution)/shard_map/ppermute | solution.py:294
  4.6 7.6 %collective-permute-start.1 = (f32[256,256]{1,0:T(8,128)S(1)}, f32[256,256]{1,0:T(8,128)S(1)}, u32[]{:S(2)}, u32[]{:S(2)}) collective-permute-start(f32[256,256]{1,0:T(8,128)S(1)} %plane.1), channel_id=1, source_target_pairs={{0,8},{1,9},{2,10},{3,11},{4,12},{5,13},{6,14},{7,15},{8,0},{9,1},... | collective-permute-start | bytes 786440 | tf_op jit(solution)/shard_map/ppermute | solution.py:294
  12.2 2.4 %collective-permute-start.2 = (f32[256,256]{1,0:T(8,128)S(1)}, f32[256,256]{1,0:T(8,128)S(1)}, u32[]{:S(2)}, u32[]{:S(2)}) collective-permute-start(f32[256,256]{1,0:T(8,128)S(1)} %collective-permute-done.1.near), channel_id=1, source_target_pairs={{0,4},{1,5},{2,6},{3,7},{4,0},{5,1},{6,2},{7,3},{8,12},{9,13},{10,... | collective-permute-start | bytes 786440 | tf_op jit(solution)/shard_map/ppermute | solution.py:294
  14.6 4.7 %collective-permute-start.5 = (f32[2,64,256]{2,1,0:T(8,128)S(1)}, f32[2,64,256]{2,1,0:T(8,128)S(1)}, u32[]{:S(2)}, u32[]{:S(2)}) collective-permute-start(f32[2,64,256]{2,1,0:T(8,128)S(1)} %get-tuple-element.42), channel_id=1, source_target_pairs={{0,1},{1,0},{2,3},{3,2},{4,5},{5,4},{6,7},{7,6},{8,9},{9,8},{10,11... | collective-permute-start | bytes 393224 | tf_op jit(solution)/shard_map/ppermute | solution.py:294
  15.3 4.5 %collective-permute-start.3 = (f32[2,64,256]{2,1,0:T(8,128)S(1)}, f32[2,64,256]{2,1,0:T(8,128)S(1)}, u32[]{:S(2)}, u32[]{:S(2)}) collective-permute-start(f32[2,64,256]{2,1,0:T(8,128)S(1)} %get-tuple-element.41.own), channel_id=1, source_target_pairs={{0,1},{4,5},{8,9},{12,13},{16,17},{20,21},{24,25},{28,29}} | collective-permute-start | bytes 393224 | tf_op jit(solution)/shard_map/ppermute | solution.py:294
  16.0 5.8 %copy-start.1 = (f32[1,1,2,2,256,256]{5,4,3,2,1,0:T(8,128)S(1)}, f32[1,1,2,2,256,256]{5,4,3,2,1,0:T(8,128)}, u32[]{:S(2)}) copy-start(f32[1,1,2,2,256,256]{5,4,3,2,1,0:T(8,128)} %u.3) | copy-start | bytes 3145732
  19.3 4.1 %collective-permute-start.6 = (f32[2,64,256]{2,1,0:T(8,128)S(1)}, f32[2,64,256]{2,1,0:T(8,128)S(1)}, u32[]{:S(2)}, u32[]{:S(2)}) collective-permute-start(f32[2,64,256]{2,1,0:T(8,128)S(1)} %extend.1), channel_id=1, source_target_pairs={{0,1},{1,2},{2,3},{3,0},{4,5},{5,6},{6,7},{7,4},{8,9},{9,10},{10,1... | collective-permute-start | bytes 393224 | tf_op jit(solution)/shard_map/ppermute | solution.py:294
  19.8 7.2 %collective-permute-start.4 = (f32[2,64,256]{2,1,0:T(8,128)S(1)}, f32[2,64,256]{2,1,0:T(8,128)S(1)}, u32[]{:S(2)}, u32[]{:S(2)}) collective-permute-start(f32[2,64,256]{2,1,0:T(8,128)S(1)} %extend_other.1), channel_id=1, source_target_pairs={{1,3},{5,7},{9,11},{13,15},{17,19},{21,23},{25,27},{29,31}} | collective-permute-start | bytes 393224 | tf_op jit(solution)/shard_map/ppermute | solution.py:294
  21.0 9.9 %collective-permute-start.8 = (f32[2,64,256]{2,1,0:T(8,128)S(1)}, f32[2,64,256]{2,1,0:T(8,128)S(1)}, u32[]{:S(2)}, u32[]{:S(2)}) collective-permute-start(f32[2,64,256]{2,1,0:T(8,128)S(1)} %extend_other.1), channel_id=1, source_target_pairs={{1,2},{5,6},{9,10},{13,14},{17,18},{21,22},{25,26},{29,30}} | collective-permute-start | bytes 393224 | tf_op jit(solution)/shard_map/ppermute | solution.py:294
  23.4 8.5 %collective-permute-start.7 = (f32[2,64,256]{2,1,0:T(8,128)S(1)}, f32[2,64,256]{2,1,0:T(8,128)S(1)}, u32[]{:S(2)}, u32[]{:S(2)}) collective-permute-start(f32[2,64,256]{2,1,0:T(8,128)S(1)} %collective-permute-done.6.across.two), channel_id=1, source_target_pairs={{2,3},{6,7},{10,11},{14,15},{18,19},{22,23},{26,27},{30,31}} | collective-permute-start | bytes 393224 | tf_op jit(solution)/shard_map/ppermute | solution.py:294
  24.7 6.5 %collective-permute-start.9 = (f32[96,256]{1,0:T(8,128)S(1)}, f32[96,256]{1,0:T(8,128)S(1)}, u32[]{:S(2)}, u32[]{:S(2)}) collective-permute-start(f32[96,256]{1,0:T(8,128)S(1)} %get-tuple-element.59), channel_id=1, source_target_pairs={{0,4},{1,5},{2,6},{3,7},{4,0},{5,1},{6,2},{7,3},{8,12},{9,13},{10,... | collective-permute-start | bytes 294920 | tf_op jit(solution)/shard_map/ppermute | solution.py:294
  26.8 4.2 %collective-permute-start.10 = (f32[80,256]{1,0:T(8,128)S(1)}, f32[80,256]{1,0:T(8,128)S(1)}, u32[]{:S(2)}, u32[]{:S(2)}) collective-permute-start(f32[80,256]{1,0:T(8,128)S(1)} %get-tuple-element.60), channel_id=1, source_target_pairs={{0,4},{1,5},{2,6},{3,7},{4,0},{5,1},{6,2},{7,3},{8,12},{9,13},{10,... | collective-permute-start | bytes 245768 | tf_op jit(solution)/shard_map/ppermute | solution.py:294
  26.9 4.3 %collective-permute-start.11 = (f32[80,256]{1,0:T(8,128)S(1)}, f32[80,256]{1,0:T(8,128)S(1)}, u32[]{:S(2)}, u32[]{:S(2)}) collective-permute-start(f32[80,256]{1,0:T(8,128)S(1)} %get-tuple-element.61), channel_id=1, source_target_pairs={{0,4},{1,5},{2,6},{3,7},{4,0},{5,1},{6,2},{7,3},{8,12},{9,13},{10,... | collective-permute-start | bytes 245768 | tf_op jit(solution)/shard_map/ppermute | solution.py:294
  30.9 2.1 %collective-permute-start.12 = (f32[2,64,256]{2,1,0:T(8,128)S(1)}, f32[2,64,256]{2,1,0:T(8,128)S(1)}, u32[]{:S(2)}, u32[]{:S(2)}) collective-permute-start(f32[2,64,256]{2,1,0:T(8,128)S(1)} %merge_early.1.early), channel_id=1, source_target_pairs={{0,4},{1,5},{2,6},{3,7},{4,0},{5,1},{6,2},{7,3},{8,12},{9,13},{10,... | collective-permute-start | bytes 393224 | tf_op jit(solution)/shard_map/ppermute | solution.py:294
  31.9 1.5 %collective-permute-start.13 = (f32[2,64,256]{2,1,0:T(8,128)S(1)}, f32[2,64,256]{2,1,0:T(8,128)S(1)}, u32[]{:S(2)}, u32[]{:S(2)}) collective-permute-start(f32[2,64,256]{2,1,0:T(8,128)S(1)} %merge_late.1.late), channel_id=1, source_target_pairs={{0,4},{1,5},{2,6},{3,7},{4,0},{5,1},{6,2},{7,3},{8,12},{9,13},{10,... | collective-permute-start | bytes 393224 | tf_op jit(solution)/shard_map/ppermute | solution.py:294

commit v10 on v9

--- a/solution.py
+++ b/solution.py
@@ -120,19 +120,26 @@
     return pick(x == 0, mine, other), pick(x == 0, other, mine)
 
 
-def strips_kernel(chip, near, far, own, other, scratch):
+def strips_kernel(chip, near, far, own, other):
     x, k, w = place()
-
-    @pl.when(w % 2 == 0)
-    def _():
-        one, two = ordered(x, k, chip, near, far)
-        put(scratch, one)
-        rows = own.shape[1]
-        half = scratch[:, pl.ds(pl.multiple_of(2 * k * rows, 2 * rows), 2 * rows), :]
-        value = product((half[0], half[1]), two)
-        top, low = tuple(v[:rows] for v in value), tuple(v[rows:] for v in value)
-        put(own, pick(x == 0, top, low))
-        put(other, pick(x == 0, low, top))
+    rows = own.shape[1]
+    at = pl.ds(pl.multiple_of(2 * k * rows, 2 * rows), 2 * rows)
+
+    @pl.when((w % 2 == 0) & (x == 0))
+    def _():
+        half = chip[:, at, :]
+        right = pick(k == 0, (near[...], far[...]), (far[...], near[...]))
+        value = product((half[0], half[1]), right)
+        put(own, tuple(v[:rows] for v in value))
+        put(other, tuple(v[rows:] for v in value))
+
+    @pl.when((w % 2 == 0) & (x == 1))
+    def _():
+        near_half, far_half = near[at, :], far[at, :]
+        left = pick(k == 0, (near_half, far_half), (far_half, near_half))
+        value = product(left, pair(chip))
+        put(own, tuple(v[rows:] for v in value))
+        put(other, tuple(v[:rows] for v in value))
 
 
 def window_kernel(chip, near, far, window):
@@ -315,9 +322,7 @@
     (chip,) = call(chip_kernel, [full], turned, turned_other, plane, name="chip")
     near_chip, chip = tie((near_chip, chip))
     far_chip = permute(near_chip, cores)
-    own, other = call(
-        strips_kernel, [strip, strip], chip, near_chip, far_chip, name="strips", scratch=[pltpu.VMEM(full, F32)]
-    )
+    own, other = call(strips_kernel, [strip, strip], chip, near_chip, far_chip, name="strips")
     one = permute(own, twins)
     (window,) = call(window_kernel, [full], chip, near_chip, far_chip, name="window")
     one_other = permute(other, zero_one)

time: 35 us -> 35 us (level)
  no operation moved by 1% of the time
where the time goes in v10:
time: 35 us; the launch traced here: 34.8 us
  starting transfers between devices  14.4 us (41%)
  waiting for transfers between devices  12.5 us (36%)
  Pallas kernels  6.49 us (19%)
  local copies, waits for them, and re-layouts  1.23 us (4%)
    ppermute x14, starting transfers between devices, permute(): return lax.ppermute(value, AXES, flat)  14.4 us
    ppermute x14, waiting for transfers between devices, permute(): return lax.ppermute(value, AXES, flat)  12.5 us
    pallas_call x16, Pallas kernels, call(): pl.pallas_call(body, out_shape=shapes, in_specs=[far if i == alias else w...  6.49 us
    unnamed x4, local copies, waits for them, and re-layouts  1.23 us
  transfers between devices with their start and end apart: 14, of which 6 were waited for; matrix products, arithmetic and copies ran while one was open for 0% of the time, Pallas kernels for 11%

profile of v10, /device:TPU:29, one launch (start us, length us, event | category | flops | bytes accessed | tf_op | source)
XLA Modules:
  0.0 34.8 jit_solution(2131010982449439221)
XLA Ops:
  0.0 0.0 copy-start
  0.0 1.2 %copy-done = f32[1,1,2,2,256,256]{5,4,3,2,1,0:T(8,128)S(1)} copy-done((f32[1,1,2,2,256,256]{5,4,3,2,1,0:T(8,128)S(1)}, f32[1,1,2,2,256,256]{5,4,3,2,1,0:T(8,128)}, u32[]{:S(2)}) %copy-start) | copy-done | bytes 1048600
  1.2 0.7 %block.1 = (f32[2,256,256]{2,1,0:T(8,128)S(1)}, f32[2,256,256]{2,1,0:T(8,128)S(1)}) custom-call(f32[1,1,2,2,256,256]{5,4,3,2,1,0:T(8,128)S(1)} %copy-done), custom_call_target="tpu_custom_call" | custom-call | tf_op jit(solution)/shard_map/block/pallas_call | solution.py:66
  1.9 0.7 %collective-permute-start = (f32[2,256,256]{2,1,0:T(8,128)S(1)}, f32[2,256,256]{2,1,0:T(8,128)S(1)}, u32[]{:S(2)}, u32[]{:S(2)}) collective-permute-start(f32[2,256,256]{2,1,0:T(8,128)S(1)} %get-tuple-element.38.mine), channel_id=1, source_target_pairs={{0,4},{1,5},{2,6},{3,7},{4,0},{5,1},{6,2},{7,3},{8,12},{9,13},{10,... | collective-permute-start | bytes 1572872 | tf_op jit(solution)/shard_map/ppermute | solution.py:301
  2.7 1.5 %collective-permute-done.theirs.turned = f32[2,256,256]{2,1,0:T(8,128)S(1)} collective-permute-done((f32[2,256,256]{2,1,0:T(8,128)S(1)}, f32[2,256,256]{2,1,0:T(8,128)S(1)}, u32[]{:S(2)}, u32[]{:S(2)}) %collective-permute-start) | collective-permute-done | bytes 524320 | tf_op jit(solution)/shard_map/ppermute | solution.py:301
  4.2 0.4 %plane.1 = f32[256,256]{1,0:T(8,128)S(1)} custom-call(f32[2,256,256]{2,1,0:T(8,128)S(1)} %get-tuple-element.38.mine, f32[2,256,256]{2,1,0:T(8,128)S(1)} %collective-permute-done.theirs.turned), custom_call_target="tpu_custom_call" | custom-call | tf_op jit(solution)/shard_map/plane/pallas_call | solution.py:66
  4.6 1.3 %collective-permute-start.1 = (f32[256,256]{1,0:T(8,128)S(1)}, f32[256,256]{1,0:T(8,128)S(1)}, u32[]{:S(2)}, u32[]{:S(2)}) collective-permute-start(f32[256,256]{1,0:T(8,128)S(1)} %plane.1), channel_id=1, source_target_pairs={{0,8},{1,9},{2,10},{3,11},{4,12},{5,13},{6,14},{7,15},{8,0},{9,1},... | collective-permute-start | bytes 786440 | tf_op jit(solution)/shard_map/ppermute | solution.py:301
  5.9 0.4 %chip.1 = f32[2,256,256]{2,1,0:T(8,128)S(1)} custom-call(f32[2,256,256]{2,1,0:T(8,128)S(1)} %get-tuple-element.38.mine, f32[2,256,256]{2,1,0:T(8,128)S(1)} %collective-permute-done.theirs.turned, f32[256,256]{1,0:T(8,128)S(1)} %plane.1), custom_call_target="tpu_custom_call" | custom-call | tf_op jit(solution)/shard_map/chip/pallas_call | solution.py:66
  6.3 5.9 %collective-permute-done.1.near = f32[256,256]{1,0:T(8,128)S(1)} collective-permute-done((f32[256,256]{1,0:T(8,128)S(1)}, f32[256,256]{1,0:T(8,128)S(1)}, u32[]{:S(2)}, u32[]{:S(2)}) %collective-permute-start.1) | collective-permute-done | bytes 262176 | tf_op jit(solution)/shard_map/ppermute | solution.py:301
  12.2 1.2 %collective-permute-start.2 = (f32[256,256]{1,0:T(8,128)S(1)}, f32[256,256]{1,0:T(8,128)S(1)}, u32[]{:S(2)}, u32[]{:S(2)}) collective-permute-start(f32[256,256]{1,0:T(8,128)S(1)} %collective-permute-done.1.near), channel_id=1, source_target_pairs={{0,4},{1,5},{2,6},{3,7},{4,0},{5,1},{6,2},{7,3},{8,12},{9,13},{10,... | collective-permute-start | bytes 786440 | tf_op jit(solution)/shard_map/ppermute | solution.py:301
  13.4 1.2 %collective-permute-done.2.far = f32[256,256]{1,0:T(8,128)S(1)} collective-permute-done((f32[256,256]{1,0:T(8,128)S(1)}, f32[256,256]{1,0:T(8,128)S(1)}, u32[]{:S(2)}, u32[]{:S(2)}) %collective-permute-start.2) | collective-permute-done | bytes 262176 | tf_op jit(solution)/shard_map/ppermute | solution.py:301
  14.6 0.6 %collective-permute-start.5 = (f32[2,64,256]{2,1,0:T(8,128)S(1)}, f32[2,64,256]{2,1,0:T(8,128)S(1)}, u32[]{:S(2)}, u32[]{:S(2)}) collective-permute-start(f32[2,64,256]{2,1,0:T(8,128)S(1)} %get-tuple-element.42), channel_id=1, source_target_pairs={{0,1},{1,0},{2,3},{3,2},{4,5},{5,4},{6,7},{7,6},{8,9},{9,8},{10,11... | collective-permute-start | bytes 393224 | tf_op jit(solution)/shard_map/ppermute | solution.py:301
  15.2 0.7 %collective-permute-start.3 = (f32[2,64,256]{2,1,0:T(8,128)S(1)}, f32[2,64,256]{2,1,0:T(8,128)S(1)}, u32[]{:S(2)}, u32[]{:S(2)}) collective-permute-start(f32[2,64,256]{2,1,0:T(8,128)S(1)} %get-tuple-element.41.own), channel_id=1, source_target_pairs={{0,1},{4,5},{8,9},{12,13},{16,17},{20,21},{24,25},{28,29}} | collective-permute-start | bytes 393224 | tf_op jit(solution)/shard_map/ppermute | solution.py:301
  15.9 0.0 copy-start.1
  15.9 3.4 %collective-permute-done.5.piece.near.one = f32[2,64,256]{2,1,0:T(8,128)S(1)} collective-permute-done((f32[2,64,256]{2,1,0:T(8,128)S(1)}, f32[2,64,256]{2,1,0:T(8,128)S(1)}, u32[]{:S(2)}, u32[]{:S(2)}) %collective-permute-start.5) | collective-permute-done | bytes 131104 | tf_op jit(solution)/shard_map/ppermute | solution.py:301
  19.3 0.4 %collective-permute-start.6 = (f32[2,64,256]{2,1,0:T(8,128)S(1)}, f32[2,64,256]{2,1,0:T(8,128)S(1)}, u32[]{:S(2)}, u32[]{:S(2)}) collective-permute-start(f32[2,64,256]{2,1,0:T(8,128)S(1)} %extend.1), channel_id=1, source_target_pairs={{0,1},{1,2},{2,3},{3,0},{4,5},{5,6},{6,7},{7,4},{8,9},{9,10},{10,1... | collective-permute-start | bytes 393224 | tf_op jit(solution)/shard_map/ppermute | solution.py:301
  19.7 0.0 collective-permute-done.3.piece.one
  19.7 1.3 %collective-permute-start.4 = (f32[2,64,256]{2,1,0:T(8,128)S(1)}, f32[2,64,256]{2,1,0:T(8,128)S(1)}, u32[]{:S(2)}, u32[]{:S(2)}) collective-permute-start(f32[2,64,256]{2,1,0:T(8,128)S(1)} %extend_other.1), channel_id=1, source_target_pairs={{1,3},{5,7},{9,11},{13,15},{17,19},{21,23},{25,27},{29,31}} | collective-permute-start | bytes 393224 | tf_op jit(solution)/shard_map/ppermute | solution.py:301
  21.0 0.7 %collective-permute-start.8 = (f32[2,64,256]{2,1,0:T(8,128)S(1)}, f32[2,64,256]{2,1,0:T(8,128)S(1)}, u32[]{:S(2)}, u32[]{:S(2)}) collective-permute-start(f32[2,64,256]{2,1,0:T(8,128)S(1)} %extend_other.1), channel_id=1, source_target_pairs={{1,2},{5,6},{9,10},{13,14},{17,18},{21,22},{25,26},{29,30}} | collective-permute-start | bytes 393224 | tf_op jit(solution)/shard_map/ppermute | solution.py:301
  21.7 0.0 copy-done.1
  21.7 1.6 %before.1 = (f32[2,2,256,256]{3,2,1,0:T(8,128)S(1)}, bf16[2,2,256,256]{3,2,1,0:T(8,128)(2,1)S(1)}, bf16[2,2,256,256]{3,2,1,0:T(8,128)(2,1)S(1)}) custom-call(f32[1,1,2,2,256,256]{5,4,3,2,1,0:T(8,128)S(1)} %copy-done.1, f32[2,256,256]{2,1,0:T(8,128)S(1)} %get-tuple-element.43.block, f32[2,256,256]{2,1,0:T(8,128)S(1)} %collective-permute-done.theirs.turned, ...), custom_call_target="tpu_custom_call" | custom-call | tf_op jit(solution)/shard_map/before/pallas_call | solution.py:66
  23.3 0.0 collective-permute-done.6.across.two
  23.3 1.3 %collective-permute-start.7 = (f32[2,64,256]{2,1,0:T(8,128)S(1)}, f32[2,64,256]{2,1,0:T(8,128)S(1)}, u32[]{:S(2)}, u32[]{:S(2)}) collective-permute-start(f32[2,64,256]{2,1,0:T(8,128)S(1)} %collective-permute-done.6.across.two), channel_id=1, source_target_pairs={{2,3},{6,7},{10,11},{14,15},{18,19},{22,23},{26,27},{30,31}} | collective-permute-start | bytes 393224 | tf_op jit(solution)/shard_map/ppermute | solution.py:301
  24.6 2.2 %collective-permute-start.9 = (f32[96,256]{1,0:T(8,128)S(1)}, f32[96,256]{1,0:T(8,128)S(1)}, u32[]{:S(2)}, u32[]{:S(2)}) collective-permute-start(f32[96,256]{1,0:T(8,128)S(1)} %get-tuple-element.59), channel_id=1, source_target_pairs={{0,4},{1,5},{2,6},{3,7},{4,0},{5,1},{6,2},{7,3},{8,12},{9,13},{10,... | collective-permute-start | bytes 294920 | tf_op jit(solution)/shard_map/ppermute | solution.py:301
  26.8 0.1 collective-permute-start.10
  26.9 0.0 collective-permute-done.4.three
  26.9 3.3 %collective-permute-start.11 = (f32[80,256]{1,0:T(8,128)S(1)}, f32[80,256]{1,0:T(8,128)S(1)}, u32[]{:S(2)}, u32[]{:S(2)}) collective-permute-start(f32[80,256]{1,0:T(8,128)S(1)} %get-tuple-element.61), channel_id=1, source_target_pairs={{0,4},{1,5},{2,6},{3,7},{4,0},{5,1},{6,2},{7,3},{8,12},{9,13},{10,... | collective-permute-start | bytes 245768 | tf_op jit(solution)/shard_map/ppermute | solution.py:301
  30.2 0.6 %left.1 = (bf16[2,2,256,128]{3,2,1,0:T(8,128)(2,1)S(1)}, bf16[2,2,256,128]{3,2,1,0:T(8,128)(2,1)S(1)}) custom-call(bf16[2,2,256,256]{3,2,1,0:T(8,128)(2,1)S(1)} %get-tuple-element.49.before_high, bf16[2,2,256,256]{3,2,1,0:T(8,128)(2,1)S(1)} %get-tuple-element.50.before_low, f32[2,64,256]{2,1,0:T(8,128)S(1)} %collective-permute-done.5.piece.near.one, ...), custom_call_target="tpu_custom_call" | custom-call | tf_op jit(solution)/shard_map/left/pallas_call | solution.py:66
  30.9 0.0 collective-permute-done.8.two.three
  30.9 0.1 collective-permute-start.12
  31.0 0.0 collective-permute-done.10.refs_1_
  31.0 0.1 collective-permute-done.11.refs_2_
  31.1 0.0 collective-permute-done.9.refs_0_
  31.1 0.6 %left_far.1 = (bf16[2,2,256,128]{3,2,1,0:T(8,128)(2,1)S(1)}, bf16[2,2,256,128]{3,2,1,0:T(8,128)(2,1)S(1)}) custom-call(bf16[2,2,256,256]{3,2,1,0:T(8,128)(2,1)S(1)} %get-tuple-element.49.before_high, bf16[2,2,256,256]{3,2,1,0:T(8,128)(2,1)S(1)} %get-tuple-element.50.before_low, f32[96,256]{1,0:T(8,128)S(1)} %collective-permute-done.9.refs_0_, ...), custom_call_target="tpu_custom_call" | custom-call | tf_op jit(solution)/shard_map/left_far/pallas_call | solution.py:66
  31.8 0.0 collective-permute-done.7.three
  31.8 0.6 %collective-permute-start.13 = (f32[2,64,256]{2,1,0:T(8,128)S(1)}, f32[2,64,256]{2,1,0:T(8,128)S(1)}, u32[]{:S(2)}, u32[]{:S(2)}) collective-permute-start(f32[2,64,256]{2,1,0:T(8,128)S(1)} %merge_late.1.late), channel_id=1, source_target_pairs={{0,4},{1,5},{2,6},{3,7},{4,0},{5,1},{6,2},{7,3},{8,12},{9,13},{10,... | collective-permute-start | bytes 393224 | tf_op jit(solution)/shard_map/ppermute | solution.py:301
  32.4 0.6 %near.1 = (f32[2,2,256,128]{3,2,1,0:T(8,128)S(1)}, bf16[2,2,256,256]{3,2,1,0:T(8,128)(2,1)S(1)}, bf16[2,2,256,256]{3,2,1,0:T(8,128)(2,1)S(1)}) custom-call(bf16[2,2,256,128]{3,2,1,0:T(8,128)(2,1)S(1)} %get-tuple-element.55.high, bf16[2,2,256,128]{3,2,1,0:T(8,128)(2,1)S(1)} %get-tuple-element.56.low, bf16[2,2,256,128]{3,2,1,0:T(8,128)(2,1)S(1)} %get-tuple-element.63.far_high, ...), custom_call_target="tpu_custom_call" | custom-call | tf_op jit(solution)/shard_map/near/pallas_call | solution.py:66
  33.0 0.0 collective-permute-done.12.early
  33.0 0.3 collective-permute-done.13.late
  33.4 1.4 %far.1 = f32[1,1,2,2,256,256]{5,4,3,2,1,0:T(8,128)} custom-call(f32[2,2,256,256]{3,2,1,0:T(8,128)S(1)} %get-tuple-element.47.before, f32[2,2,256,128]{3,2,1,0:T(8,128)S(1)} %get-tuple-element.68.near, bf16[2,2,256,256]{3,2,1,0:T(8,128)(2,1)S(1)} %get-tuple-element.69.high, bf16[2,2,256,256]{3,2,1,0:T(8,128)(2,1)S(1)} %get-tuple-element.70.low, ...), custom_call_target="tpu_custom_call" | custom-call | tf_op jit(solution)/shard_map/far/pallas_call | solution.py:66
  (8 shorter events, 0.1 us)
Async XLA Ops:
  0.0 1.2 %copy-start = (f32[1,1,2,2,256,256]{5,4,3,2,1,0:T(8,128)S(1)}, f32[1,1,2,2,256,256]{5,4,3,2,1,0:T(8,128)}, u32[]{:S(2)}) copy-start(f32[1,1,2,2,256,256]{5,4,3,2,1,0:T(8,128)} %u.3) | copy-start | bytes 3145732
  1.9 2.3 %collective-permute-start = (f32[2,256,256]{2,1,0:T(8,128)S(1)}, f32[2,256,256]{2,1,0:T(8,128)S(1)}, u32[]{:S(2)}, u32[]{:S(2)}) collective-permute-start(f32[2,256,256]{2,1,0:T(8,128)S(1)} %get-tuple-element.38.mine), channel_id=1, source_target_pairs={{0,4},{1,5},{2,6},{3,7},{4,0},{5,1},{6,2},{7,3},{8,12},{9,13},{10,... | collective-permute-start | bytes 1572872 | tf_op jit(solution)/shard_map/ppermute | solution.py:301
  4.6 7.6 %collective-permute-start.1 = (f32[256,256]{1,0:T(8,128)S(1)}, f32[256,256]{1,0:T(8,128)S(1)}, u32[]{:S(2)}, u32[]{:S(2)}) collective-permute-start(f32[256,256]{1,0:T(8,128)S(1)} %plane.1), channel_id=1, source_target_pairs={{0,8},{1,9},{2,10},{3,11},{4,12},{5,13},{6,14},{7,15},{8,0},{9,1},... | collective-permute-start | bytes 786440 | tf_op jit(solution)/shard_map/ppermute | solution.py:301
  12.2 2.4 %collective-permute-start.2 = (f32[256,256]{1,0:T(8,128)S(1)}, f32[256,256]{1,0:T(8,128)S(1)}, u32[]{:S(2)}, u32[]{:S(2)}) collective-permute-start(f32[256,256]{1,0:T(8,128)S(1)} %collective-permute-done.1.near), channel_id=1, source_target_pairs={{0,4},{1,5},{2,6},{3,7},{4,0},{5,1},{6,2},{7,3},{8,12},{9,13},{10,... | collective-permute-start | bytes 786440 | tf_op jit(solution)/shard_map/ppermute | solution.py:301
  14.6 4.7 %collective-permute-start.5 = (f32[2,64,256]{2,1,0:T(8,128)S(1)}, f32[2,64,256]{2,1,0:T(8,128)S(1)}, u32[]{:S(2)}, u32[]{:S(2)}) collective-permute-start(f32[2,64,256]{2,1,0:T(8,128)S(1)} %get-tuple-element.42), channel_id=1, source_target_pairs={{0,1},{1,0},{2,3},{3,2},{4,5},{5,4},{6,7},{7,6},{8,9},{9,8},{10,11... | collective-permute-start | bytes 393224 | tf_op jit(solution)/shard_map/ppermute | solution.py:301
  15.2 4.5 %collective-permute-start.3 = (f32[2,64,256]{2,1,0:T(8,128)S(1)}, f32[2,64,256]{2,1,0:T(8,128)S(1)}, u32[]{:S(2)}, u32[]{:S(2)}) collective-permute-start(f32[2,64,256]{2,1,0:T(8,128)S(1)} %get-tuple-element.41.own), channel_id=1, source_target_pairs={{0,1},{4,5},{8,9},{12,13},{16,17},{20,21},{24,25},{28,29}} | collective-permute-start | bytes 393224 | tf_op jit(solution)/shard_map/ppermute | solution.py:301
  15.9 5.8 %copy-start.1 = (f32[1,1,2,2,256,256]{5,4,3,2,1,0:T(8,128)S(1)}, f32[1,1,2,2,256,256]{5,4,3,2,1,0:T(8,128)}, u32[]{:S(2)}) copy-start(f32[1,1,2,2,256,256]{5,4,3,2,1,0:T(8,128)} %u.3) | copy-start | bytes 3145732
  19.3 4.0 %collective-permute-start.6 = (f32[2,64,256]{2,1,0:T(8,128)S(1)}, f32[2,64,256]{2,1,0:T(8,128)S(1)}, u32[]{:S(2)}, u32[]{:S(2)}) collective-permute-start(f32[2,64,256]{2,1,0:T(8,128)S(1)} %extend.1), channel_id=1, source_target_pairs={{0,1},{1,2},{2,3},{3,0},{4,5},{5,6},{6,7},{7,4},{8,9},{9,10},{10,1... | collective-permute-start | bytes 393224 | tf_op jit(solution)/shard_map/ppermute | solution.py:301
  19.7 7.2 %collective-permute-start.4 = (f32[2,64,256]{2,1,0:T(8,128)S(1)}, f32[2,64,256]{2,1,0:T(8,128)S(1)}, u32[]{:S(2)}, u32[]{:S(2)}) collective-permute-start(f32[2,64,256]{2,1,0:T(8,128)S(1)} %extend_other.1), channel_id=1, source_target_pairs={{1,3},{5,7},{9,11},{13,15},{17,19},{21,23},{25,27},{29,31}} | collective-permute-start | bytes 393224 | tf_op jit(solution)/shard_map/ppermute | solution.py:301
  21.0 9.9 %collective-permute-start.8 = (f32[2,64,256]{2,1,0:T(8,128)S(1)}, f32[2,64,256]{2,1,0:T(8,128)S(1)}, u32[]{:S(2)}, u32[]{:S(2)}) collective-permute-start(f32[2,64,256]{2,1,0:T(8,128)S(1)} %extend_other.1), channel_id=1, source_target_pairs={{1,2},{5,6},{9,10},{13,14},{17,18},{21,22},{25,26},{29,30}} | collective-permute-start | bytes 393224 | tf_op jit(solution)/shard_map/ppermute | solution.py:301
  23.3 8.5 %collective-permute-start.7 = (f32[2,64,256]{2,1,0:T(8,128)S(1)}, f32[2,64,256]{2,1,0:T(8,128)S(1)}, u32[]{:S(2)}, u32[]{:S(2)}) collective-permute-start(f32[2,64,256]{2,1,0:T(8,128)S(1)} %collective-permute-done.6.across.two), channel_id=1, source_target_pairs={{2,3},{6,7},{10,11},{14,15},{18,19},{22,23},{26,27},{30,31}} | collective-permute-start | bytes 393224 | tf_op jit(solution)/shard_map/ppermute | solution.py:301
  24.6 6.5 %collective-permute-start.9 = (f32[96,256]{1,0:T(8,128)S(1)}, f32[96,256]{1,0:T(8,128)S(1)}, u32[]{:S(2)}, u32[]{:S(2)}) collective-permute-start(f32[96,256]{1,0:T(8,128)S(1)} %get-tuple-element.59), channel_id=1, source_target_pairs={{0,4},{1,5},{2,6},{3,7},{4,0},{5,1},{6,2},{7,3},{8,12},{9,13},{10,... | collective-permute-start | bytes 294920 | tf_op jit(solution)/shard_map/ppermute | solution.py:301
  26.8 4.1 %collective-permute-start.10 = (f32[80,256]{1,0:T(8,128)S(1)}, f32[80,256]{1,0:T(8,128)S(1)}, u32[]{:S(2)}, u32[]{:S(2)}) collective-permute-start(f32[80,256]{1,0:T(8,128)S(1)} %get-tuple-element.60), channel_id=1, source_target_pairs={{0,4},{1,5},{2,6},{3,7},{4,0},{5,1},{6,2},{7,3},{8,12},{9,13},{10,... | collective-permute-start | bytes 245768 | tf_op jit(solution)/shard_map/ppermute | solution.py:301
  26.9 4.2 %collective-permute-start.11 = (f32[80,256]{1,0:T(8,128)S(1)}, f32[80,256]{1,0:T(8,128)S(1)}, u32[]{:S(2)}, u32[]{:S(2)}) collective-permute-start(f32[80,256]{1,0:T(8,128)S(1)} %get-tuple-element.61), channel_id=1, source_target_pairs={{0,4},{1,5},{2,6},{3,7},{4,0},{5,1},{6,2},{7,3},{8,12},{9,13},{10,... | collective-permute-start | bytes 245768 | tf_op jit(solution)/shard_map/ppermute | solution.py:301
  30.9 2.2 %collective-permute-start.12 = (f32[2,64,256]{2,1,0:T(8,128)S(1)}, f32[2,64,256]{2,1,0:T(8,128)S(1)}, u32[]{:S(2)}, u32[]{:S(2)}) collective-permute-start(f32[2,64,256]{2,1,0:T(8,128)S(1)} %merge_early.1.early), channel_id=1, source_target_pairs={{0,4},{1,5},{2,6},{3,7},{4,0},{5,1},{6,2},{7,3},{8,12},{9,13},{10,... | collective-permute-start | bytes 393224 | tf_op jit(solution)/shard_map/ppermute | solution.py:301
  31.8 1.6 %collective-permute-start.13 = (f32[2,64,256]{2,1,0:T(8,128)S(1)}, f32[2,64,256]{2,1,0:T(8,128)S(1)}, u32[]{:S(2)}, u32[]{:S(2)}) collective-permute-start(f32[2,64,256]{2,1,0:T(8,128)S(1)} %merge_late.1.late), channel_id=1, source_target_pairs={{0,4},{1,5},{2,6},{3,7},{4,0},{5,1},{6,2},{7,3},{8,12},{9,13},{10,... | collective-permute-start | bytes 393224 | tf_op jit(solution)/shard_map/ppermute | solution.py:301

commit v11 on v10

--- a/solution.py
+++ b/solution.py
@@ -236,14 +236,6 @@
     return real[:, :width] - imag[:, width:], real[:, width:] + imag[:, :width]
 
 
-def joined(k, mine, theirs):
-    def plane(slot, index):
-        a, b = mine[slot, index], theirs[slot, index]
-        return jnp.concatenate([jnp.where(k == 0, a, b), jnp.where(k == 0, b, a)], axis=1)
-
-    return {(slot, index): plane(slot, index) for slot in range(2) for index in range(2)}
-
-
 def left_far_kernel(before_high, before_low, *refs):
     _, k, _ = place()
     *pieces, high, low = refs
@@ -254,16 +246,17 @@
 
 def near_kernel(high, low, far_high, far_low, early, late, out, whole_high, whole_low):
     x, k, w = place()
+    width = high.shape[-1]
 
     @pl.when(w != 0)
     def _():
-        both_high, both_low = joined(k, high, far_high), joined(k, low, far_low)
-        for slot in range(2):
-            for plane in range(2):
-                whole_high[slot, plane], whole_low[slot, plane] = both_high[slot, plane], both_low[slot, plane]
+        for core, parts in ((k, (high, low)), (1 - k, (far_high, far_low))):
+            at = pl.ds(pl.multiple_of(core * width, width), width)
+            for part, joined in zip(parts, (whole_high, whole_low), strict=True):
+                joined[:, :, :, at] = part[...]
         offset = halves(jnp.concatenate(half(jnp.where(w == 3, 1 - x, x), early, late), axis=0))
         for slot in range(2):
-            put(out.at[slot], columns_of(both_high, both_low, slot, offset))
+            put(out.at[slot], columns_of(whole_high, whole_low, slot, offset))
 
 
 def far_kernel(before, near, high, low, early, late, out, far, sems):
@@ -341,7 +334,6 @@
     thirds = [(3 * width // 8, width)] + [(5 * width // 16, width)] * 2
     planes = call(planes_kernel, thirds, own, past, name="planes")
     far_strips = [permute(plane, cores) for plane in planes]
-    three_other, before = tie((three_other, before))
     parts = [jax.ShapeDtypeStruct((2, 2, width, width // 2), jnp.bfloat16)] * 2
     high, low = call(left_kernel, parts, *before_parts, own, past, name="left")
     three_other, high = tie((three_other, high))

time: 35 us -> 35 us (level)
  no operation moved by 1% of the time
where the time goes in v11:
time: 35 us; the launch traced here: 34.8 us
  starting transfers between devices  14.4 us (41%)
  waiting for transfers between devices  12.4 us (35%)
  Pallas kernels  6.51 us (19%)
  local copies, waits for them, and re-layouts  1.23 us (4%)
    ppermute x14, starting transfers between devices, permute(): return lax.ppermute(value, AXES, flat)  14.4 us
    ppermute x14, waiting for transfers between devices, permute(): return lax.ppermute(value, AXES, flat)  12.4 us
    pallas_call x16, Pallas kernels, call(): pl.pallas_call(body, out_shape=shapes, in_specs=[far if i == alias else w...  6.51 us
    unnamed x4, local copies, waits for them, and re-layouts  1.23 us
  transfers between devices with their start and end apart: 14, of which 6 were waited for; matrix products, arithmetic and copies ran while one was open for 0% of the time, Pallas kernels for 11%

profile of v11, /device:TPU:29, one launch (start us, length us, event | category | flops | bytes accessed | tf_op | source)
XLA Modules:
  0.0 34.8 jit_solution(3347222440082095115)
XLA Ops:
  0.0 0.0 copy-start
  0.0 1.2 %copy-done = f32[1,1,2,2,256,256]{5,4,3,2,1,0:T(8,128)S(1)} copy-done((f32[1,1,2,2,256,256]{5,4,3,2,1,0:T(8,128)S(1)}, f32[1,1,2,2,256,256]{5,4,3,2,1,0:T(8,128)}, u32[]{:S(2)}) %copy-start) | copy-done | bytes 1048600
  1.2 0.7 %block.1 = (f32[2,256,256]{2,1,0:T(8,128)S(1)}, f32[2,256,256]{2,1,0:T(8,128)S(1)}) custom-call(f32[1,1,2,2,256,256]{5,4,3,2,1,0:T(8,128)S(1)} %copy-done), custom_call_target="tpu_custom_call" | custom-call | tf_op jit(solution)/shard_map/block/pallas_call | solution.py:66
  1.9 0.7 %collective-permute-start = (f32[2,256,256]{2,1,0:T(8,128)S(1)}, f32[2,256,256]{2,1,0:T(8,128)S(1)}, u32[]{:S(2)}, u32[]{:S(2)}) collective-permute-start(f32[2,256,256]{2,1,0:T(8,128)S(1)} %get-tuple-element.36.mine), channel_id=1, source_target_pairs={{0,4},{1,5},{2,6},{3,7},{4,0},{5,1},{6,2},{7,3},{8,12},{9,13},{10,... | collective-permute-start | bytes 1572872 | tf_op jit(solution)/shard_map/ppermute | solution.py:294
  2.7 1.5 %collective-permute-done.theirs.turned = f32[2,256,256]{2,1,0:T(8,128)S(1)} collective-permute-done((f32[2,256,256]{2,1,0:T(8,128)S(1)}, f32[2,256,256]{2,1,0:T(8,128)S(1)}, u32[]{:S(2)}, u32[]{:S(2)}) %collective-permute-start) | collective-permute-done | bytes 524320 | tf_op jit(solution)/shard_map/ppermute | solution.py:294
  4.2 0.4 %plane.1 = f32[256,256]{1,0:T(8,128)S(1)} custom-call(f32[2,256,256]{2,1,0:T(8,128)S(1)} %get-tuple-element.36.mine, f32[2,256,256]{2,1,0:T(8,128)S(1)} %collective-permute-done.theirs.turned), custom_call_target="tpu_custom_call" | custom-call | tf_op jit(solution)/shard_map/plane/pallas_call | solution.py:66
  4.6 1.3 %collective-permute-start.1 = (f32[256,256]{1,0:T(8,128)S(1)}, f32[256,256]{1,0:T(8,128)S(1)}, u32[]{:S(2)}, u32[]{:S(2)}) collective-permute-start(f32[256,256]{1,0:T(8,128)S(1)} %plane.1), channel_id=1, source_target_pairs={{0,8},{1,9},{2,10},{3,11},{4,12},{5,13},{6,14},{7,15},{8,0},{9,1},... | collective-permute-start | bytes 786440 | tf_op jit(solution)/shard_map/ppermute | solution.py:294
  5.9 0.4 %chip.1 = f32[2,256,256]{2,1,0:T(8,128)S(1)} custom-call(f32[2,256,256]{2,1,0:T(8,128)S(1)} %get-tuple-element.36.mine, f32[2,256,256]{2,1,0:T(8,128)S(1)} %collective-permute-done.theirs.turned, f32[256,256]{1,0:T(8,128)S(1)} %plane.1), custom_call_target="tpu_custom_call" | custom-call | tf_op jit(solution)/shard_map/chip/pallas_call | solution.py:66
  6.3 5.9 %collective-permute-done.1.near = f32[256,256]{1,0:T(8,128)S(1)} collective-permute-done((f32[256,256]{1,0:T(8,128)S(1)}, f32[256,256]{1,0:T(8,128)S(1)}, u32[]{:S(2)}, u32[]{:S(2)}) %collective-permute-start.1) | collective-permute-done | bytes 262176 | tf_op jit(solution)/shard_map/ppermute | solution.py:294
  12.2 1.2 %collective-permute-start.2 = (f32[256,256]{1,0:T(8,128)S(1)}, f32[256,256]{1,0:T(8,128)S(1)}, u32[]{:S(2)}, u32[]{:S(2)}) collective-permute-start(f32[256,256]{1,0:T(8,128)S(1)} %collective-permute-done.1.near), channel_id=1, source_target_pairs={{0,4},{1,5},{2,6},{3,7},{4,0},{5,1},{6,2},{7,3},{8,12},{9,13},{10,... | collective-permute-start | bytes 786440 | tf_op jit(solution)/shard_map/ppermute | solution.py:294
  13.4 1.2 %collective-permute-done.2.far = f32[256,256]{1,0:T(8,128)S(1)} collective-permute-done((f32[256,256]{1,0:T(8,128)S(1)}, f32[256,256]{1,0:T(8,128)S(1)}, u32[]{:S(2)}, u32[]{:S(2)}) %collective-permute-start.2) | collective-permute-done | bytes 262176 | tf_op jit(solution)/shard_map/ppermute | solution.py:294
  14.6 0.6 %collective-permute-start.3 = (f32[2,64,256]{2,1,0:T(8,128)S(1)}, f32[2,64,256]{2,1,0:T(8,128)S(1)}, u32[]{:S(2)}, u32[]{:S(2)}) collective-permute-start(f32[2,64,256]{2,1,0:T(8,128)S(1)} %get-tuple-element.39), channel_id=1, source_target_pairs={{0,1},{1,0},{2,3},{3,2},{4,5},{5,4},{6,7},{7,6},{8,9},{9,8},{10,11... | collective-permute-start | bytes 393224 | tf_op jit(solution)/shard_map/ppermute | solution.py:294
  15.2 0.7 %collective-permute-start.5 = (f32[2,64,256]{2,1,0:T(8,128)S(1)}, f32[2,64,256]{2,1,0:T(8,128)S(1)}, u32[]{:S(2)}, u32[]{:S(2)}) collective-permute-start(f32[2,64,256]{2,1,0:T(8,128)S(1)} %get-tuple-element.40.own), channel_id=1, source_target_pairs={{0,1},{4,5},{8,9},{12,13},{16,17},{20,21},{24,25},{28,29}} | collective-permute-start | bytes 393224 | tf_op jit(solution)/shard_map/ppermute | solution.py:294
  15.9 0.0 copy-start.1
  15.9 3.4 %collective-permute-done.3.piece.near.one = f32[2,64,256]{2,1,0:T(8,128)S(1)} collective-permute-done((f32[2,64,256]{2,1,0:T(8,128)S(1)}, f32[2,64,256]{2,1,0:T(8,128)S(1)}, u32[]{:S(2)}, u32[]{:S(2)}) %collective-permute-start.3) | collective-permute-done | bytes 131104 | tf_op jit(solution)/shard_map/ppermute | solution.py:294
  19.3 0.4 %collective-permute-start.4 = (f32[2,64,256]{2,1,0:T(8,128)S(1)}, f32[2,64,256]{2,1,0:T(8,128)S(1)}, u32[]{:S(2)}, u32[]{:S(2)}) collective-permute-start(f32[2,64,256]{2,1,0:T(8,128)S(1)} %extend.1), channel_id=1, source_target_pairs={{0,1},{1,2},{2,3},{3,0},{4,5},{5,6},{6,7},{7,4},{8,9},{9,10},{10,1... | collective-permute-start | bytes 393224 | tf_op jit(solution)/shard_map/ppermute | solution.py:294
  19.7 0.0 collective-permute-done.5.piece.one
  19.7 1.3 %collective-permute-start.6 = (f32[2,64,256]{2,1,0:T(8,128)S(1)}, f32[2,64,256]{2,1,0:T(8,128)S(1)}, u32[]{:S(2)}, u32[]{:S(2)}) collective-permute-start(f32[2,64,256]{2,1,0:T(8,128)S(1)} %extend_other.1), channel_id=1, source_target_pairs={{1,3},{5,7},{9,11},{13,15},{17,19},{21,23},{25,27},{29,31}} | collective-permute-start | bytes 393224 | tf_op jit(solution)/shard_map/ppermute | solution.py:294
  21.0 0.7 %collective-permute-start.8 = (f32[2,64,256]{2,1,0:T(8,128)S(1)}, f32[2,64,256]{2,1,0:T(8,128)S(1)}, u32[]{:S(2)}, u32[]{:S(2)}) collective-permute-start(f32[2,64,256]{2,1,0:T(8,128)S(1)} %extend_other.1), channel_id=1, source_target_pairs={{1,2},{5,6},{9,10},{13,14},{17,18},{21,22},{25,26},{29,30}} | collective-permute-start | bytes 393224 | tf_op jit(solution)/shard_map/ppermute | solution.py:294
  21.7 0.0 copy-done.1
  21.7 1.6 %before.1 = (f32[2,2,256,256]{3,2,1,0:T(8,128)S(1)}, bf16[2,2,256,256]{3,2,1,0:T(8,128)(2,1)S(1)}, bf16[2,2,256,256]{3,2,1,0:T(8,128)(2,1)S(1)}) custom-call(f32[1,1,2,2,256,256]{5,4,3,2,1,0:T(8,128)S(1)} %copy-done.1, f32[2,256,256]{2,1,0:T(8,128)S(1)} %get-tuple-element.41.block, f32[2,256,256]{2,1,0:T(8,128)S(1)} %collective-permute-done.theirs.turned, ...), custom_call_target="tpu_custom_call" | custom-call | tf_op jit(solution)/shard_map/before/pallas_call | solution.py:66
  23.3 0.0 collective-permute-done.4.across.two
  23.3 1.3 %collective-permute-start.7 = (f32[2,64,256]{2,1,0:T(8,128)S(1)}, f32[2,64,256]{2,1,0:T(8,128)S(1)}, u32[]{:S(2)}, u32[]{:S(2)}) collective-permute-start(f32[2,64,256]{2,1,0:T(8,128)S(1)} %collective-permute-done.4.across.two), channel_id=1, source_target_pairs={{2,3},{6,7},{10,11},{14,15},{18,19},{22,23},{26,27},{30,31}} | collective-permute-start | bytes 393224 | tf_op jit(solution)/shard_map/ppermute | solution.py:294
  24.6 2.2 %collective-permute-start.9 = (f32[96,256]{1,0:T(8,128)S(1)}, f32[96,256]{1,0:T(8,128)S(1)}, u32[]{:S(2)}, u32[]{:S(2)}) collective-permute-start(f32[96,256]{1,0:T(8,128)S(1)} %get-tuple-element.55), channel_id=1, source_target_pairs={{0,4},{1,5},{2,6},{3,7},{4,0},{5,1},{6,2},{7,3},{8,12},{9,13},{10,... | collective-permute-start | bytes 294920 | tf_op jit(solution)/shard_map/ppermute | solution.py:294
  26.8 0.1 collective-permute-start.10
  26.9 0.0 collective-permute-done.6.three
  26.9 3.3 %collective-permute-start.11 = (f32[80,256]{1,0:T(8,128)S(1)}, f32[80,256]{1,0:T(8,128)S(1)}, u32[]{:S(2)}, u32[]{:S(2)}) collective-permute-start(f32[80,256]{1,0:T(8,128)S(1)} %get-tuple-element.57), channel_id=1, source_target_pairs={{0,4},{1,5},{2,6},{3,7},{4,0},{5,1},{6,2},{7,3},{8,12},{9,13},{10,... | collective-permute-start | bytes 245768 | tf_op jit(solution)/shard_map/ppermute | solution.py:294
  30.2 0.6 %left.1 = (bf16[2,2,256,128]{3,2,1,0:T(8,128)(2,1)S(1)}, bf16[2,2,256,128]{3,2,1,0:T(8,128)(2,1)S(1)}) custom-call(bf16[2,2,256,256]{3,2,1,0:T(8,128)(2,1)S(1)} %get-tuple-element.45.before_high, bf16[2,2,256,256]{3,2,1,0:T(8,128)(2,1)S(1)} %get-tuple-element.46.before_low, f32[2,64,256]{2,1,0:T(8,128)S(1)} %collective-permute-done.3.piece.near.one, ...), custom_call_target="tpu_custom_call" | custom-call | tf_op jit(solution)/shard_map/left/pallas_call | solution.py:66
  30.9 0.0 collective-permute-done.8.two.three
  30.9 0.1 collective-permute-start.12
  31.0 0.0 collective-permute-done.10.refs_1_
  31.0 0.1 collective-permute-done.11.refs_2_
  31.1 0.0 collective-permute-done.9.refs_0_
  31.1 0.6 %left_far.1 = (bf16[2,2,256,128]{3,2,1,0:T(8,128)(2,1)S(1)}, bf16[2,2,256,128]{3,2,1,0:T(8,128)(2,1)S(1)}) custom-call(bf16[2,2,256,256]{3,2,1,0:T(8,128)(2,1)S(1)} %get-tuple-element.45.before_high, bf16[2,2,256,256]{3,2,1,0:T(8,128)(2,1)S(1)} %get-tuple-element.46.before_low, f32[96,256]{1,0:T(8,128)S(1)} %collective-permute-done.9.refs_0_, ...), custom_call_target="tpu_custom_call" | custom-call | tf_op jit(solution)/shard_map/left_far/pallas_call | solution.py:66
  31.8 0.0 collective-permute-done.7.three
  31.8 0.6 %collective-permute-start.13 = (f32[2,64,256]{2,1,0:T(8,128)S(1)}, f32[2,64,256]{2,1,0:T(8,128)S(1)}, u32[]{:S(2)}, u32[]{:S(2)}) collective-permute-start(f32[2,64,256]{2,1,0:T(8,128)S(1)} %merge_late.1.late), channel_id=1, source_target_pairs={{0,4},{1,5},{2,6},{3,7},{4,0},{5,1},{6,2},{7,3},{8,12},{9,13},{10,... | collective-permute-start | bytes 393224 | tf_op jit(solution)/shard_map/ppermute | solution.py:294
  32.4 0.6 %near.1 = (f32[2,2,256,128]{3,2,1,0:T(8,128)S(1)}, bf16[2,2,256,256]{3,2,1,0:T(8,128)(2,1)S(1)}, bf16[2,2,256,256]{3,2,1,0:T(8,128)(2,1)S(1)}) custom-call(bf16[2,2,256,128]{3,2,1,0:T(8,128)(2,1)S(1)} %get-tuple-element.51.high, bf16[2,2,256,128]{3,2,1,0:T(8,128)(2,1)S(1)} %get-tuple-element.52.low, bf16[2,2,256,128]{3,2,1,0:T(8,128)(2,1)S(1)} %get-tuple-element.59.far_high, ...), custom_call_target="tpu_custom_call" | custom-call | tf_op jit(solution)/shard_map/near/pallas_call | solution.py:66
  33.1 0.0 collective-permute-done.12.early
  33.1 0.3 collective-permute-done.13.late
  33.4 1.4 %far.1 = f32[1,1,2,2,256,256]{5,4,3,2,1,0:T(8,128)} custom-call(f32[2,2,256,256]{3,2,1,0:T(8,128)S(1)} %get-tuple-element.44.before, f32[2,2,256,128]{3,2,1,0:T(8,128)S(1)} %get-tuple-element.64.near, bf16[2,2,256,256]{3,2,1,0:T(8,128)(2,1)S(1)} %get-tuple-element.65.high, bf16[2,2,256,256]{3,2,1,0:T(8,128)(2,1)S(1)} %get-tuple-element.66.low, ...), custom_call_target="tpu_custom_call" | custom-call | tf_op jit(solution)/shard_map/far/pallas_call | solution.py:66
  (8 shorter events, 0.1 us)
Async XLA Ops:
  0.0 1.2 %copy-start = (f32[1,1,2,2,256,256]{5,4,3,2,1,0:T(8,128)S(1)}, f32[1,1,2,2,256,256]{5,4,3,2,1,0:T(8,128)}, u32[]{:S(2)}) copy-start(f32[1,1,2,2,256,256]{5,4,3,2,1,0:T(8,128)} %u.3) | copy-start | bytes 3145732
  1.9 2.3 %collective-permute-start = (f32[2,256,256]{2,1,0:T(8,128)S(1)}, f32[2,256,256]{2,1,0:T(8,128)S(1)}, u32[]{:S(2)}, u32[]{:S(2)}) collective-permute-start(f32[2,256,256]{2,1,0:T(8,128)S(1)} %get-tuple-element.36.mine), channel_id=1, source_target_pairs={{0,4},{1,5},{2,6},{3,7},{4,0},{5,1},{6,2},{7,3},{8,12},{9,13},{10,... | collective-permute-start | bytes 1572872 | tf_op jit(solution)/shard_map/ppermute | solution.py:294
  4.6 7.6 %collective-permute-start.1 = (f32[256,256]{1,0:T(8,128)S(1)}, f32[256,256]{1,0:T(8,128)S(1)}, u32[]{:S(2)}, u32[]{:S(2)}) collective-permute-start(f32[256,256]{1,0:T(8,128)S(1)} %plane.1), channel_id=1, source_target_pairs={{0,8},{1,9},{2,10},{3,11},{4,12},{5,13},{6,14},{7,15},{8,0},{9,1},... | collective-permute-start | bytes 786440 | tf_op jit(solution)/shard_map/ppermute | solution.py:294
  12.2 2.4 %collective-permute-start.2 = (f32[256,256]{1,0:T(8,128)S(1)}, f32[256,256]{1,0:T(8,128)S(1)}, u32[]{:S(2)}, u32[]{:S(2)}) collective-permute-start(f32[256,256]{1,0:T(8,128)S(1)} %collective-permute-done.1.near), channel_id=1, source_target_pairs={{0,4},{1,5},{2,6},{3,7},{4,0},{5,1},{6,2},{7,3},{8,12},{9,13},{10,... | collective-permute-start | bytes 786440 | tf_op jit(solution)/shard_map/ppermute | solution.py:294
  14.6 4.7 %collective-permute-start.3 = (f32[2,64,256]{2,1,0:T(8,128)S(1)}, f32[2,64,256]{2,1,0:T(8,128)S(1)}, u32[]{:S(2)}, u32[]{:S(2)}) collective-permute-start(f32[2,64,256]{2,1,0:T(8,128)S(1)} %get-tuple-element.39), channel_id=1, source_target_pairs={{0,1},{1,0},{2,3},{3,2},{4,5},{5,4},{6,7},{7,6},{8,9},{9,8},{10,11... | collective-permute-start | bytes 393224 | tf_op jit(solution)/shard_map/ppermute | solution.py:294
  15.2 4.5 %collective-permute-start.5 = (f32[2,64,256]{2,1,0:T(8,128)S(1)}, f32[2,64,256]{2,1,0:T(8,128)S(1)}, u32[]{:S(2)}, u32[]{:S(2)}) collective-permute-start(f32[2,64,256]{2,1,0:T(8,128)S(1)} %get-tuple-element.40.own), channel_id=1, source_target_pairs={{0,1},{4,5},{8,9},{12,13},{16,17},{20,21},{24,25},{28,29}} | collective-permute-start | bytes 393224 | tf_op jit(solution)/shard_map/ppermute | solution.py:294
  15.9 5.8 %copy-start.1 = (f32[1,1,2,2,256,256]{5,4,3,2,1,0:T(8,128)S(1)}, f32[1,1,2,2,256,256]{5,4,3,2,1,0:T(8,128)}, u32[]{:S(2)}) copy-start(f32[1,1,2,2,256,256]{5,4,3,2,1,0:T(8,128)} %u.3) | copy-start | bytes 3145732
  19.3 4.0 %collective-permute-start.4 = (f32[2,64,256]{2,1,0:T(8,128)S(1)}, f32[2,64,256]{2,1,0:T(8,128)S(1)}, u32[]{:S(2)}, u32[]{:S(2)}) collective-permute-start(f32[2,64,256]{2,1,0:T(8,128)S(1)} %extend.1), channel_id=1, source_target_pairs={{0,1},{1,2},{2,3},{3,0},{4,5},{5,6},{6,7},{7,4},{8,9},{9,10},{10,1... | collective-permute-start | bytes 393224 | tf_op jit(solution)/shard_map/ppermute | solution.py:294
  19.7 7.2 %collective-permute-start.6 = (f32[2,64,256]{2,1,0:T(8,128)S(1)}, f32[2,64,256]{2,1,0:T(8,128)S(1)}, u32[]{:S(2)}, u32[]{:S(2)}) collective-permute-start(f32[2,64,256]{2,1,0:T(8,128)S(1)} %extend_other.1), channel_id=1, source_target_pairs={{1,3},{5,7},{9,11},{13,15},{17,19},{21,23},{25,27},{29,31}} | collective-permute-start | bytes 393224 | tf_op jit(solution)/shard_map/ppermute | solution.py:294
  21.0 9.9 %collective-permute-start.8 = (f32[2,64,256]{2,1,0:T(8,128)S(1)}, f32[2,64,256]{2,1,0:T(8,128)S(1)}, u32[]{:S(2)}, u32[]{:S(2)}) collective-permute-start(f32[2,64,256]{2,1,0:T(8,128)S(1)} %extend_other.1), channel_id=1, source_target_pairs={{1,2},{5,6},{9,10},{13,14},{17,18},{21,22},{25,26},{29,30}} | collective-permute-start | bytes 393224 | tf_op jit(solution)/shard_map/ppermute | solution.py:294
  23.3 8.5 %collective-permute-start.7 = (f32[2,64,256]{2,1,0:T(8,128)S(1)}, f32[2,64,256]{2,1,0:T(8,128)S(1)}, u32[]{:S(2)}, u32[]{:S(2)}) collective-permute-start(f32[2,64,256]{2,1,0:T(8,128)S(1)} %collective-permute-done.4.across.two), channel_id=1, source_target_pairs={{2,3},{6,7},{10,11},{14,15},{18,19},{22,23},{26,27},{30,31}} | collective-permute-start | bytes 393224 | tf_op jit(solution)/shard_map/ppermute | solution.py:294
  24.6 6.5 %collective-permute-start.9 = (f32[96,256]{1,0:T(8,128)S(1)}, f32[96,256]{1,0:T(8,128)S(1)}, u32[]{:S(2)}, u32[]{:S(2)}) collective-permute-start(f32[96,256]{1,0:T(8,128)S(1)} %get-tuple-element.55), channel_id=1, source_target_pairs={{0,4},{1,5},{2,6},{3,7},{4,0},{5,1},{6,2},{7,3},{8,12},{9,13},{10,... | collective-permute-start | bytes 294920 | tf_op jit(solution)/shard_map/ppermute | solution.py:294
  26.8 4.1 %collective-permute-start.10 = (f32[80,256]{1,0:T(8,128)S(1)}, f32[80,256]{1,0:T(8,128)S(1)}, u32[]{:S(2)}, u32[]{:S(2)}) collective-permute-start(f32[80,256]{1,0:T(8,128)S(1)} %get-tuple-element.56), channel_id=1, source_target_pairs={{0,4},{1,5},{2,6},{3,7},{4,0},{5,1},{6,2},{7,3},{8,12},{9,13},{10,... | collective-permute-start | bytes 245768 | tf_op jit(solution)/shard_map/ppermute | solution.py:294
  26.9 4.2 %collective-permute-start.11 = (f32[80,256]{1,0:T(8,128)S(1)}, f32[80,256]{1,0:T(8,128)S(1)}, u32[]{:S(2)}, u32[]{:S(2)}) collective-permute-start(f32[80,256]{1,0:T(8,128)S(1)} %get-tuple-element.57), channel_id=1, source_target_pairs={{0,4},{1,5},{2,6},{3,7},{4,0},{5,1},{6,2},{7,3},{8,12},{9,13},{10,... | collective-permute-start | bytes 245768 | tf_op jit(solution)/shard_map/ppermute | solution.py:294
  30.9 2.2 %collective-permute-start.12 = (f32[2,64,256]{2,1,0:T(8,128)S(1)}, f32[2,64,256]{2,1,0:T(8,128)S(1)}, u32[]{:S(2)}, u32[]{:S(2)}) collective-permute-start(f32[2,64,256]{2,1,0:T(8,128)S(1)} %merge_early.1.early), channel_id=1, source_target_pairs={{0,4},{1,5},{2,6},{3,7},{4,0},{5,1},{6,2},{7,3},{8,12},{9,13},{10,... | collective-permute-start | bytes 393224 | tf_op jit(solution)/shard_map/ppermute | solution.py:294
  31.8 1.6 %collective-permute-start.13 = (f32[2,64,256]{2,1,0:T(8,128)S(1)}, f32[2,64,256]{2,1,0:T(8,128)S(1)}, u32[]{:S(2)}, u32[]{:S(2)}) collective-permute-start(f32[2,64,256]{2,1,0:T(8,128)S(1)} %merge_late.1.late), channel_id=1, source_target_pairs={{0,4},{1,5},{2,6},{3,7},{4,0},{5,1},{6,2},{7,3},{8,12},{9,13},{10,... | collective-permute-start | bytes 393224 | tf_op jit(solution)/shard_map/ppermute | solution.py:294

commit v12 on v11

--- a/solution.py
+++ b/solution.py
@@ -339,7 +339,6 @@
     three_other, high = tie((three_other, high))
     (early,) = call(merge_kernel, [strip], one, two, three_other, name="merge_early")
     far_early = permute(early, cores)
-    two_other, early = tie((two_other, early))
     (other,) = call(merge_kernel, [strip], one_other, two_other, two_other, name="merge_other")
     far_high, far_low = call(left_far_kernel, parts, *before_parts, *far_strips, name="left_far")
     three, other, far_high = tie((three, other, far_high))

time: 35 us -> 35 us (level)
  no operation moved by 1% of the time
where the time goes in v12:
time: 35 us; the launch traced here: 34.8 us
  starting transfers between devices  14.4 us (41%)
  waiting for transfers between devices  12.4 us (35%)
  Pallas kernels  6.51 us (19%)
  local copies, waits for them, and re-layouts  1.23 us (4%)
    ppermute x14, starting transfers between devices, permute(): return lax.ppermute(value, AXES, flat)  14.4 us
    ppermute x14, waiting for transfers between devices, permute(): return lax.ppermute(value, AXES, flat)  12.4 us
    pallas_call x16, Pallas kernels, call(): pl.pallas_call(body, out_shape=shapes, in_specs=[far if i == alias else w...  6.51 us
    unnamed x4, local copies, waits for them, and re-layouts  1.23 us
  transfers between devices with their start and end apart: 14, of which 6 were waited for; matrix products, arithmetic and copies ran while one was open for 0% of the time, Pallas kernels for 11%

profile of v12, /device:TPU:29, one launch (start us, length us, event | category | flops | bytes accessed | tf_op | source)
XLA Modules:
  0.0 34.8 jit_solution(3347222440082095115)
XLA Ops:
  0.0 0.0 copy-start
  0.0 1.2 %copy-done = f32[1,1,2,2,256,256]{5,4,3,2,1,0:T(8,128)S(1)} copy-done((f32[1,1,2,2,256,256]{5,4,3,2,1,0:T(8,128)S(1)}, f32[1,1,2,2,256,256]{5,4,3,2,1,0:T(8,128)}, u32[]{:S(2)}) %copy-start) | copy-done | bytes 1048600
  1.2 0.7 %block.1 = (f32[2,256,256]{2,1,0:T(8,128)S(1)}, f32[2,256,256]{2,1,0:T(8,128)S(1)}) custom-call(f32[1,1,2,2,256,256]{5,4,3,2,1,0:T(8,128)S(1)} %copy-done), custom_call_target="tpu_custom_call" | custom-call | tf_op jit(solution)/shard_map/block/pallas_call | solution.py:66
  1.9 0.7 %collective-permute-start = (f32[2,256,256]{2,1,0:T(8,128)S(1)}, f32[2,256,256]{2,1,0:T(8,128)S(1)}, u32[]{:S(2)}, u32[]{:S(2)}) collective-permute-start(f32[2,256,256]{2,1,0:T(8,128)S(1)} %get-tuple-element.34.mine), channel_id=1, source_target_pairs={{0,4},{1,5},{2,6},{3,7},{4,0},{5,1},{6,2},{7,3},{8,12},{9,13},{10,... | collective-permute-start | bytes 1572872 | tf_op jit(solution)/shard_map/ppermute | solution.py:294
  2.7 1.5 %collective-permute-done.theirs.turned = f32[2,256,256]{2,1,0:T(8,128)S(1)} collective-permute-done((f32[2,256,256]{2,1,0:T(8,128)S(1)}, f32[2,256,256]{2,1,0:T(8,128)S(1)}, u32[]{:S(2)}, u32[]{:S(2)}) %collective-permute-start) | collective-permute-done | bytes 524320 | tf_op jit(solution)/shard_map/ppermute | solution.py:294
  4.2 0.4 %plane.1 = f32[256,256]{1,0:T(8,128)S(1)} custom-call(f32[2,256,256]{2,1,0:T(8,128)S(1)} %get-tuple-element.34.mine, f32[2,256,256]{2,1,0:T(8,128)S(1)} %collective-permute-done.theirs.turned), custom_call_target="tpu_custom_call" | custom-call | tf_op jit(solution)/shard_map/plane/pallas_call | solution.py:66
  4.6 1.3 %collective-permute-start.1 = (f32[256,256]{1,0:T(8,128)S(1)}, f32[256,256]{1,0:T(8,128)S(1)}, u32[]{:S(2)}, u32[]{:S(2)}) collective-permute-start(f32[256,256]{1,0:T(8,128)S(1)} %plane.1), channel_id=1, source_target_pairs={{0,8},{1,9},{2,10},{3,11},{4,12},{5,13},{6,14},{7,15},{8,0},{9,1},... | collective-permute-start | bytes 786440 | tf_op jit(solution)/shard_map/ppermute | solution.py:294
  5.9 0.4 %chip.1 = f32[2,256,256]{2,1,0:T(8,128)S(1)} custom-call(f32[2,256,256]{2,1,0:T(8,128)S(1)} %get-tuple-element.34.mine, f32[2,256,256]{2,1,0:T(8,128)S(1)} %collective-permute-done.theirs.turned, f32[256,256]{1,0:T(8,128)S(1)} %plane.1), custom_call_target="tpu_custom_call" | custom-call | tf_op jit(solution)/shard_map/chip/pallas_call | solution.py:66
  6.3 5.9 %collective-permute-done.1.near = f32[256,256]{1,0:T(8,128)S(1)} collective-permute-done((f32[256,256]{1,0:T(8,128)S(1)}, f32[256,256]{1,0:T(8,128)S(1)}, u32[]{:S(2)}, u32[]{:S(2)}) %collective-permute-start.1) | collective-permute-done | bytes 262176 | tf_op jit(solution)/shard_map/ppermute | solution.py:294
  12.2 1.2 %collective-permute-start.2 = (f32[256,256]{1,0:T(8,128)S(1)}, f32[256,256]{1,0:T(8,128)S(1)}, u32[]{:S(2)}, u32[]{:S(2)}) collective-permute-start(f32[256,256]{1,0:T(8,128)S(1)} %collective-permute-done.1.near), channel_id=1, source_target_pairs={{0,4},{1,5},{2,6},{3,7},{4,0},{5,1},{6,2},{7,3},{8,12},{9,13},{10,... | collective-permute-start | bytes 786440 | tf_op jit(solution)/shard_map/ppermute | solution.py:294
  13.4 1.2 %collective-permute-done.2.far = f32[256,256]{1,0:T(8,128)S(1)} collective-permute-done((f32[256,256]{1,0:T(8,128)S(1)}, f32[256,256]{1,0:T(8,128)S(1)}, u32[]{:S(2)}, u32[]{:S(2)}) %collective-permute-start.2) | collective-permute-done | bytes 262176 | tf_op jit(solution)/shard_map/ppermute | solution.py:294
  14.6 0.6 %collective-permute-start.3 = (f32[2,64,256]{2,1,0:T(8,128)S(1)}, f32[2,64,256]{2,1,0:T(8,128)S(1)}, u32[]{:S(2)}, u32[]{:S(2)}) collective-permute-start(f32[2,64,256]{2,1,0:T(8,128)S(1)} %get-tuple-element.37), channel_id=1, source_target_pairs={{0,1},{1,0},{2,3},{3,2},{4,5},{5,4},{6,7},{7,6},{8,9},{9,8},{10,11... | collective-permute-start | bytes 393224 | tf_op jit(solution)/shard_map/ppermute | solution.py:294
  15.2 0.7 %collective-permute-start.5 = (f32[2,64,256]{2,1,0:T(8,128)S(1)}, f32[2,64,256]{2,1,0:T(8,128)S(1)}, u32[]{:S(2)}, u32[]{:S(2)}) collective-permute-start(f32[2,64,256]{2,1,0:T(8,128)S(1)} %get-tuple-element.38.own), channel_id=1, source_target_pairs={{0,1},{4,5},{8,9},{12,13},{16,17},{20,21},{24,25},{28,29}} | collective-permute-start | bytes 393224 | tf_op jit(solution)/shard_map/ppermute | solution.py:294
  15.9 0.0 copy-start.1
  15.9 3.4 %collective-permute-done.3.piece.near.one = f32[2,64,256]{2,1,0:T(8,128)S(1)} collective-permute-done((f32[2,64,256]{2,1,0:T(8,128)S(1)}, f32[2,64,256]{2,1,0:T(8,128)S(1)}, u32[]{:S(2)}, u32[]{:S(2)}) %collective-permute-start.3) | collective-permute-done | bytes 131104 | tf_op jit(solution)/shard_map/ppermute | solution.py:294
  19.3 0.4 %collective-permute-start.4 = (f32[2,64,256]{2,1,0:T(8,128)S(1)}, f32[2,64,256]{2,1,0:T(8,128)S(1)}, u32[]{:S(2)}, u32[]{:S(2)}) collective-permute-start(f32[2,64,256]{2,1,0:T(8,128)S(1)} %extend.1), channel_id=1, source_target_pairs={{0,1},{1,2},{2,3},{3,0},{4,5},{5,6},{6,7},{7,4},{8,9},{9,10},{10,1... | collective-permute-start | bytes 393224 | tf_op jit(solution)/shard_map/ppermute | solution.py:294
  19.7 0.0 collective-permute-done.5.piece.one
  19.7 1.3 %collective-permute-start.6 = (f32[2,64,256]{2,1,0:T(8,128)S(1)}, f32[2,64,256]{2,1,0:T(8,128)S(1)}, u32[]{:S(2)}, u32[]{:S(2)}) collective-permute-start(f32[2,64,256]{2,1,0:T(8,128)S(1)} %extend_other.1), channel_id=1, source_target_pairs={{1,3},{5,7},{9,11},{13,15},{17,19},{21,23},{25,27},{29,31}} | collective-permute-start | bytes 393224 | tf_op jit(solution)/shard_map/ppermute | solution.py:294
  21.0 0.7 %collective-permute-start.8 = (f32[2,64,256]{2,1,0:T(8,128)S(1)}, f32[2,64,256]{2,1,0:T(8,128)S(1)}, u32[]{:S(2)}, u32[]{:S(2)}) collective-permute-start(f32[2,64,256]{2,1,0:T(8,128)S(1)} %extend_other.1), channel_id=1, source_target_pairs={{1,2},{5,6},{9,10},{13,14},{17,18},{21,22},{25,26},{29,30}} | collective-permute-start | bytes 393224 | tf_op jit(solution)/shard_map/ppermute | solution.py:294
  21.7 0.0 copy-done.1
  21.7 1.6 %before.1 = (f32[2,2,256,256]{3,2,1,0:T(8,128)S(1)}, bf16[2,2,256,256]{3,2,1,0:T(8,128)(2,1)S(1)}, bf16[2,2,256,256]{3,2,1,0:T(8,128)(2,1)S(1)}) custom-call(f32[1,1,2,2,256,256]{5,4,3,2,1,0:T(8,128)S(1)} %copy-done.1, f32[2,256,256]{2,1,0:T(8,128)S(1)} %get-tuple-element.39.block, f32[2,256,256]{2,1,0:T(8,128)S(1)} %collective-permute-done.theirs.turned, ...), custom_call_target="tpu_custom_call" | custom-call | tf_op jit(solution)/shard_map/before/pallas_call | solution.py:66
  23.3 0.0 collective-permute-done.4.across.two
  23.3 1.3 %collective-permute-start.7 = (f32[2,64,256]{2,1,0:T(8,128)S(1)}, f32[2,64,256]{2,1,0:T(8,128)S(1)}, u32[]{:S(2)}, u32[]{:S(2)}) collective-permute-start(f32[2,64,256]{2,1,0:T(8,128)S(1)} %collective-permute-done.4.across.two), channel_id=1, source_target_pairs={{2,3},{6,7},{10,11},{14,15},{18,19},{22,23},{26,27},{30,31}} | collective-permute-start | bytes 393224 | tf_op jit(solution)/shard_map/ppermute | solution.py:294
  24.6 2.2 %collective-permute-start.9 = (f32[96,256]{1,0:T(8,128)S(1)}, f32[96,256]{1,0:T(8,128)S(1)}, u32[]{:S(2)}, u32[]{:S(2)}) collective-permute-start(f32[96,256]{1,0:T(8,128)S(1)} %get-tuple-element.51), channel_id=1, source_target_pairs={{0,4},{1,5},{2,6},{3,7},{4,0},{5,1},{6,2},{7,3},{8,12},{9,13},{10,... | collective-permute-start | bytes 294920 | tf_op jit(solution)/shard_map/ppermute | solution.py:294
  26.8 0.1 collective-permute-start.10
  26.9 0.0 collective-permute-done.6.three
  26.9 3.3 %collective-permute-start.11 = (f32[80,256]{1,0:T(8,128)S(1)}, f32[80,256]{1,0:T(8,128)S(1)}, u32[]{:S(2)}, u32[]{:S(2)}) collective-permute-start(f32[80,256]{1,0:T(8,128)S(1)} %get-tuple-element.53), channel_id=1, source_target_pairs={{0,4},{1,5},{2,6},{3,7},{4,0},{5,1},{6,2},{7,3},{8,12},{9,13},{10,... | collective-permute-start | bytes 245768 | tf_op jit(solution)/shard_map/ppermute | solution.py:294
  30.2 0.6 %left.1 = (bf16[2,2,256,128]{3,2,1,0:T(8,128)(2,1)S(1)}, bf16[2,2,256,128]{3,2,1,0:T(8,128)(2,1)S(1)}) custom-call(bf16[2,2,256,256]{3,2,1,0:T(8,128)(2,1)S(1)} %get-tuple-element.43.before_high, bf16[2,2,256,256]{3,2,1,0:T(8,128)(2,1)S(1)} %get-tuple-element.44.before_low, f32[2,64,256]{2,1,0:T(8,128)S(1)} %collective-permute-done.3.piece.near.one, ...), custom_call_target="tpu_custom_call" | custom-call | tf_op jit(solution)/shard_map/left/pallas_call | solution.py:66
  30.9 0.0 collective-permute-done.8.two.three
  30.9 0.1 collective-permute-start.12
  31.0 0.0 collective-permute-done.10.refs_1_
  31.0 0.1 collective-permute-done.11.refs_2_
  31.1 0.0 collective-permute-done.9.refs_0_
  31.1 0.6 %left_far.1 = (bf16[2,2,256,128]{3,2,1,0:T(8,128)(2,1)S(1)}, bf16[2,2,256,128]{3,2,1,0:T(8,128)(2,1)S(1)}) custom-call(bf16[2,2,256,256]{3,2,1,0:T(8,128)(2,1)S(1)} %get-tuple-element.43.before_high, bf16[2,2,256,256]{3,2,1,0:T(8,128)(2,1)S(1)} %get-tuple-element.44.before_low, f32[96,256]{1,0:T(8,128)S(1)} %collective-permute-done.9.refs_0_, ...), custom_call_target="tpu_custom_call" | custom-call | tf_op jit(solution)/shard_map/left_far/pallas_call | solution.py:66
  31.8 0.0 collective-permute-done.7.three
  31.8 0.6 %collective-permute-start.13 = (f32[2,64,256]{2,1,0:T(8,128)S(1)}, f32[2,64,256]{2,1,0:T(8,128)S(1)}, u32[]{:S(2)}, u32[]{:S(2)}) collective-permute-start(f32[2,64,256]{2,1,0:T(8,128)S(1)} %merge_late.1.late), channel_id=1, source_target_pairs={{0,4},{1,5},{2,6},{3,7},{4,0},{5,1},{6,2},{7,3},{8,12},{9,13},{10,... | collective-permute-start | bytes 393224 | tf_op jit(solution)/shard_map/ppermute | solution.py:294
  32.4 0.6 %near.1 = (f32[2,2,256,128]{3,2,1,0:T(8,128)S(1)}, bf16[2,2,256,256]{3,2,1,0:T(8,128)(2,1)S(1)}, bf16[2,2,256,256]{3,2,1,0:T(8,128)(2,1)S(1)}) custom-call(bf16[2,2,256,128]{3,2,1,0:T(8,128)(2,1)S(1)} %get-tuple-element.49.high, bf16[2,2,256,128]{3,2,1,0:T(8,128)(2,1)S(1)} %get-tuple-element.50.low, bf16[2,2,256,128]{3,2,1,0:T(8,128)(2,1)S(1)} %get-tuple-element.55.far_high, ...), custom_call_target="tpu_custom_call" | custom-call | tf_op jit(solution)/shard_map/near/pallas_call | solution.py:66
  33.1 0.0 collective-permute-done.12.early
  33.1 0.3 collective-permute-done.13.late
  33.4 1.4 %far.1 = f32[1,1,2,2,256,256]{5,4,3,2,1,0:T(8,128)} custom-call(f32[2,2,256,256]{3,2,1,0:T(8,128)S(1)} %get-tuple-element.42.before, f32[2,2,256,128]{3,2,1,0:T(8,128)S(1)} %get-tuple-element.60.near, bf16[2,2,256,256]{3,2,1,0:T(8,128)(2,1)S(1)} %get-tuple-element.61.high, bf16[2,2,256,256]{3,2,1,0:T(8,128)(2,1)S(1)} %get-tuple-element.62.low, ...), custom_call_target="tpu_custom_call" | custom-call | tf_op jit(solution)/shard_map/far/pallas_call | solution.py:66
  (8 shorter events, 0.1 us)
Async XLA Ops:
  0.0 1.2 %copy-start = (f32[1,1,2,2,256,256]{5,4,3,2,1,0:T(8,128)S(1)}, f32[1,1,2,2,256,256]{5,4,3,2,1,0:T(8,128)}, u32[]{:S(2)}) copy-start(f32[1,1,2,2,256,256]{5,4,3,2,1,0:T(8,128)} %u.3) | copy-start | bytes 3145732
  1.9 2.3 %collective-permute-start = (f32[2,256,256]{2,1,0:T(8,128)S(1)}, f32[2,256,256]{2,1,0:T(8,128)S(1)}, u32[]{:S(2)}, u32[]{:S(2)}) collective-permute-start(f32[2,256,256]{2,1,0:T(8,128)S(1)} %get-tuple-element.34.mine), channel_id=1, source_target_pairs={{0,4},{1,5},{2,6},{3,7},{4,0},{5,1},{6,2},{7,3},{8,12},{9,13},{10,... | collective-permute-start | bytes 1572872 | tf_op jit(solution)/shard_map/ppermute | solution.py:294
  4.6 7.6 %collective-permute-start.1 = (f32[256,256]{1,0:T(8,128)S(1)}, f32[256,256]{1,0:T(8,128)S(1)}, u32[]{:S(2)}, u32[]{:S(2)}) collective-permute-start(f32[256,256]{1,0:T(8,128)S(1)} %plane.1), channel_id=1, source_target_pairs={{0,8},{1,9},{2,10},{3,11},{4,12},{5,13},{6,14},{7,15},{8,0},{9,1},... | collective-permute-start | bytes 786440 | tf_op jit(solution)/shard_map/ppermute | solution.py:294
  12.2 2.4 %collective-permute-start.2 = (f32[256,256]{1,0:T(8,128)S(1)}, f32[256,256]{1,0:T(8,128)S(1)}, u32[]{:S(2)}, u32[]{:S(2)}) collective-permute-start(f32[256,256]{1,0:T(8,128)S(1)} %collective-permute-done.1.near), channel_id=1, source_target_pairs={{0,4},{1,5},{2,6},{3,7},{4,0},{5,1},{6,2},{7,3},{8,12},{9,13},{10,... | collective-permute-start | bytes 786440 | tf_op jit(solution)/shard_map/ppermute | solution.py:294
  14.6 4.7 %collective-permute-start.3 = (f32[2,64,256]{2,1,0:T(8,128)S(1)}, f32[2,64,256]{2,1,0:T(8,128)S(1)}, u32[]{:S(2)}, u32[]{:S(2)}) collective-permute-start(f32[2,64,256]{2,1,0:T(8,128)S(1)} %get-tuple-element.37), channel_id=1, source_target_pairs={{0,1},{1,0},{2,3},{3,2},{4,5},{5,4},{6,7},{7,6},{8,9},{9,8},{10,11... | collective-permute-start | bytes 393224 | tf_op jit(solution)/shard_map/ppermute | solution.py:294
  15.2 4.5 %collective-permute-start.5 = (f32[2,64,256]{2,1,0:T(8,128)S(1)}, f32[2,64,256]{2,1,0:T(8,128)S(1)}, u32[]{:S(2)}, u32[]{:S(2)}) collective-permute-start(f32[2,64,256]{2,1,0:T(8,128)S(1)} %get-tuple-element.38.own), channel_id=1, source_target_pairs={{0,1},{4,5},{8,9},{12,13},{16,17},{20,21},{24,25},{28,29}} | collective-permute-start | bytes 393224 | tf_op jit(solution)/shard_map/ppermute | solution.py:294
  15.9 5.8 %copy-start.1 = (f32[1,1,2,2,256,256]{5,4,3,2,1,0:T(8,128)S(1)}, f32[1,1,2,2,256,256]{5,4,3,2,1,0:T(8,128)}, u32[]{:S(2)}) copy-start(f32[1,1,2,2,256,256]{5,4,3,2,1,0:T(8,128)} %u.3) | copy-start | bytes 3145732
  19.3 4.0 %collective-permute-start.4 = (f32[2,64,256]{2,1,0:T(8,128)S(1)}, f32[2,64,256]{2,1,0:T(8,128)S(1)}, u32[]{:S(2)}, u32[]{:S(2)}) collective-permute-start(f32[2,64,256]{2,1,0:T(8,128)S(1)} %extend.1), channel_id=1, source_target_pairs={{0,1},{1,2},{2,3},{3,0},{4,5},{5,6},{6,7},{7,4},{8,9},{9,10},{10,1... | collective-permute-start | bytes 393224 | tf_op jit(solution)/shard_map/ppermute | solution.py:294
  19.7 7.2 %collective-permute-start.6 = (f32[2,64,256]{2,1,0:T(8,128)S(1)}, f32[2,64,256]{2,1,0:T(8,128)S(1)}, u32[]{:S(2)}, u32[]{:S(2)}) collective-permute-start(f32[2,64,256]{2,1,0:T(8,128)S(1)} %extend_other.1), channel_id=1, source_target_pairs={{1,3},{5,7},{9,11},{13,15},{17,19},{21,23},{25,27},{29,31}} | collective-permute-start | bytes 393224 | tf_op jit(solution)/shard_map/ppermute | solution.py:294
  21.0 9.9 %collective-permute-start.8 = (f32[2,64,256]{2,1,0:T(8,128)S(1)}, f32[2,64,256]{2,1,0:T(8,128)S(1)}, u32[]{:S(2)}, u32[]{:S(2)}) collective-permute-start(f32[2,64,256]{2,1,0:T(8,128)S(1)} %extend_other.1), channel_id=1, source_target_pairs={{1,2},{5,6},{9,10},{13,14},{17,18},{21,22},{25,26},{29,30}} | collective-permute-start | bytes 393224 | tf_op jit(solution)/shard_map/ppermute | solution.py:294
  23.3 8.5 %collective-permute-start.7 = (f32[2,64,256]{2,1,0:T(8,128)S(1)}, f32[2,64,256]{2,1,0:T(8,128)S(1)}, u32[]{:S(2)}, u32[]{:S(2)}) collective-permute-start(f32[2,64,256]{2,1,0:T(8,128)S(1)} %collective-permute-done.4.across.two), channel_id=1, source_target_pairs={{2,3},{6,7},{10,11},{14,15},{18,19},{22,23},{26,27},{30,31}} | collective-permute-start | bytes 393224 | tf_op jit(solution)/shard_map/ppermute | solution.py:294
  24.6 6.5 %collective-permute-start.9 = (f32[96,256]{1,0:T(8,128)S(1)}, f32[96,256]{1,0:T(8,128)S(1)}, u32[]{:S(2)}, u32[]{:S(2)}) collective-permute-start(f32[96,256]{1,0:T(8,128)S(1)} %get-tuple-element.51), channel_id=1, source_target_pairs={{0,4},{1,5},{2,6},{3,7},{4,0},{5,1},{6,2},{7,3},{8,12},{9,13},{10,... | collective-permute-start | bytes 294920 | tf_op jit(solution)/shard_map/ppermute | solution.py:294
  26.8 4.1 %collective-permute-start.10 = (f32[80,256]{1,0:T(8,128)S(1)}, f32[80,256]{1,0:T(8,128)S(1)}, u32[]{:S(2)}, u32[]{:S(2)}) collective-permute-start(f32[80,256]{1,0:T(8,128)S(1)} %get-tuple-element.52), channel_id=1, source_target_pairs={{0,4},{1,5},{2,6},{3,7},{4,0},{5,1},{6,2},{7,3},{8,12},{9,13},{10,... | collective-permute-start | bytes 245768 | tf_op jit(solution)/shard_map/ppermute | solution.py:294
  26.9 4.2 %collective-permute-start.11 = (f32[80,256]{1,0:T(8,128)S(1)}, f32[80,256]{1,0:T(8,128)S(1)}, u32[]{:S(2)}, u32[]{:S(2)}) collective-permute-start(f32[80,256]{1,0:T(8,128)S(1)} %get-tuple-element.53), channel_id=1, source_target_pairs={{0,4},{1,5},{2,6},{3,7},{4,0},{5,1},{6,2},{7,3},{8,12},{9,13},{10,... | collective-permute-start | bytes 245768 | tf_op jit(solution)/shard_map/ppermute | solution.py:294
  30.9 2.2 %collective-permute-start.12 = (f32[2,64,256]{2,1,0:T(8,128)S(1)}, f32[2,64,256]{2,1,0:T(8,128)S(1)}, u32[]{:S(2)}, u32[]{:S(2)}) collective-permute-start(f32[2,64,256]{2,1,0:T(8,128)S(1)} %merge_early.1.early), channel_id=1, source_target_pairs={{0,4},{1,5},{2,6},{3,7},{4,0},{5,1},{6,2},{7,3},{8,12},{9,13},{10,... | collective-permute-start | bytes 393224 | tf_op jit(solution)/shard_map/ppermute | solution.py:294
  31.8 1.6 %collective-permute-start.13 = (f32[2,64,256]{2,1,0:T(8,128)S(1)}, f32[2,64,256]{2,1,0:T(8,128)S(1)}, u32[]{:S(2)}, u32[]{:S(2)}) collective-permute-start(f32[2,64,256]{2,1,0:T(8,128)S(1)} %merge_late.1.late), channel_id=1, source_target_pairs={{0,4},{1,5},{2,6},{3,7},{4,0},{5,1},{6,2},{7,3},{8,12},{9,13},{10,... | collective-permute-start | bytes 393224 | tf_op jit(solution)/shard_map/ppermute | solution.py:294
